TPU v7x, 128 devices: a whole 4x4x4 slice. The times are simulated.
128 devices in a mesh: gz: 32 (over y, x_hi, z), vert: 4 (over x_lo, core).
Axes of the slice: x: 4 (x_hi: 2, x_lo: 2; x = x_hi * 2 + x_lo), y: 4, z: 4, core: 2. Of those that a mesh axis runs over, the one named last changes fastest.
Arguments:
- volume: bfloat16 [32, 131072], P('gz'), may hold values from -3 to 3
- dual: float32 [16, 64, 2048], P('vert', 'gz'), may hold values from -6 to 6
- counts: float32 [16, 64, 2048], P('vert', 'gz'), may hold values from 0 to 2.5
- cotangent: float32 [32, 131072], P('gz')
- dual_in: float32 [32, 3], replicated, may hold values from -3.5 to 3.5
- dual_bias: float32 [32], replicated, may hold values from -3 to 3
- dual_out: float32 [32], replicated, may hold values from -1 to 1
- primal_in: float32 [32, 2], replicated, may hold values from -4 to 4
- primal_bias: float32 [32], replicated, may hold values from -3 to 3
- primal_out: float32 [32], replicated, may hold values from -1 to 1
- blocks: bfloat16 [32, 4, 512, 128, 128], P('gz', 'vert'), may hold values from 0 to 0.079589844
- block_ray: int32 [32, 4, 512], P('gz', 'vert'), may hold values from 0 to 127
- block_vox: int32 [32, 4, 512], P('gz', 'vert'), may hold values from 0 to 3071
- block_count: int32 [32, 4], P('gz', 'vert'), may hold values from 128 to 512, as said below
Outputs:
- grad_volume: float32 [32, 131072], P('gz', 'vert')
- grad_dual: float32 [16, 64, 2048], P('vert', 'gz')
- grad_dual_in: float32 [32, 3], replicated
- grad_dual_bias: float32 [32], replicated
- grad_dual_out: float32 [32], replicated
- grad_primal_in: float32 [32, 2], replicated
- grad_primal_bias: float32 [32], replicated
- grad_primal_out: float32 [32], replicated
Inputs may be any that keep to these rules, and one draw needn't show every extreme that they name: Blocks block_count to 511 of a device's list are padding; in every draw some device has all 512 blocks valid.
All inputs are finite; a program needn't handle non-finite values.
Results may differ from a plain program's by a relative error of at most 0.00033.
Values may be sent and summed in bfloat16 or wider, within the bound.
No kernel may reach another device: no remote copies, remote signals or barrier semaphores. Data moves between devices by JAX's collectives and lax.ppermute only.
A program may use at most 192 MiB of HBM per device.

v0:
```python
import functools

import jax
import jax.numpy as jnp
from jax import lax
from jax.experimental import pallas as pl
from jax.experimental.pallas import tpu as pltpu
from jax.sharding import PartitionSpec as P

F32 = jnp.float32
BF16 = jnp.bfloat16
VMEM = pl.BlockSpec(memory_space=pltpu.VMEM)
SMEM = pl.BlockSpec(memory_space=pltpu.SMEM)
HBM = pl.BlockSpec(memory_space=pl.ANY)
NT = (((1,), (1,)), ((), ()))
GROUP = 16
CHUNKS = 16
MIB = 1024 * 1024


def sigmoid(x):
    return 0.5 * jnp.tanh(0.5 * x) + 0.5


def in_three(x):
    high = x.astype(BF16)
    rest = x - high.astype(F32)
    middle = rest.astype(BF16)
    return high, middle, (rest - middle.astype(F32)).astype(BF16)


def dot(a, b):
    return jnp.dot(a, b, preferred_element_type=F32)


def load_blocks(blocks, held, sems):
    per = held.shape[0] // CHUNKS
    copies = [
        pltpu.make_async_copy(
            blocks.at[pl.ds(i * per, per), :], held.at[pl.ds(i * per, per), :], sems.at[i]
        )
        for i in range(CHUNKS)
    ]
    for copy in copies:
        copy.start()
    return copies


def gather_tiles(vox, ext, picked):
    def body(i, carry):
        for j in range(16):
            b = i * 16 + j
            picked[pl.ds(b, 1), :] = ext[pl.ds(vox[b], 1), :]
        return carry

    lax.fori_loop(0, picked.shape[0] // 16, body, 0)


def project(copies, held, picked, products):
    count, size = picked.shape
    row = lax.broadcasted_iota(jnp.int32, (GROUP, size), 0)
    per = count // CHUNKS // GROUP
    for i, copy in enumerate(copies):
        copy.wait()
        for g in range(i * per, (i + 1) * per):
            x = picked[g * GROUP : (g + 1) * GROUP, :].astype(BF16)
            full = lax.dot_general(
                x,
                held[g * GROUP * size : (g + 1) * GROUP * size, :],
                NT,
                preferred_element_type=F32,
            )
            y = full[:, :size]
            for b in range(1, GROUP):
                y = jnp.where(row == b, full[:, b * size : (b + 1) * size], y)
            products[g * GROUP : (g + 1) * GROUP, :] = y


def spread(held, picked, out):
    count, size = out.shape
    row = lax.broadcasted_iota(jnp.int32, (GROUP, size), 0)
    for g in range(count // GROUP):
        s = picked[g * GROUP : (g + 1) * GROUP, :]
        diagonal = jnp.concatenate(
            [jnp.where(row == b, s, 0.0).astype(BF16) for b in range(GROUP)], axis=1
        )
        out[g * GROUP : (g + 1) * GROUP, :] = dot(
            diagonal, held[g * GROUP * size : (g + 1) * GROUP * size, :]
        )


def ray_choice(ray, count, tiles):
    shape = (tiles, ray.shape[1])
    tile = lax.broadcasted_iota(jnp.int32, shape, 0)
    block = lax.broadcasted_iota(jnp.int32, shape, 1)
    return jnp.where((ray[...] == tile) & (block < count[0]), 1.0, 0.0)


def add_rays(chosen, products):
    chosen = chosen.astype(BF16)
    high, middle, low = in_three(products[...])
    return dot(chosen, high) + dot(chosen, middle) + dot(chosen, low)


def forward_kernel(
    count, vox, ray, low, own, high, blocks, dual, counts, w_in, w_bias, w_out,
    sinogram, partial, ext, picked, products, held, sems,
):
    copies = load_blocks(blocks, held, sems)
    rows = own.shape[0]
    for i, field in enumerate((low, own, high)):
        ext[i * rows : (i + 1) * rows, :] = field[...].astype(F32)
    gather_tiles(vox, ext, picked)
    project(copies, held, picked, products)
    tiles, size = dual.shape
    chosen = ray_choice(ray, count, tiles)
    sinogram[...] = add_rays(chosen, products)
    part = 64
    fresh = []
    for start in range(0, tiles, part):
        rows = slice(start, start + part)
        d = dual[rows, :]
        s = sinogram[rows, :]
        r = jnp.exp(-s) - counts[rows, :]

        def channel(c, total):
            h = w_in[c, 0] * d + w_in[c, 1] * s + w_in[c, 2] * r + w_bias[c]
            return total + w_out[c] * (h * sigmoid(h))

        fresh.append(lax.fori_loop(0, w_bias.shape[0], channel, jnp.zeros_like(d), unroll=4) + d)
    new_dual = jnp.concatenate(fresh, axis=0).astype(BF16)
    picked[...] = dot(chosen.T.astype(BF16), new_dual)
    spread(held, picked, partial)


def backward_kernel(
    me, count, vox, ray, low, high, own, near1, own1, near2, own2, near3, own3,
    blocks, dual, counts, sinogram, w_in, w_bias, w_out,
    grad_dual, partial, sums, ext, picked, products, held, totals, sems,
):
    copies = load_blocks(blocks, held, sems)
    rows = own.shape[0]
    pieces = [
        (low, own, high),
        (near1.at[0], own1, near1.at[1]),
        (near2.at[0], own2, near2.at[1]),
        (near3.at[0], own3, near3.at[1]),
    ]
    for d, fields in enumerate(pieces):
        for i, field in enumerate(fields):
            at = pl.multiple_of((i * len(pieces) + (me[0] ^ d)) * rows, rows)
            ext[pl.ds(at, rows), :] = field[...].astype(F32)
    gather_tiles(vox, ext, picked)
    project(copies, held, picked, products)
    tiles, size = dual.shape
    chosen = ray_choice(ray, count, tiles)
    products[0:tiles, :] = add_rays(chosen, products)
    totals[...] = jnp.zeros_like(totals)
    part = 32
    grads = []
    for start in range(0, tiles, part):
        rows = slice(start, start + part)
        d = dual[rows, :]
        s = sinogram[rows, :]
        e = jnp.exp(-s)
        r = e - counts[rows, :]
        g = products[rows, :]

        def channel(c, carry):
            p0, p1, p2 = carry
            w0, w1, w2 = w_in[c, 0], w_in[c, 1], w_in[c, 2]
            h = w0 * d + w1 * s + w2 * r + w_bias[c]
            gate = sigmoid(h)
            act = h * gate
            err = (w_out[c] * g) * (gate + act * (1.0 - gate))

            def fold(x):
                return jnp.sum(x.reshape(part // 8, 8, size), axis=0)

            totals[c, 0] += fold(err * d)
            totals[c, 1] += fold(err * s)
            totals[c, 2] += fold(err * r)
            totals[c, 3] += fold(err)
            totals[c, 4] += fold(act * g)
            return p0 + w0 * err, p1 + w1 * err, p2 + w2 * err

        zero = jnp.zeros_like(d)
        p0, p1, p2 = lax.fori_loop(0, w_bias.shape[0], channel, (zero, zero, zero), unroll=2)
        grad_dual[rows, :] = g + p0
        grads.append(p1 - e * p2)
    sino_grad = jnp.concatenate(grads, axis=0).astype(BF16)
    picked[...] = dot(chosen.T.astype(BF16), sino_grad)
    spread(held, picked, partial)
    channels = w_bias.shape[0]
    for k in range(5):
        lanes = jnp.sum(totals[:, k], axis=1)
        sums[k : k + 1, :] = jnp.sum(lanes.T, axis=0, keepdims=True)


def place(vox, values, first, rows):
    tile = lax.broadcasted_iota(jnp.int32, (rows, vox.shape[1]), 0)
    chosen = jnp.where(vox[...] - first == tile, 1.0, 0.0).astype(BF16)
    size = values.shape[1] // 3
    out = dot(chosen, values)
    return out[:, :size] + out[:, size : 2 * size] + out[:, 2 * size :]


def own_kernel(me, vox, values, out):
    groups, rows, _ = out.shape
    parts = jnp.concatenate(in_three(values[...]), axis=1)
    for d in range(groups):
        first = (groups + (me[0] ^ d)) * rows
        out[d] = place(vox, parts, first, rows)


def fold_kernel(me, held, vox_low, from_low, vox_high, from_high, *outs):
    groups, rows, _ = held.shape
    low = jnp.concatenate(in_three(from_low[...]), axis=1)
    high = jnp.concatenate(in_three(from_high[...]), axis=1)
    for d in range(groups):
        first = (me[0] ^ d) * rows
        outs[d][...] = (
            held[d]
            + place(vox_low, low, 2 * groups * rows + first, rows)
            + place(vox_high, high, first, rows)
        )


def primal_kernel(
    me, own, peer1, peer2, peer3, volume, cotangent, w_in, w_bias, w_out,
    back_grad, direct, sums, totals,
):
    rows, size = own.shape
    base = me[0] * rows
    totals[...] = jnp.zeros_like(totals)
    part = 64

    def chunk(i, done):
        at = pl.ds(pl.multiple_of(i * part, part), part)
        there = pl.ds(pl.multiple_of(base + i * part, part), part)
        b = own[at, :] + peer1[at, :] + peer2[at, :] + peer3[at, :]
        v = volume[there, :].astype(F32)
        t = cotangent[there, :]

        def channel(c, carry):
            p0, p1 = carry
            w0, w1 = w_in[c, 0], w_in[c, 1]
            h = w0 * v + w1 * b + w_bias[c]
            gate = sigmoid(h)
            act = h * gate
            err = (w_out[c] * t) * (gate + act * (1.0 - gate))

            def fold(x):
                return jnp.sum(x.reshape(part // 8, 8, size), axis=0)

            totals[c, 0] += fold(err * v)
            totals[c, 1] += fold(err * b)
            totals[c, 2] += fold(err)
            totals[c, 3] += fold(act * t)
            return p0 + w0 * err, p1 + w1 * err

        zero = jnp.zeros_like(t)
        p0, p1 = lax.fori_loop(0, w_bias.shape[0], channel, (zero, zero), unroll=2)
        back_grad[at, :] = p1.astype(BF16)
        direct[at, :] = t + p0
        return done

    lax.fori_loop(0, rows // part, chunk, 0)
    for k in range(4):
        lanes = jnp.sum(totals[:, k], axis=1)
        sums[k : k + 1, :] = jnp.sum(lanes.T, axis=0, keepdims=True)


def call(body, out_shapes, specs, args, scratch=(), flops=0, bytes_moved=0, limit=56):
    return pl.pallas_call(
        body,
        out_shape=out_shapes,
        in_specs=specs,
        out_specs=[VMEM] * len(out_shapes),
        scratch_shapes=list(scratch),
        compiler_params=pltpu.CompilerParams(vmem_limit_bytes=limit * MIB),
        cost_estimate=pl.CostEstimate(
            flops=flops, bytes_accessed=bytes_moved, transcendentals=0
        ),
    )(*args)


def local(
    volume, dual, counts, cotangent, dual_in, dual_bias, dual_out,
    primal_in, primal_bias, primal_out, blocks, block_ray, block_vox, block_count,
):
    listed, tr, tv = blocks.shape[2:]
    voxels = volume.shape[1]
    tiles = voxels // tv
    views, det_rows, cols = dual.shape
    col_tiles = cols // tr
    ray_tiles = dual.size // tr
    channels = dual_bias.shape[0]
    groups = lax.axis_size("vert")
    slabs = lax.axis_size("gz")
    rows = tiles // groups
    me = lax.axis_index("vert").reshape(1).astype(jnp.int32)
    ray_total = 1.0 / (dual.size * slabs * groups)
    vox_total = 1.0 / (voxels * slabs)
    up = [(i, i + 1) for i in range(slabs - 1)]
    down = [(i + 1, i) for i in range(slabs - 1)]

    def shape(*dims, dtype=F32):
        return jax.ShapeDtypeStruct(dims, dtype)

    def beside(x):
        return lax.ppermute(x, "gz", up), lax.ppermute(x, "gz", down)

    def peer(x, d):
        return lax.ppermute(x, "vert", [(i, i ^ d) for i in range(groups)])

    def to_tiles(x):
        x = x.reshape(views, det_rows, col_tiles, tr).transpose(0, 2, 1, 3)
        return x.reshape(ray_tiles, tr)

    def from_tiles(x):
        x = x.reshape(views, col_tiles, det_rows, tr).transpose(0, 2, 1, 3)
        return x.reshape(views, det_rows, cols)

    matrix = blocks.reshape(listed * tr, tv)
    count = block_count.reshape(1)
    vox = block_vox.reshape(listed)
    ray = block_ray.reshape(1, listed)
    per_view = det_rows * col_tiles
    ray = (ray // per_view) * per_view + (ray % col_tiles) * det_rows + (ray // col_tiles) % det_rows
    listed_at = lax.broadcasted_iota(jnp.int32, (1, listed), 1)
    vox_row = jnp.where(listed_at < count[0], vox[None, :], -1)
    field = volume.reshape(tiles, tv)
    cot = cotangent.reshape(tiles, tv)
    dual_tiles = to_tiles(dual)
    count_tiles = to_tiles(counts)

    big = [
        pltpu.VMEM((3 * tiles, tv), F32),
        pltpu.VMEM((listed, tv), F32),
        pltpu.VMEM((listed, tr), F32),
        pltpu.VMEM((listed * tr, tv), BF16),
    ]
    low, high = beside(field)
    vox_low, vox_high = beside(vox_row)
    sinogram, partial = call(
        forward_kernel,
        [shape(ray_tiles, tr), shape(listed, tv)],
        [SMEM, SMEM, VMEM, VMEM, VMEM, VMEM, HBM, VMEM, VMEM, SMEM, SMEM, SMEM],
        (count, vox, ray, low, field, high, matrix, dual_tiles, count_tiles,
         dual_in, dual_bias, dual_out),
        big + [pltpu.SemaphoreType.DMA((CHUNKS,))],
        bytes_moved=3 * matrix.size,
    )

    def reduced(partial):
        from_low, from_high = beside(partial)
        held = call(
            own_kernel,
            [shape(groups, rows, tv)],
            [SMEM, VMEM, VMEM],
            (me, vox_row, partial),
            bytes_moved=4 * MIB,
            limit=32,
        )[0]
        parts = call(
            fold_kernel,
            [shape(rows, tv)] * groups,
            [SMEM] + [VMEM] * 5,
            (me, held, vox_low, from_low, vox_high, from_high),
            bytes_moved=8 * MIB,
            limit=32,
        )
        return [parts[0]] + [peer(parts[d], d) for d in range(1, groups)]

    pieces = reduced(partial)
    back_grad, direct, primal_sums = call(
        primal_kernel,
        [shape(rows, tv, dtype=BF16), shape(rows, tv), shape(4, channels)],
        [SMEM] + [VMEM] * 6 + [SMEM] * 3,
        (me, *pieces, field, cot, primal_in, primal_bias, primal_out),
        [pltpu.VMEM((channels, 4, 8, tv), F32)],
        bytes_moved=16 * MIB,
        limit=32,
    )
    near_low, near_high = beside(back_grad)
    near = jnp.stack([near_low, near_high])
    fields = [near_low, near_high, back_grad]
    for d in range(1, groups):
        fields += [peer(near, d), peer(back_grad, d)]
    grad_dual, partial, dual_sums = call(
        backward_kernel,
        [shape(ray_tiles, tr), shape(listed, tv), shape(5, channels)],
        [SMEM] * 3 + [VMEM] * 10 + [HBM] + [VMEM] * 3 + [SMEM] * 3,
        (me, count, vox, ray, *fields, matrix, dual_tiles, count_tiles, sinogram,
         dual_in, dual_bias, dual_out),
        big + [pltpu.VMEM((channels, 5, 8, tr), F32), pltpu.SemaphoreType.DMA((CHUNKS,))],
        bytes_moved=3 * matrix.size,
    )
    pieces = reduced(partial)
    grad_volume = pieces[0] + pieces[1] + pieces[2] + pieces[3] + direct

    sums = jnp.concatenate([dual_sums * ray_total, primal_sums * vox_total])
    sent = jnp.broadcast_to(sums[None], (slabs * groups, *sums.shape))
    summed = jnp.sum(lax.all_to_all(sent, ("gz", "vert"), 0, 0), axis=0)
    return (
        grad_volume.reshape(1, rows * tv),
        from_tiles(grad_dual),
        summed[0:3].T,
        summed[3],
        summed[4],
        summed[5:7].T,
        summed[7],
        summed[8],
    )


def solution(mesh):
    in_specs = (
        P("gz", None),
        P("vert", "gz", None),
        P("vert", "gz", None),
        P("gz", None),
        P(), P(), P(), P(), P(), P(),
        P("gz", "vert", None, None, None),
        P("gz", "vert", None),
        P("gz", "vert", None),
        P("gz", "vert"),
    )
    out_specs = (P("gz", "vert"), P("vert", "gz", None), P(), P(), P(), P(), P(), P())
    return jax.shard_map(local, mesh=mesh, in_specs=in_specs, out_specs=out_specs, check_vma=False)
```

profile of v0, /device:TPU:103, one launch (start us, length us, event | category | flops | bytes accessed | tf_op | source)
XLA Modules:
  0.0 151.7 jit_solution(1417645817945512888)
XLA Ops:
  0.6 0.0 copy-start.17
  0.7 2.5 %reduce = bf16[131072]{0:T(1024)(128)(2,1)S(1)} reduce(bf16[1,131072]{1,0:T(2,128)(2,1)} %param.14, bf16[]{:T(256)} %constant.71), dimensions={0}, to_apply=%param.14.reduce_sub_computation | reduce | bytes 524290 | tf_op args[0]
  3.2 2.7 %collective-permute-start = (bf16[1024,128]{1,0:T(8,128)(2,1)S(1)}, bf16[1024,128]{1,0:T(8,128)(2,1)S(1)}, u32[]{:S(2)}, u32[]{:S(2)}) collective-permute-start(bf16[1024,128]{1,0:T(8,128)(2,1)S(1)} %bitcast.58), channel_id=1, source_target_pairs={{0,4},{4,8},{8,12},{12,16},{16,20},{20,24},{24,28},{28,32},{32,36}... | collective-permute-start | bytes 786440 | tf_op jit(solution)/shard_map/ppermute | solution.py:312
  5.9 2.6 %collective-permute-start.1 = (bf16[1024,128]{1,0:T(8,128)(2,1)S(1)}, bf16[1024,128]{1,0:T(8,128)(2,1)S(1)}, u32[]{:S(2)}, u32[]{:S(2)}) collective-permute-start(bf16[1024,128]{1,0:T(8,128)(2,1)S(1)} %bitcast.59), channel_id=1, source_target_pairs={{4,0},{8,4},{12,8},{16,12},{20,16},{24,20},{28,24},{32,28},{36,32}... | collective-permute-start | bytes 786440 | tf_op jit(solution)/shard_map/ppermute | solution.py:312
  9.2 1.4 copy.36.w_in
  10.5 1.3 fusion.ray
  11.8 0.5 collective-permute-done.low
  12.3 6.9 %collective-permute-done.1.high = bf16[1024,128]{1,0:T(8,128)(2,1)S(1)} collective-permute-done((bf16[1024,128]{1,0:T(8,128)(2,1)S(1)}, bf16[1024,128]{1,0:T(8,128)(2,1)S(1)}, u32[]{:S(2)}, u32[]{:S(2)}) %collective-permute-start.1) | collective-permute-done | bytes 262176 | tf_op jit(solution)/shard_map/ppermute | solution.py:312
  19.2 0.7 copy-done.8
  19.9 13.2 %shard_map.197 = (f32[128,128]{1,0:T(8,128)}, f32[512,128]{1,0:T(8,128)}) custom-call(s32[1]{0:T(128)} %bitcast.56.count, s32[512]{0:T(512)} %bitcast.72, s32[1,512]{1,0:T(1,128)} %fusion.ray, bf16[1024,128]{1,0:T(8,128)(2,1)} %copy-done.7, bf16[1024,128]{1,0:T(8,128)(2,1)} %bitcast.60, bf16[1024,128]{1,0:T(8,128)(2,1)} %copy-done.8, ...), custom_call_target="tpu_custom_call" | custom-call | bytes 25165824 | tf_op jit(solution)/shard_map/pallas_call | solution.py:275
  33.1 1.9 %collective-permute-start.3 = (f32[512,128]{1,0:T(8,128)}, f32[512,128]{1,0:T(8,128)S(1)}, u32[]{:S(2)}, u32[]{:S(2)}) collective-permute-start(f32[512,128]{1,0:T(8,128)} %get-tuple-element.24.values), channel_id=1, source_target_pairs={{0,4},{4,8},{8,12},{12,16},{16,20},{20,24},{24,28},{28,32},{32,36}... | collective-permute-start | bytes 786440 | tf_op jit(solution)/shard_map/ppermute | solution.py:312
  35.1 3.4 %collective-permute-start.5 = (f32[512,128]{1,0:T(8,128)}, f32[512,128]{1,0:T(8,128)S(1)}, u32[]{:S(2)}, u32[]{:S(2)}) collective-permute-start(f32[512,128]{1,0:T(8,128)} %get-tuple-element.24.values), channel_id=1, source_target_pairs={{4,0},{8,4},{12,8},{16,12},{20,16},{24,20},{28,24},{32,28},{36,32}... | collective-permute-start | bytes 786440 | tf_op jit(solution)/shard_map/ppermute | solution.py:312
  38.5 6.4 %collective-permute-start.2 = (s32[1,512]{1,0:T(1,128)S(1)}, s32[1,512]{1,0:T(1,128)S(1)}, u32[]{:S(2)}, u32[]{:S(2)}) collective-permute-start(s32[1,512]{1,0:T(1,128)S(1)} %compare_select_fusion.2.vox), channel_id=1, source_target_pairs={{0,4},{4,8},{8,12},{12,16},{16,20},{20,24},{24,28},{28,32},{32,36}... | collective-permute-start | bytes 6152 | tf_op jit(solution)/shard_map/ppermute | solution.py:312
  44.9 1.9 %collective-permute-start.4 = (s32[1,512]{1,0:T(1,128)S(1)}, s32[1,512]{1,0:T(1,128)S(1)}, u32[]{:S(2)}, u32[]{:S(2)}) collective-permute-start(s32[1,512]{1,0:T(1,128)S(1)} %compare_select_fusion.2.vox), channel_id=1, source_target_pairs={{4,0},{8,4},{12,8},{16,12},{20,16},{24,20},{28,24},{32,28},{36,32}... | collective-permute-start | bytes 6152 | tf_op jit(solution)/shard_map/ppermute | solution.py:312
  46.9 0.9 copy-done.3
  47.8 0.7 shard_map.198.held
  48.5 5.2 %collective-permute-done.4.vox_high = s32[1,512]{1,0:T(1,128)S(1)} collective-permute-done((s32[1,512]{1,0:T(1,128)S(1)}, s32[1,512]{1,0:T(1,128)S(1)}, u32[]{:S(2)}, u32[]{:S(2)}) %collective-permute-start.4) | collective-permute-done | bytes 2080 | tf_op jit(solution)/shard_map/ppermute | solution.py:312
  53.8 0.0 collective-permute-done.3.from_low
  53.8 0.0 collective-permute-done.5.from_high
  53.8 1.3 shard_map.199
  55.0 3.7 %collective-permute-start.6 = (f32[256,128]{1,0:T(8,128)S(1)}, f32[256,128]{1,0:T(8,128)S(1)}, u32[]{:S(2)}, u32[]{:S(2)}) collective-permute-start(f32[256,128]{1,0:T(8,128)S(1)} %get-tuple-element.26), channel_id=1, source_target_pairs={{0,1},{1,0},{2,3},{3,2},{4,5},{5,4},{6,7},{7,6},{8,9},{9,8},{10,11... | collective-permute-start | bytes 393224 | tf_op jit(solution)/shard_map/ppermute | solution.py:315
  58.7 0.0 collective-permute-start.7
  58.7 1.7 %collective-permute-start.8 = (f32[256,128]{1,0:T(8,128)S(1)}, f32[256,128]{1,0:T(8,128)S(1)}, u32[]{:S(2)}, u32[]{:S(2)}) collective-permute-start(f32[256,128]{1,0:T(8,128)S(1)} %get-tuple-element.28), channel_id=1, source_target_pairs={{0,3},{1,2},{2,1},{3,0},{4,7},{5,6},{6,5},{7,4},{8,11},{9,10},{10,... | collective-permute-start | bytes 393224 | tf_op jit(solution)/shard_map/ppermute | solution.py:315
  60.4 0.1 copy.37.w_in
  60.5 3.2 %collective-permute-done.7.peer2 = f32[256,128]{1,0:T(8,128)S(1)} collective-permute-done((f32[256,128]{1,0:T(8,128)S(1)}, f32[256,128]{1,0:T(8,128)S(1)}, u32[]{:S(2)}, u32[]{:S(2)}) %collective-permute-start.7) | collective-permute-done | bytes 131104 | tf_op jit(solution)/shard_map/ppermute | solution.py:315
  63.8 3.0 %collective-permute-done.8.peer3 = f32[256,128]{1,0:T(8,128)S(1)} collective-permute-done((f32[256,128]{1,0:T(8,128)S(1)}, f32[256,128]{1,0:T(8,128)S(1)}, u32[]{:S(2)}, u32[]{:S(2)}) %collective-permute-start.8) | collective-permute-done | bytes 131104 | tf_op jit(solution)/shard_map/ppermute | solution.py:315
  66.8 0.9 copy-done.1
  67.7 5.5 %shard_map.200 = (bf16[256,128]{1,0:T(8,128)(2,1)S(1)}, f32[256,128]{1,0:T(8,128)S(1)}, f32[4,32]{1,0:T(4,128)S(1)}) custom-call(s32[1]{0:T(128)} %bitcast.me, f32[256,128]{1,0:T(8,128)S(1)} %get-tuple-element.25.own, f32[256,128]{1,0:T(8,128)S(1)} %collective-permute-done.6.peer1, f32[256,128]{1,0:T(8,128)S(1)} %collective-permute-done.7.peer2, ...), custom_call_target="tpu_custom_call" | custom-call | bytes 16777216 | tf_op jit(solution)/shard_map/pallas_call | solution.py:275
  73.2 1.9 %collective-permute-start.9 = (bf16[256,128]{1,0:T(8,128)(2,1)S(1)}, bf16[256,128]{1,0:T(8,128)(2,1)S(1)}, u32[]{:S(2)}, u32[]{:S(2)}) collective-permute-start(bf16[256,128]{1,0:T(8,128)(2,1)S(1)} %get-tuple-element.29.own), channel_id=1, source_target_pairs={{0,4},{4,8},{8,12},{12,16},{16,20},{20,24},{24,28},{28,32},{32,36}... | collective-permute-start | bytes 196616 | tf_op jit(solution)/shard_map/ppermute | solution.py:312
  75.1 3.4 %collective-permute-start.10 = (bf16[256,128]{1,0:T(8,128)(2,1)S(1)}, bf16[256,128]{1,0:T(8,128)(2,1)S(1)}, u32[]{:S(2)}, u32[]{:S(2)}) collective-permute-start(bf16[256,128]{1,0:T(8,128)(2,1)S(1)} %get-tuple-element.29.own), channel_id=1, source_target_pairs={{4,0},{8,4},{12,8},{16,12},{20,16},{24,20},{28,24},{32,28},{36,32}... | collective-permute-start | bytes 196616 | tf_op jit(solution)/shard_map/ppermute | solution.py:312
  78.5 0.9 collective-permute-start.12
  79.3 0.1 collective-permute-start.14
  79.5 1.6 %collective-permute-start.16 = (bf16[256,128]{1,0:T(8,128)(2,1)S(1)}, bf16[256,128]{1,0:T(8,128)(2,1)S(1)}, u32[]{:S(2)}, u32[]{:S(2)}) collective-permute-start(bf16[256,128]{1,0:T(8,128)(2,1)S(1)} %get-tuple-element.29.own), channel_id=1, source_target_pairs={{0,3},{1,2},{2,1},{3,0},{4,7},{5,6},{6,5},{7,4},{8,11},{9,10},{10,... | collective-permute-start | bytes 196616 | tf_op jit(solution)/shard_map/ppermute | solution.py:315
  81.1 3.6 %collective-permute-done.10.high = bf16[256,128]{1,0:T(8,128)(2,1)S(1)} collective-permute-done((bf16[256,128]{1,0:T(8,128)(2,1)S(1)}, bf16[256,128]{1,0:T(8,128)(2,1)S(1)}, u32[]{:S(2)}, u32[]{:S(2)}) %collective-permute-start.10) | collective-permute-done | bytes 65568 | tf_op jit(solution)/shard_map/ppermute | solution.py:312
  84.7 1.9 %collective-permute-start.11 = (bf16[2,256,128]{2,1,0:T(8,128)(2,1)S(1)}, bf16[2,256,128]{2,1,0:T(8,128)(2,1)S(1)}, u32[]{:S(2)}, u32[]{:S(2)}) collective-permute-start(bf16[2,256,128]{2,1,0:T(8,128)(2,1)S(1)} %pad_maximum_fusion), channel_id=1, source_target_pairs={{0,1},{1,0},{2,3},{3,2},{4,5},{5,4},{6,7},{7,6},{8,9},{9,8},{10,11... | collective-permute-start | bytes 393224 | tf_op jit(solution)/shard_map/ppermute | solution.py:315
  86.5 0.0 collective-permute-start.13
  86.5 1.9 %collective-permute-start.15 = (bf16[2,256,128]{2,1,0:T(8,128)(2,1)S(1)}, bf16[2,256,128]{2,1,0:T(8,128)(2,1)S(1)}, u32[]{:S(2)}, u32[]{:S(2)}) collective-permute-start(bf16[2,256,128]{2,1,0:T(8,128)(2,1)S(1)} %pad_maximum_fusion), channel_id=1, source_target_pairs={{0,3},{1,2},{2,1},{3,0},{4,7},{5,6},{6,5},{7,4},{8,11},{9,10},{10,... | collective-permute-start | bytes 393224 | tf_op jit(solution)/shard_map/ppermute | solution.py:315
  88.5 0.0 copy-start.11
  88.5 2.9 %collective-permute-done.13.near2 = bf16[2,256,128]{2,1,0:T(8,128)(2,1)S(1)} collective-permute-done((bf16[2,256,128]{2,1,0:T(8,128)(2,1)S(1)}, bf16[2,256,128]{2,1,0:T(8,128)(2,1)S(1)}, u32[]{:S(2)}, u32[]{:S(2)}) %collective-permute-start.13) | collective-permute-done | bytes 131104 | tf_op jit(solution)/shard_map/ppermute | solution.py:315
  91.4 3.2 %collective-permute-done.15.near3 = bf16[2,256,128]{2,1,0:T(8,128)(2,1)S(1)} collective-permute-done((bf16[2,256,128]{2,1,0:T(8,128)(2,1)S(1)}, bf16[2,256,128]{2,1,0:T(8,128)(2,1)S(1)}, u32[]{:S(2)}, u32[]{:S(2)}) %collective-permute-start.15) | collective-permute-done | bytes 131104 | tf_op jit(solution)/shard_map/ppermute | solution.py:315
  94.6 0.6 copy-done.13
  95.2 15.3 %shard_map.201 = (f32[128,128]{1,0:T(8,128)}, f32[512,128]{1,0:T(8,128)}, f32[5,32]{1,0:T(8,128)}) custom-call(s32[1]{0:T(128)} %bitcast.me, s32[1]{0:T(128)} %bitcast.57.count, s32[512]{0:T(512)} %bitcast.73, s32[1,512]{1,0:T(1,128)} %fusion.ray, bf16[256,128]{1,0:T(8,128)(2,1)} %copy-done.9, bf16[256,128]{1,0:T(8,128)(2,1)} %copy-done.10, ...), custom_call_target="tpu_custom_call" | custom-call | bytes 25165824 | tf_op jit(solution)/shard_map/pallas_call | solution.py:275
  110.5 0.7 broadcast_multiply_fusion
  111.2 0.1 broadcast_in_dim.11
  111.3 1.2 reshape.342
  112.5 8.9 %all-to-all-start = ((f32[128,1,288]{2,1,0:T(1,128)}), f32[128,1,288]{2,1,0:T(1,128)S(1)}, u32[]{:S(2)}, u32[]{:S(2)}) async-start(f32[128,1,288]{2,1,0:T(1,128)} %reshape.342), calls=%async_computation | async-start | bytes 393216 | tf_op jit(solution)/shard_map/all_to_all | solution.py:405
  121.4 1.7 %shard_map.202.held = f32[4,256,128]{2,1,0:T(8,128)S(1)} custom-call(s32[1]{0:T(128)} %bitcast.me, s32[1,512]{1,0:T(1,128)S(1)} %compare_select_fusion.2.vox, f32[512,128]{1,0:T(8,128)} %get-tuple-element.31.values), custom_call_target="tpu_custom_call" | custom-call | bytes 4194304 | tf_op jit(solution)/shard_map/pallas_call | solution.py:275
  123.0 3.3 %collective-permute-start.17 = (f32[512,128]{1,0:T(8,128)}, f32[512,128]{1,0:T(8,128)S(1)}, u32[]{:S(2)}, u32[]{:S(2)}) collective-permute-start(f32[512,128]{1,0:T(8,128)} %get-tuple-element.31.values), channel_id=1, source_target_pairs={{0,4},{4,8},{8,12},{12,16},{16,20},{20,24},{24,28},{28,32},{32,36}... | collective-permute-start | bytes 786440 | tf_op jit(solution)/shard_map/ppermute | solution.py:312
  126.3 2.0 %collective-permute-start.18 = (f32[512,128]{1,0:T(8,128)}, f32[512,128]{1,0:T(8,128)S(1)}, u32[]{:S(2)}, u32[]{:S(2)}) collective-permute-start(f32[512,128]{1,0:T(8,128)} %get-tuple-element.31.values), channel_id=1, source_target_pairs={{4,0},{8,4},{12,8},{16,12},{20,16},{24,20},{28,24},{32,28},{36,32}... | collective-permute-start | bytes 786440 | tf_op jit(solution)/shard_map/ppermute | solution.py:312
  128.3 0.5 broadcast.207
  128.8 1.1 reduce.1
  130.0 0.2 reshape.343
  130.2 0.1 reduce_sum.9
  130.3 0.5 slice_bitcast_fusion.2
  130.9 0.6 slice_bitcast_fusion
  131.5 1.2 collective-permute-done.17.from_low
  132.7 7.5 %collective-permute-done.18.from_high = f32[512,128]{1,0:T(8,128)S(1)} collective-permute-done((f32[512,128]{1,0:T(8,128)}, f32[512,128]{1,0:T(8,128)S(1)}, u32[]{:S(2)}, u32[]{:S(2)}) %collective-permute-start.18) | collective-permute-done | bytes 262176 | tf_op jit(solution)/shard_map/ppermute | solution.py:312
  140.1 1.3 shard_map.203
  141.4 1.6 %collective-permute-start.19 = (f32[256,128]{1,0:T(8,128)S(1)}, f32[256,128]{1,0:T(8,128)S(1)}, u32[]{:S(2)}, u32[]{:S(2)}) collective-permute-start(f32[256,128]{1,0:T(8,128)S(1)} %get-tuple-element.33), channel_id=1, source_target_pairs={{0,1},{1,0},{2,3},{3,2},{4,5},{5,4},{6,7},{7,6},{8,9},{9,8},{10,11... | collective-permute-start | bytes 393224 | tf_op jit(solution)/shard_map/ppermute | solution.py:315
  143.0 1.7 %collective-permute-start.21 = (f32[256,128]{1,0:T(8,128)S(1)}, f32[256,128]{1,0:T(8,128)S(1)}, u32[]{:S(2)}, u32[]{:S(2)}) collective-permute-start(f32[256,128]{1,0:T(8,128)S(1)} %get-tuple-element.35), channel_id=1, source_target_pairs={{0,3},{1,2},{2,1},{3,0},{4,7},{5,6},{6,5},{7,4},{8,11},{9,10},{10,... | collective-permute-start | bytes 393224 | tf_op jit(solution)/shard_map/ppermute | solution.py:315
  144.7 0.6 slice_bitcast_fusion.1
  145.3 2.8 %collective-permute-done.20 = f32[256,128]{1,0:T(8,128)S(1)} collective-permute-done((f32[256,128]{1,0:T(8,128)S(1)}, f32[256,128]{1,0:T(8,128)S(1)}, u32[]{:S(2)}, u32[]{:S(2)}) %collective-permute-start.20) | collective-permute-done | bytes 131104 | tf_op jit(solution)/shard_map/ppermute | solution.py:315
  148.1 3.0 %collective-permute-done.21 = f32[256,128]{1,0:T(8,128)S(1)} collective-permute-done((f32[256,128]{1,0:T(8,128)S(1)}, f32[256,128]{1,0:T(8,128)S(1)}, u32[]{:S(2)}, u32[]{:S(2)}) %collective-permute-start.21) | collective-permute-done | bytes 131104 | tf_op jit(solution)/shard_map/ppermute | solution.py:315
  151.1 0.7 add_add_fusion
  (46 shorter events, 0.1 us)
Async XLA Ops:
  0.6 37.8 %copy-start.17 = (s32[1,1,512]{2,1,0:T(1,128)S(1)}, s32[1,1,512]{2,1,0:T(1,128)}, u32[]{:S(2)}) copy-start(s32[1,1,512]{2,1,0:T(1,128)} %param.26) | copy-start | bytes 6148
  0.6 59.8 %copy-start.18 = (f32[32,2]{0,1:T(2,128)S(1)}, f32[32,2]{0,1:T(2,128)}, u32[]{:S(2)}) copy-start(f32[32,2]{0,1:T(2,128)} %param.21) | copy-start | bytes 772
  0.7 66.1 %copy-start.2 = (f32[1,131072]{1,0:T(1,128)S(1)}, f32[1,131072]{1,0:T(1,128)}, u32[]{:S(2)}) copy-start(f32[1,131072]{1,0:T(1,128)} %param.17) | copy-start | bytes 1572868
  0.7 66.1 %copy-start.5 = (f32[32]{0:T(128)S(1)}, f32[32]{0:T(128)}, u32[]{:S(2)}) copy-start(f32[32]{0:T(128)} %w_bias.4) | copy-start | bytes 388
  0.7 66.1 %copy-start.6 = (f32[32]{0:T(128)S(1)}, f32[32]{0:T(128)}, u32[]{:S(2)}) copy-start(f32[32]{0:T(128)} %w_out.4) | copy-start | bytes 388
  3.2 16.0 %copy-start = (bf16[131072]{0:T(1024)(128)(2,1)}, bf16[131072]{0:T(1024)(128)(2,1)S(1)}, u32[]{:S(2)}) copy-start(bf16[131072]{0:T(1024)(128)(2,1)S(1)} %reduce) | copy-start | bytes 786436
  3.2 9.1 %collective-permute-start = (bf16[1024,128]{1,0:T(8,128)(2,1)S(1)}, bf16[1024,128]{1,0:T(8,128)(2,1)S(1)}, u32[]{:S(2)}, u32[]{:S(2)}) collective-permute-start(bf16[1024,128]{1,0:T(8,128)(2,1)S(1)} %bitcast.58), channel_id=1, source_target_pairs={{0,4},{4,8},{8,12},{12,16},{16,20},{20,24},{24,28},{28,32},{32,36}... | collective-permute-start | bytes 786440 | tf_op jit(solution)/shard_map/ppermute | solution.py:312
  5.9 13.3 %collective-permute-start.1 = (bf16[1024,128]{1,0:T(8,128)(2,1)S(1)}, bf16[1024,128]{1,0:T(8,128)(2,1)S(1)}, u32[]{:S(2)}, u32[]{:S(2)}) collective-permute-start(bf16[1024,128]{1,0:T(8,128)(2,1)S(1)} %bitcast.59), channel_id=1, source_target_pairs={{4,0},{8,4},{12,8},{16,12},{20,16},{24,20},{28,24},{32,28},{36,32}... | collective-permute-start | bytes 786440 | tf_op jit(solution)/shard_map/ppermute | solution.py:312
  12.3 6.9 %copy-start.7 = (bf16[1024,128]{1,0:T(8,128)(2,1)}, bf16[1024,128]{1,0:T(8,128)(2,1)S(1)}, u32[]{:S(2)}) copy-start(bf16[1024,128]{1,0:T(8,128)(2,1)S(1)} %collective-permute-done.low) | copy-start | bytes 786436
  19.2 0.7 copy-start.8
  33.1 20.6 %collective-permute-start.3 = (f32[512,128]{1,0:T(8,128)}, f32[512,128]{1,0:T(8,128)S(1)}, u32[]{:S(2)}, u32[]{:S(2)}) collective-permute-start(f32[512,128]{1,0:T(8,128)} %get-tuple-element.24.values), channel_id=1, source_target_pairs={{0,4},{4,8},{8,12},{12,16},{16,20},{20,24},{24,28},{28,32},{32,36}... | collective-permute-start | bytes 786440 | tf_op jit(solution)/shard_map/ppermute | solution.py:312
  35.1 18.7 %collective-permute-start.5 = (f32[512,128]{1,0:T(8,128)}, f32[512,128]{1,0:T(8,128)S(1)}, u32[]{:S(2)}, u32[]{:S(2)}) collective-permute-start(f32[512,128]{1,0:T(8,128)} %get-tuple-element.24.values), channel_id=1, source_target_pairs={{4,0},{8,4},{12,8},{16,12},{20,16},{24,20},{28,24},{32,28},{36,32}... | collective-permute-start | bytes 786440 | tf_op jit(solution)/shard_map/ppermute | solution.py:312
  38.5 10.0 %collective-permute-start.2 = (s32[1,512]{1,0:T(1,128)S(1)}, s32[1,512]{1,0:T(1,128)S(1)}, u32[]{:S(2)}, u32[]{:S(2)}) collective-permute-start(s32[1,512]{1,0:T(1,128)S(1)} %compare_select_fusion.2.vox), channel_id=1, source_target_pairs={{0,4},{4,8},{8,12},{12,16},{16,20},{20,24},{24,28},{28,32},{32,36}... | collective-permute-start | bytes 6152 | tf_op jit(solution)/shard_map/ppermute | solution.py:312
  44.9 8.8 %collective-permute-start.4 = (s32[1,512]{1,0:T(1,128)S(1)}, s32[1,512]{1,0:T(1,128)S(1)}, u32[]{:S(2)}, u32[]{:S(2)}) collective-permute-start(s32[1,512]{1,0:T(1,128)S(1)} %compare_select_fusion.2.vox), channel_id=1, source_target_pairs={{4,0},{8,4},{12,8},{16,12},{20,16},{24,20},{28,24},{32,28},{36,32}... | collective-permute-start | bytes 6152 | tf_op jit(solution)/shard_map/ppermute | solution.py:312
  46.8 1.0 copy-start.3
  55.0 5.5 %collective-permute-start.6 = (f32[256,128]{1,0:T(8,128)S(1)}, f32[256,128]{1,0:T(8,128)S(1)}, u32[]{:S(2)}, u32[]{:S(2)}) collective-permute-start(f32[256,128]{1,0:T(8,128)S(1)} %get-tuple-element.26), channel_id=1, source_target_pairs={{0,1},{1,0},{2,3},{3,2},{4,5},{5,4},{6,7},{7,6},{8,9},{9,8},{10,11... | collective-permute-start | bytes 393224 | tf_op jit(solution)/shard_map/ppermute | solution.py:315
  58.7 5.1 %collective-permute-start.7 = (f32[256,128]{1,0:T(8,128)S(1)}, f32[256,128]{1,0:T(8,128)S(1)}, u32[]{:S(2)}, u32[]{:S(2)}) collective-permute-start(f32[256,128]{1,0:T(8,128)S(1)} %get-tuple-element.27), channel_id=1, source_target_pairs={{0,2},{1,3},{2,0},{3,1},{4,6},{5,7},{6,4},{7,5},{8,10},{9,11},{10,... | collective-permute-start | bytes 393224 | tf_op jit(solution)/shard_map/ppermute | solution.py:315
  58.7 8.0 %collective-permute-start.8 = (f32[256,128]{1,0:T(8,128)S(1)}, f32[256,128]{1,0:T(8,128)S(1)}, u32[]{:S(2)}, u32[]{:S(2)}) collective-permute-start(f32[256,128]{1,0:T(8,128)S(1)} %get-tuple-element.28), channel_id=1, source_target_pairs={{0,3},{1,2},{2,1},{3,0},{4,7},{5,6},{6,5},{7,4},{8,11},{9,10},{10,... | collective-permute-start | bytes 393224 | tf_op jit(solution)/shard_map/ppermute | solution.py:315
  66.8 1.0 copy-start.1
  73.2 21.4 %copy-start.4 = (bf16[256,128]{1,0:T(8,128)(2,1)}, bf16[256,128]{1,0:T(8,128)(2,1)S(1)}, u32[]{:S(2)}) copy-start(bf16[256,128]{1,0:T(8,128)(2,1)S(1)} %get-tuple-element.29.own) | copy-start | bytes 196612
  73.2 7.9 %collective-permute-start.9 = (bf16[256,128]{1,0:T(8,128)(2,1)S(1)}, bf16[256,128]{1,0:T(8,128)(2,1)S(1)}, u32[]{:S(2)}, u32[]{:S(2)}) collective-permute-start(bf16[256,128]{1,0:T(8,128)(2,1)S(1)} %get-tuple-element.29.own), channel_id=1, source_target_pairs={{0,4},{4,8},{8,12},{12,16},{16,20},{20,24},{24,28},{28,32},{32,36}... | collective-permute-start | bytes 196616 | tf_op jit(solution)/shard_map/ppermute | solution.py:312
  75.1 9.5 %collective-permute-start.10 = (bf16[256,128]{1,0:T(8,128)(2,1)S(1)}, bf16[256,128]{1,0:T(8,128)(2,1)S(1)}, u32[]{:S(2)}, u32[]{:S(2)}) collective-permute-start(bf16[256,128]{1,0:T(8,128)(2,1)S(1)} %get-tuple-element.29.own), channel_id=1, source_target_pairs={{4,0},{8,4},{12,8},{16,12},{20,16},{24,20},{28,24},{32,28},{36,32}... | collective-permute-start | bytes 196616 | tf_op jit(solution)/shard_map/ppermute | solution.py:312
  78.5 8.0 %collective-permute-start.12 = (bf16[256,128]{1,0:T(8,128)(2,1)S(1)}, bf16[256,128]{1,0:T(8,128)(2,1)S(1)}, u32[]{:S(2)}, u32[]{:S(2)}) collective-permute-start(bf16[256,128]{1,0:T(8,128)(2,1)S(1)} %get-tuple-element.29.own), channel_id=1, source_target_pairs={{0,1},{1,0},{2,3},{3,2},{4,5},{5,4},{6,7},{7,6},{8,9},{9,8},{10,11... | collective-permute-start | bytes 196616 | tf_op jit(solution)/shard_map/ppermute | solution.py:315
  79.3 9.1 %collective-permute-start.14 = (bf16[256,128]{1,0:T(8,128)(2,1)S(1)}, bf16[256,128]{1,0:T(8,128)(2,1)S(1)}, u32[]{:S(2)}, u32[]{:S(2)}) collective-permute-start(bf16[256,128]{1,0:T(8,128)(2,1)S(1)} %get-tuple-element.29.own), channel_id=1, source_target_pairs={{0,2},{1,3},{2,0},{3,1},{4,6},{5,7},{6,4},{7,5},{8,10},{9,11},{10,... | collective-permute-start | bytes 196616 | tf_op jit(solution)/shard_map/ppermute | solution.py:315
  79.5 9.0 %collective-permute-start.16 = (bf16[256,128]{1,0:T(8,128)(2,1)S(1)}, bf16[256,128]{1,0:T(8,128)(2,1)S(1)}, u32[]{:S(2)}, u32[]{:S(2)}) collective-permute-start(bf16[256,128]{1,0:T(8,128)(2,1)S(1)} %get-tuple-element.29.own), channel_id=1, source_target_pairs={{0,3},{1,2},{2,1},{3,0},{4,7},{5,6},{6,5},{7,4},{8,11},{9,10},{10,... | collective-permute-start | bytes 196616 | tf_op jit(solution)/shard_map/ppermute | solution.py:315
  81.1 13.5 %copy-start.9 = (bf16[256,128]{1,0:T(8,128)(2,1)}, bf16[256,128]{1,0:T(8,128)(2,1)S(1)}, u32[]{:S(2)}) copy-start(bf16[256,128]{1,0:T(8,128)(2,1)S(1)} %collective-permute-done.9.low) | copy-start | bytes 196612
  84.6 9.9 %copy-start.10 = (bf16[256,128]{1,0:T(8,128)(2,1)}, bf16[256,128]{1,0:T(8,128)(2,1)S(1)}, u32[]{:S(2)}) copy-start(bf16[256,128]{1,0:T(8,128)(2,1)S(1)} %collective-permute-done.10.high) | copy-start | bytes 196612
  84.7 3.8 %collective-permute-start.11 = (bf16[2,256,128]{2,1,0:T(8,128)(2,1)S(1)}, bf16[2,256,128]{2,1,0:T(8,128)(2,1)S(1)}, u32[]{:S(2)}, u32[]{:S(2)}) collective-permute-start(bf16[2,256,128]{2,1,0:T(8,128)(2,1)S(1)} %pad_maximum_fusion), channel_id=1, source_target_pairs={{0,1},{1,0},{2,3},{3,2},{4,5},{5,4},{6,7},{7,6},{8,9},{9,8},{10,11... | collective-permute-start | bytes 393224 | tf_op jit(solution)/shard_map/ppermute | solution.py:315
  86.5 4.8 %collective-permute-start.13 = (bf16[2,256,128]{2,1,0:T(8,128)(2,1)S(1)}, bf16[2,256,128]{2,1,0:T(8,128)(2,1)S(1)}, u32[]{:S(2)}, u32[]{:S(2)}) collective-permute-start(bf16[2,256,128]{2,1,0:T(8,128)(2,1)S(1)} %pad_maximum_fusion), channel_id=1, source_target_pairs={{0,2},{1,3},{2,0},{3,1},{4,6},{5,7},{6,4},{7,5},{8,10},{9,11},{10,... | collective-permute-start | bytes 393224 | tf_op jit(solution)/shard_map/ppermute | solution.py:315
  86.5 8.0 %copy-start.14 = (bf16[256,128]{1,0:T(8,128)(2,1)}, bf16[256,128]{1,0:T(8,128)(2,1)S(1)}, u32[]{:S(2)}) copy-start(bf16[256,128]{1,0:T(8,128)(2,1)S(1)} %collective-permute-done.12.own1) | copy-start | bytes 196612
  86.5 8.0 %collective-permute-start.15 = (bf16[2,256,128]{2,1,0:T(8,128)(2,1)S(1)}, bf16[2,256,128]{2,1,0:T(8,128)(2,1)S(1)}, u32[]{:S(2)}, u32[]{:S(2)}) collective-permute-start(bf16[2,256,128]{2,1,0:T(8,128)(2,1)S(1)} %pad_maximum_fusion), channel_id=1, source_target_pairs={{0,3},{1,2},{2,1},{3,0},{4,7},{5,6},{6,5},{7,4},{8,11},{9,10},{10,... | collective-permute-start | bytes 393224 | tf_op jit(solution)/shard_map/ppermute | solution.py:315
  88.4 6.1 %copy-start.15 = (bf16[256,128]{1,0:T(8,128)(2,1)}, bf16[256,128]{1,0:T(8,128)(2,1)S(1)}, u32[]{:S(2)}) copy-start(bf16[256,128]{1,0:T(8,128)(2,1)S(1)} %collective-permute-done.14.own2) | copy-start | bytes 196612
  88.5 6.1 %copy-start.16 = (bf16[256,128]{1,0:T(8,128)(2,1)}, bf16[256,128]{1,0:T(8,128)(2,1)S(1)}, u32[]{:S(2)}) copy-start(bf16[256,128]{1,0:T(8,128)(2,1)S(1)} %collective-permute-done.16.own3) | copy-start | bytes 196612
  88.5 6.1 %copy-start.11 = (bf16[2,256,128]{2,1,0:T(8,128)(2,1)}, bf16[2,256,128]{2,1,0:T(8,128)(2,1)S(1)}, u32[]{:S(2)}) copy-start(bf16[2,256,128]{2,1,0:T(8,128)(2,1)S(1)} %collective-permute-done.11.near1) | copy-start | bytes 393220
  91.4 3.3 %copy-start.12 = (bf16[2,256,128]{2,1,0:T(8,128)(2,1)}, bf16[2,256,128]{2,1,0:T(8,128)(2,1)S(1)}, u32[]{:S(2)}) copy-start(bf16[2,256,128]{2,1,0:T(8,128)(2,1)S(1)} %collective-permute-done.13.near2) | copy-start | bytes 393220
  94.6 0.7 copy-start.13
  112.5 15.9 %all-to-all-start = ((f32[128,1,288]{2,1,0:T(1,128)}), f32[128,1,288]{2,1,0:T(1,128)S(1)}, u32[]{:S(2)}, u32[]{:S(2)}) async-start(f32[128,1,288]{2,1,0:T(1,128)} %reshape.342), calls=%async_computation | async-start | bytes 393216 | tf_op jit(solution)/shard_map/all_to_all | solution.py:405
  123.0 9.6 %collective-permute-start.17 = (f32[512,128]{1,0:T(8,128)}, f32[512,128]{1,0:T(8,128)S(1)}, u32[]{:S(2)}, u32[]{:S(2)}) collective-permute-start(f32[512,128]{1,0:T(8,128)} %get-tuple-element.31.values), channel_id=1, source_target_pairs={{0,4},{4,8},{8,12},{12,16},{16,20},{20,24},{24,28},{28,32},{32,36}... | collective-permute-start | bytes 786440 | tf_op jit(solution)/shard_map/ppermute | solution.py:312
  126.3 13.8 %collective-permute-start.18 = (f32[512,128]{1,0:T(8,128)}, f32[512,128]{1,0:T(8,128)S(1)}, u32[]{:S(2)}, u32[]{:S(2)}) collective-permute-start(f32[512,128]{1,0:T(8,128)} %get-tuple-element.31.values), channel_id=1, source_target_pairs={{4,0},{8,4},{12,8},{16,12},{20,16},{24,20},{28,24},{32,28},{36,32}... | collective-permute-start | bytes 786440 | tf_op jit(solution)/shard_map/ppermute | solution.py:312
  141.4 3.9 %collective-permute-start.19 = (f32[256,128]{1,0:T(8,128)S(1)}, f32[256,128]{1,0:T(8,128)S(1)}, u32[]{:S(2)}, u32[]{:S(2)}) collective-permute-start(f32[256,128]{1,0:T(8,128)S(1)} %get-tuple-element.33), channel_id=1, source_target_pairs={{0,1},{1,0},{2,3},{3,2},{4,5},{5,4},{6,7},{7,6},{8,9},{9,8},{10,11... | collective-permute-start | bytes 393224 | tf_op jit(solution)/shard_map/ppermute | solution.py:315
  143.0 5.1 %collective-permute-start.20 = (f32[256,128]{1,0:T(8,128)S(1)}, f32[256,128]{1,0:T(8,128)S(1)}, u32[]{:S(2)}, u32[]{:S(2)}) collective-permute-start(f32[256,128]{1,0:T(8,128)S(1)} %get-tuple-element.34), channel_id=1, source_target_pairs={{0,2},{1,3},{2,0},{3,1},{4,6},{5,7},{6,4},{7,5},{8,10},{9,11},{10,... | collective-permute-start | bytes 393224 | tf_op jit(solution)/shard_map/ppermute | solution.py:315
  143.0 8.0 %collective-permute-start.21 = (f32[256,128]{1,0:T(8,128)S(1)}, f32[256,128]{1,0:T(8,128)S(1)}, u32[]{:S(2)}, u32[]{:S(2)}) collective-permute-start(f32[256,128]{1,0:T(8,128)S(1)} %get-tuple-element.35), channel_id=1, source_target_pairs={{0,3},{1,2},{2,1},{3,0},{4,7},{5,6},{6,5},{7,4},{8,11},{9,10},{10,... | collective-permute-start | bytes 393224 | tf_op jit(solution)/shard_map/ppermute | solution.py:315
where the time goes:
time: 152 us
  starting transfers between devices  53.4 us (35%)
  waiting for transfers between devices  42.9 us (28%)
  Pallas kernels  38.9 us (26%)
  local copies, waits for them, and re-layouts  8.34 us (5%)
  other arithmetic  6.52 us (4%)
  between operations  1.64 us (1%)
    pallas_call x7, Pallas kernels, call(): pl.pallas_call(body, out_shape=out_shapes, in_specs=specs, out_specs=[VME...  38.9 us
    ppermute x10, starting transfers between devices, beside(): return (lax.ppermute(x, 'gz', up), lax.ppermute(x, 'gz', down))  29.5 us
    ppermute x10, waiting for transfers between devices, beside(): return (lax.ppermute(x, 'gz', up), lax.ppermute(x, 'gz', down))  24.8 us
    ppermute x12, waiting for transfers between devices, peer(): return lax.ppermute(x, 'vert', [(i, i ^ d) for i in range(groups)])  18.1 us
    ppermute x12, starting transfers between devices, peer(): return lax.ppermute(x, 'vert', [(i, i ^ d) for i in range(groups)])  15 us
    all_to_all x1, starting transfers between devices, local(): summed = jnp.sum(lax.all_to_all(sent, ('gz', 'vert'), 0, 0), axis=0)  8.88 us
    unnamed x42, local copies, waits for them, and re-layouts  6.08 us
  transfers between devices with their start and end apart: 23, of which 12 were waited for; matrix products, arithmetic and copies ran while one was open for 4% of the time, Pallas kernels for 2%

commit v1 on v0

--- a/solution.py
+++ b/solution.py
@@ -33,17 +33,15 @@
     return jnp.dot(a, b, preferred_element_type=F32)
 
 
-def load_blocks(blocks, held, sems):
+def hold_kernel(blocks, _, held, sems):
     per = held.shape[0] // CHUNKS
-    copies = [
-        pltpu.make_async_copy(
-            blocks.at[pl.ds(i * per, per), :], held.at[pl.ds(i * per, per), :], sems.at[i]
-        )
-        for i in range(CHUNKS)
-    ]
+    copies = []
+    for i in range(CHUNKS):
+        rows = pl.ds(i * per, per)
+        copies.append(pltpu.make_async_copy(blocks.at[rows, :], held.at[rows, :], sems.at[i]))
+        copies[i].start()
     for copy in copies:
-        copy.start()
-    return copies
+        copy.wait()
 
 
 def gather_tiles(vox, ext, picked):
@@ -56,28 +54,25 @@
     lax.fori_loop(0, picked.shape[0] // 16, body, 0)
 
 
-def project(copies, held, picked, products):
+def project(held, picked, products):
     count, size = picked.shape
     row = lax.broadcasted_iota(jnp.int32, (GROUP, size), 0)
-    per = count // CHUNKS // GROUP
-    for i, copy in enumerate(copies):
-        copy.wait()
-        for g in range(i * per, (i + 1) * per):
-            x = picked[g * GROUP : (g + 1) * GROUP, :].astype(BF16)
-            full = lax.dot_general(
-                x,
-                held[g * GROUP * size : (g + 1) * GROUP * size, :],
-                NT,
-                preferred_element_type=F32,
-            )
-            y = full[:, :size]
-            for b in range(1, GROUP):
-                y = jnp.where(row == b, full[:, b * size : (b + 1) * size], y)
-            products[g * GROUP : (g + 1) * GROUP, :] = y
+    for g in range(count // GROUP):
+        x = picked[g * GROUP : (g + 1) * GROUP, :].astype(BF16)
+        full = lax.dot_general(
+            x,
+            held[g * GROUP * size : (g + 1) * GROUP * size, :],
+            NT,
+            preferred_element_type=F32,
+        )
+        y = full[:, :size]
+        for b in range(1, GROUP):
+            y = jnp.where(row == b, full[:, b * size : (b + 1) * size], y)
+        products[g * GROUP : (g + 1) * GROUP, :] = y
 
 
 def spread(held, picked, out):
-    count, size = out.shape
+    count, size = picked.shape
     row = lax.broadcasted_iota(jnp.int32, (GROUP, size), 0)
     for g in range(count // GROUP):
         s = picked[g * GROUP : (g + 1) * GROUP, :]
@@ -89,6 +84,13 @@
         )
 
 
+def mark_tiles(tile, out):
+    count, size = tile.shape[1], out.shape[1]
+    parts = [tile[:, i * size : (i + 1) * size] for i in range(count // size)]
+    rows = jnp.concatenate(parts + parts, axis=0)
+    out[count : count + 8, :] = rows.astype(F32)
+
+
 def ray_choice(ray, count, tiles):
     shape = (tiles, ray.shape[1])
     tile = lax.broadcasted_iota(jnp.int32, shape, 0)
@@ -103,15 +105,14 @@
 
 
 def forward_kernel(
-    count, vox, ray, low, own, high, blocks, dual, counts, w_in, w_bias, w_out,
-    sinogram, partial, ext, picked, products, held, sems,
+    count, vox, tile, ray, low, own, high, blocks, dual, counts, w_in, w_bias, w_out,
+    sinogram, partial, ext, picked, products,
 ):
-    copies = load_blocks(blocks, held, sems)
     rows = own.shape[0]
     for i, field in enumerate((low, own, high)):
         ext[i * rows : (i + 1) * rows, :] = field[...].astype(F32)
     gather_tiles(vox, ext, picked)
-    project(copies, held, picked, products)
+    project(blocks, picked, products)
     tiles, size = dual.shape
     chosen = ray_choice(ray, count, tiles)
     sinogram[...] = add_rays(chosen, products)
@@ -130,15 +131,15 @@
         fresh.append(lax.fori_loop(0, w_bias.shape[0], channel, jnp.zeros_like(d), unroll=4) + d)
     new_dual = jnp.concatenate(fresh, axis=0).astype(BF16)
     picked[...] = dot(chosen.T.astype(BF16), new_dual)
-    spread(held, picked, partial)
+    spread(blocks, picked, partial)
+    mark_tiles(tile, partial)
 
 
 def backward_kernel(
-    me, count, vox, ray, low, high, own, near1, own1, near2, own2, near3, own3,
+    me, count, vox, tile, ray, low, high, own, near1, own1, near2, own2, near3, own3,
     blocks, dual, counts, sinogram, w_in, w_bias, w_out,
-    grad_dual, partial, sums, ext, picked, products, held, totals, sems,
+    grad_dual, partial, sums, ext, picked, products, totals,
 ):
-    copies = load_blocks(blocks, held, sems)
     rows = own.shape[0]
     pieces = [
         (low, own, high),
@@ -151,7 +152,7 @@
             at = pl.multiple_of((i * len(pieces) + (me[0] ^ d)) * rows, rows)
             ext[pl.ds(at, rows), :] = field[...].astype(F32)
     gather_tiles(vox, ext, picked)
-    project(copies, held, picked, products)
+    project(blocks, picked, products)
     tiles, size = dual.shape
     chosen = ray_choice(ray, count, tiles)
     products[0:tiles, :] = add_rays(chosen, products)
@@ -190,33 +191,41 @@
         grads.append(p1 - e * p2)
     sino_grad = jnp.concatenate(grads, axis=0).astype(BF16)
     picked[...] = dot(chosen.T.astype(BF16), sino_grad)
-    spread(held, picked, partial)
+    spread(blocks, picked, partial)
+    mark_tiles(tile, partial)
     channels = w_bias.shape[0]
     for k in range(5):
         lanes = jnp.sum(totals[:, k], axis=1)
         sums[k : k + 1, :] = jnp.sum(lanes.T, axis=0, keepdims=True)
 
 
+def split_marked(marked):
+    count = marked.shape[0] - 8
+    marks = marked[count:, :].astype(jnp.int32)
+    vox = jnp.concatenate([marks[i : i + 1, :] for i in range(count // marked.shape[1])], axis=1)
+    return vox, jnp.concatenate(in_three(marked[:count, :]), axis=1)
+
+
 def place(vox, values, first, rows):
     tile = lax.broadcasted_iota(jnp.int32, (rows, vox.shape[1]), 0)
-    chosen = jnp.where(vox[...] - first == tile, 1.0, 0.0).astype(BF16)
+    chosen = jnp.where(vox - first == tile, 1.0, 0.0).astype(BF16)
     size = values.shape[1] // 3
     out = dot(chosen, values)
     return out[:, :size] + out[:, size : 2 * size] + out[:, 2 * size :]
 
 
-def own_kernel(me, vox, values, out):
+def own_kernel(me, partial, sums, out, sums_out):
     groups, rows, _ = out.shape
-    parts = jnp.concatenate(in_three(values[...]), axis=1)
+    sums_out[...] = sums[...]
+    vox, values = split_marked(partial)
     for d in range(groups):
-        first = (groups + (me[0] ^ d)) * rows
-        out[d] = place(vox, parts, first, rows)
-
-
-def fold_kernel(me, held, vox_low, from_low, vox_high, from_high, *outs):
+        out[d] = place(vox, values, (groups + (me[0] ^ d)) * rows, rows)
+
+
+def fold_kernel(me, held, from_low, from_high, *outs):
     groups, rows, _ = held.shape
-    low = jnp.concatenate(in_three(from_low[...]), axis=1)
-    high = jnp.concatenate(in_three(from_high[...]), axis=1)
+    vox_low, low = split_marked(from_low)
+    vox_high, high = split_marked(from_high)
     for d in range(groups):
         first = (me[0] ^ d) * rows
         outs[d][...] = (
@@ -323,6 +332,19 @@
         return x.reshape(views, det_rows, cols)
 
     matrix = blocks.reshape(listed * tr, tv)
+
+    def in_vmem(after):
+        held = call(
+            hold_kernel,
+            [pltpu.VMEM(matrix.shape, BF16)],
+            [HBM, HBM],
+            (pltpu.with_memory_space_constraint(matrix, pltpu.HBM), after),
+            [pltpu.SemaphoreType.DMA((CHUNKS,))],
+            bytes_moved=4 * matrix.size,
+            limit=12,
+        )[0]
+        return pltpu.with_memory_space_constraint(held, pltpu.VMEM)
+
     count = block_count.reshape(1)
     vox = block_vox.reshape(listed)
     ray = block_ray.reshape(1, listed)
@@ -339,41 +361,40 @@
         pltpu.VMEM((3 * tiles, tv), F32),
         pltpu.VMEM((listed, tv), F32),
         pltpu.VMEM((listed, tr), F32),
-        pltpu.VMEM((listed * tr, tv), BF16),
     ]
     low, high = beside(field)
-    vox_low, vox_high = beside(vox_row)
     sinogram, partial = call(
         forward_kernel,
-        [shape(ray_tiles, tr), shape(listed, tv)],
-        [SMEM, SMEM, VMEM, VMEM, VMEM, VMEM, HBM, VMEM, VMEM, SMEM, SMEM, SMEM],
-        (count, vox, ray, low, field, high, matrix, dual_tiles, count_tiles,
+        [shape(ray_tiles, tr), shape(listed + 8, tv)],
+        [SMEM] * 2 + [VMEM] * 8 + [SMEM] * 3,
+        (count, vox, vox_row, ray, low, field, high, in_vmem(block_count), dual_tiles, count_tiles,
          dual_in, dual_bias, dual_out),
-        big + [pltpu.SemaphoreType.DMA((CHUNKS,))],
+        big,
         bytes_moved=3 * matrix.size,
+        limit=12,
     )
 
-    def reduced(partial):
+    def reduced(partial, sums):
         from_low, from_high = beside(partial)
-        held = call(
+        held, sums = call(
             own_kernel,
-            [shape(groups, rows, tv)],
+            [shape(groups, rows, tv), shape(*sums.shape)],
             [SMEM, VMEM, VMEM],
-            (me, vox_row, partial),
+            (me, partial, sums),
             bytes_moved=4 * MIB,
-            limit=32,
-        )[0]
+            limit=16,
+        )
         parts = call(
             fold_kernel,
             [shape(rows, tv)] * groups,
-            [SMEM] + [VMEM] * 5,
-            (me, held, vox_low, from_low, vox_high, from_high),
+            [SMEM] + [VMEM] * 3,
+            (me, held, from_low, from_high),
             bytes_moved=8 * MIB,
-            limit=32,
-        )
-        return [parts[0]] + [peer(parts[d], d) for d in range(1, groups)]
-
-    pieces = reduced(partial)
+            limit=16,
+        )
+        return [parts[0]] + [peer(parts[d], d) for d in range(1, groups)], sums
+
+    pieces, _ = reduced(partial, dual_bias)
     back_grad, direct, primal_sums = call(
         primal_kernel,
         [shape(rows, tv, dtype=BF16), shape(rows, tv), shape(4, channels)],
@@ -381,7 +402,7 @@
         (me, *pieces, field, cot, primal_in, primal_bias, primal_out),
         [pltpu.VMEM((channels, 4, 8, tv), F32)],
         bytes_moved=16 * MIB,
-        limit=32,
+        limit=16,
     )
     near_low, near_high = beside(back_grad)
     near = jnp.stack([near_low, near_high])
@@ -390,17 +411,18 @@
         fields += [peer(near, d), peer(back_grad, d)]
     grad_dual, partial, dual_sums = call(
         backward_kernel,
-        [shape(ray_tiles, tr), shape(listed, tv), shape(5, channels)],
-        [SMEM] * 3 + [VMEM] * 10 + [HBM] + [VMEM] * 3 + [SMEM] * 3,
-        (me, count, vox, ray, *fields, matrix, dual_tiles, count_tiles, sinogram,
+        [shape(ray_tiles, tr), shape(listed + 8, tv), shape(5, channels)],
+        [SMEM] * 3 + [VMEM] * 15 + [SMEM] * 3,
+        (me, count, vox, vox_row, ray, *fields, in_vmem(near), dual_tiles, count_tiles, sinogram,
          dual_in, dual_bias, dual_out),
-        big + [pltpu.VMEM((channels, 5, 8, tr), F32), pltpu.SemaphoreType.DMA((CHUNKS,))],
+        big + [pltpu.VMEM((channels, 5, 8, tr), F32)],
         bytes_moved=3 * matrix.size,
+        limit=12,
     )
-    pieces = reduced(partial)
+    sums = jnp.concatenate([dual_sums * ray_total, primal_sums * vox_total])
+    pieces, sums = reduced(partial, sums)
     grad_volume = pieces[0] + pieces[1] + pieces[2] + pieces[3] + direct
 
-    sums = jnp.concatenate([dual_sums * ray_total, primal_sums * vox_total])
     sent = jnp.broadcast_to(sums[None], (slabs * groups, *sums.shape))
     summed = jnp.sum(lax.all_to_all(sent, ("gz", "vert"), 0, 0), axis=0)
     return (

time: 152 us -> 137 us (0.901)
  starting transfers between devices: 53.4 us -> 44.3 us
  waiting for transfers between devices: 42.9 us -> 37.3 us
  Pallas kernels: 38.9 us -> 43.9 us
  local copies, waits for them, and re-layouts: 8.34 us -> 4.53 us
  other arithmetic: 6.52 us -> 4.52 us
    ppermute x10 -> x8, starting transfers between devices: 29.5 us -> 21.9 us  [beside(): return (lax.ppermute(x, 'gz', up), lax.ppermute(x, 'gz', down))]
    ppermute x12, waiting for transfers between devices: 18.1 us -> 12 us  [peer(): return lax.ppermute(x, 'vert', [(i, i ^ d) for i in range(groups)])]
    pallas_call x7 -> x9, Pallas kernels: 38.9 us -> 43.9 us  [call(): pl.pallas_call(body, out_shape=out_shapes, in_specs=specs, out_specs=[VME...]
    unnamed x42 -> x24, local copies, waits for them, and re-layouts: 6.08 us -> 2.28 us
    ppermute x12, starting transfers between devices: 15 us -> 13 us  [peer(): return lax.ppermute(x, 'vert', [(i, i ^ d) for i in range(groups)])]
    ppermute x10 -> x8, waiting for transfers between devices: 24.8 us -> 24.3 us  [beside(): return (lax.ppermute(x, 'gz', up), lax.ppermute(x, 'gz', down))]
  transfers between devices with their start and end apart: 23 -> 21, of which waited for: 12 -> 11; matrix products, arithmetic and copies ran while one was open for 4% -> 3% of each run, Pallas kernels for 2% -> 10%
where the time goes in v1:
time: 137 us; the launch traced here: 136 us
  starting transfers between devices  44.3 us (32%)
  Pallas kernels  43.9 us (32%)
  waiting for transfers between devices  37.3 us (27%)
  local copies, waits for them, and re-layouts  4.53 us (3%)
  other arithmetic  4.52 us (3%)
  between operations  1.59 us (1%)
    pallas_call x9, Pallas kernels, call(): pl.pallas_call(body, out_shape=out_shapes, in_specs=specs, out_specs=[VME...  43.9 us
    ppermute x8, waiting for transfers between devices, beside(): return (lax.ppermute(x, 'gz', up), lax.ppermute(x, 'gz', down))  24.3 us
    ppermute x8, starting transfers between devices, beside(): return (lax.ppermute(x, 'gz', up), lax.ppermute(x, 'gz', down))  21.9 us
    ppermute x12, starting transfers between devices, peer(): return lax.ppermute(x, 'vert', [(i, i ^ d) for i in range(groups)])  13 us
    ppermute x12, waiting for transfers between devices, peer(): return lax.ppermute(x, 'vert', [(i, i ^ d) for i in range(groups)])  12 us
    all_to_all x1, starting transfers between devices, local(): summed = jnp.sum(lax.all_to_all(sent, ('gz', 'vert'), 0, 0), axis=0)  9.45 us
  transfers between devices with their start and end apart: 21, of which 11 were waited for; matrix products, arithmetic and copies ran while one was open for 3% of the time, Pallas kernels for 10%

profile of v1, /device:TPU:103, one launch (start us, length us, event | category | flops | bytes accessed | tf_op | source)
XLA Modules:
  0.0 136.1 jit_solution(8278415996943700584)
XLA Ops:
  0.6 2.5 %reduce = bf16[131072]{0:T(1024)(128)(2,1)S(1)} reduce(bf16[1,131072]{1,0:T(2,128)(2,1)} %param.14, bf16[]{:T(256)} %constant.71), dimensions={0}, to_apply=%param.14.reduce_sub_computation | reduce | bytes 524290 | tf_op args[0]
  3.1 2.7 %collective-permute-start = (bf16[1024,128]{1,0:T(8,128)(2,1)S(1)}, bf16[1024,128]{1,0:T(8,128)(2,1)S(1)}, u32[]{:S(2)}, u32[]{:S(2)}) collective-permute-start(bf16[1024,128]{1,0:T(8,128)(2,1)S(1)} %bitcast.58), channel_id=1, source_target_pairs={{0,4},{4,8},{8,12},{12,16},{16,20},{20,24},{24,28},{28,32},{32,36}... | collective-permute-start | bytes 786440 | tf_op jit(solution)/shard_map/ppermute | solution.py:321
  5.8 2.6 %collective-permute-start.1 = (bf16[1024,128]{1,0:T(8,128)(2,1)S(1)}, bf16[1024,128]{1,0:T(8,128)(2,1)S(1)}, u32[]{:S(2)}, u32[]{:S(2)}) collective-permute-start(bf16[1024,128]{1,0:T(8,128)(2,1)S(1)} %bitcast.59), channel_id=1, source_target_pairs={{4,0},{8,4},{12,8},{16,12},{20,16},{24,20},{28,24},{32,28},{36,32}... | collective-permute-start | bytes 786440 | tf_op jit(solution)/shard_map/ppermute | solution.py:321
  9.1 0.8 copy.36.w_in
  9.8 0.0 copy-start.2
  9.9 0.0 copy-start.4
  9.9 0.0 copy-start.5
  9.9 6.0 %shard_map.197.blocks = bf16[65536,128]{1,0:T(8,128)(2,1)S(1)} custom-call(bf16[65536,128]{1,0:T(8,128)(2,1)} %bitcast.71, s32[1,1]{1,0:T(1,128)} %copy.48._), custom_call_target="tpu_custom_call" | custom-call | bytes 33554432 | tf_op jit(solution)/shard_map/pallas_call | solution.py:284
  15.9 0.0 copy-start.9
  15.9 0.0 copy-start
  15.9 0.0 copy-start.6
  15.9 0.0 copy-start.7
  16.0 0.0 collective-permute-done.low
  16.0 3.1 %collective-permute-done.1.high = bf16[1024,128]{1,0:T(8,128)(2,1)S(1)} collective-permute-done((bf16[1024,128]{1,0:T(8,128)(2,1)S(1)}, bf16[1024,128]{1,0:T(8,128)(2,1)S(1)}, u32[]{:S(2)}, u32[]{:S(2)}) %collective-permute-start.1) | collective-permute-done | bytes 262176 | tf_op jit(solution)/shard_map/ppermute | solution.py:321
  19.1 9.7 %shard_map.198 = (f32[128,128]{1,0:T(8,128)S(1)}, f32[520,128]{1,0:T(8,128)S(1)}) custom-call(s32[1]{0:T(128)} %bitcast.55.count, s32[512]{0:T(512)S(1)} %bitcast.69, s32[1,512]{1,0:T(1,128)S(1)} %get-tuple-element.50.tile, s32[1,512]{1,0:T(1,128)S(1)} %get-tuple-element.51.ray, bf16[1024,128]{1,0:T(8,128)(2,1)S(1)} %collective-permute-done.low, ...), custom_call_target="tpu_custom_call" | custom-call | bytes 25165824 | tf_op jit(solution)/shard_map/pallas_call | solution.py:284
  28.8 4.2 %collective-permute-start.2 = (f32[520,128]{1,0:T(8,128)S(1)}, f32[520,128]{1,0:T(8,128)S(1)}, u32[]{:S(2)}, u32[]{:S(2)}) collective-permute-start(f32[520,128]{1,0:T(8,128)S(1)} %get-tuple-element.27.partial), channel_id=1, source_target_pairs={{0,4},{4,8},{8,12},{12,16},{16,20},{20,24},{24,28},{28,32},{32,36}... | collective-permute-start | bytes 798728 | tf_op jit(solution)/shard_map/ppermute | solution.py:321
  33.0 1.9 %collective-permute-start.3 = (f32[520,128]{1,0:T(8,128)S(1)}, f32[520,128]{1,0:T(8,128)S(1)}, u32[]{:S(2)}, u32[]{:S(2)}) collective-permute-start(f32[520,128]{1,0:T(8,128)S(1)} %get-tuple-element.27.partial), channel_id=1, source_target_pairs={{4,0},{8,4},{12,8},{16,12},{20,16},{24,20},{28,24},{32,28},{36,32}... | collective-permute-start | bytes 798728 | tf_op jit(solution)/shard_map/ppermute | solution.py:321
  34.9 1.2 shard_map.199
  36.1 1.3 collective-permute-done.2.from_low
  37.4 8.3 %collective-permute-done.3.from_high = f32[520,128]{1,0:T(8,128)S(1)} collective-permute-done((f32[520,128]{1,0:T(8,128)S(1)}, f32[520,128]{1,0:T(8,128)S(1)}, u32[]{:S(2)}, u32[]{:S(2)}) %collective-permute-start.3) | collective-permute-done | bytes 266272 | tf_op jit(solution)/shard_map/ppermute | solution.py:321
  45.8 1.3 shard_map.200
  47.1 2.5 %collective-permute-start.4 = (f32[256,128]{1,0:T(8,128)S(1)}, f32[256,128]{1,0:T(8,128)S(1)}, u32[]{:S(2)}, u32[]{:S(2)}) collective-permute-start(f32[256,128]{1,0:T(8,128)S(1)} %get-tuple-element.30), channel_id=1, source_target_pairs={{0,1},{1,0},{2,3},{3,2},{4,5},{5,4},{6,7},{7,6},{8,9},{9,8},{10,11... | collective-permute-start | bytes 393224 | tf_op jit(solution)/shard_map/ppermute | solution.py:324
  49.6 1.7 %collective-permute-start.6 = (f32[256,128]{1,0:T(8,128)S(1)}, f32[256,128]{1,0:T(8,128)S(1)}, u32[]{:S(2)}, u32[]{:S(2)}) collective-permute-start(f32[256,128]{1,0:T(8,128)S(1)} %get-tuple-element.32), channel_id=1, source_target_pairs={{0,3},{1,2},{2,1},{3,0},{4,7},{5,6},{6,5},{7,4},{8,11},{9,10},{10,... | collective-permute-start | bytes 393224 | tf_op jit(solution)/shard_map/ppermute | solution.py:324
  51.3 0.1 copy.37.w_in
  51.4 3.2 %collective-permute-done.5.peer2 = f32[256,128]{1,0:T(8,128)S(1)} collective-permute-done((f32[256,128]{1,0:T(8,128)S(1)}, f32[256,128]{1,0:T(8,128)S(1)}, u32[]{:S(2)}, u32[]{:S(2)}) %collective-permute-start.5) | collective-permute-done | bytes 131104 | tf_op jit(solution)/shard_map/ppermute | solution.py:324
  54.6 3.0 %collective-permute-done.6.peer3 = f32[256,128]{1,0:T(8,128)S(1)} collective-permute-done((f32[256,128]{1,0:T(8,128)S(1)}, f32[256,128]{1,0:T(8,128)S(1)}, u32[]{:S(2)}, u32[]{:S(2)}) %collective-permute-start.6) | collective-permute-done | bytes 131104 | tf_op jit(solution)/shard_map/ppermute | solution.py:324
  57.6 5.5 %shard_map.201 = (bf16[256,128]{1,0:T(8,128)(2,1)S(1)}, f32[256,128]{1,0:T(8,128)S(1)}, f32[4,32]{1,0:T(4,128)S(1)}) custom-call(s32[1]{0:T(128)} %bitcast.me, f32[256,128]{1,0:T(8,128)S(1)} %get-tuple-element.29.own, f32[256,128]{1,0:T(8,128)S(1)} %collective-permute-done.4.peer1, f32[256,128]{1,0:T(8,128)S(1)} %collective-permute-done.5.peer2, ...), custom_call_target="tpu_custom_call" | custom-call | bytes 16777216 | tf_op jit(solution)/shard_map/pallas_call | solution.py:284
  63.1 1.9 %collective-permute-start.7 = (bf16[256,128]{1,0:T(8,128)(2,1)S(1)}, bf16[256,128]{1,0:T(8,128)(2,1)S(1)}, u32[]{:S(2)}, u32[]{:S(2)}) collective-permute-start(bf16[256,128]{1,0:T(8,128)(2,1)S(1)} %get-tuple-element.33.own), channel_id=1, source_target_pairs={{0,4},{4,8},{8,12},{12,16},{16,20},{20,24},{24,28},{28,32},{32,36}... | collective-permute-start | bytes 196616 | tf_op jit(solution)/shard_map/ppermute | solution.py:321
  65.0 3.4 %collective-permute-start.8 = (bf16[256,128]{1,0:T(8,128)(2,1)S(1)}, bf16[256,128]{1,0:T(8,128)(2,1)S(1)}, u32[]{:S(2)}, u32[]{:S(2)}) collective-permute-start(bf16[256,128]{1,0:T(8,128)(2,1)S(1)} %get-tuple-element.33.own), channel_id=1, source_target_pairs={{4,0},{8,4},{12,8},{16,12},{20,16},{24,20},{28,24},{32,28},{36,32}... | collective-permute-start | bytes 196616 | tf_op jit(solution)/shard_map/ppermute | solution.py:321
  68.4 0.9 collective-permute-start.10
  69.3 0.1 collective-permute-start.12
  69.4 1.6 %collective-permute-start.14 = (bf16[256,128]{1,0:T(8,128)(2,1)S(1)}, bf16[256,128]{1,0:T(8,128)(2,1)S(1)}, u32[]{:S(2)}, u32[]{:S(2)}) collective-permute-start(bf16[256,128]{1,0:T(8,128)(2,1)S(1)} %get-tuple-element.33.own), channel_id=1, source_target_pairs={{0,3},{1,2},{2,1},{3,0},{4,7},{5,6},{6,5},{7,4},{8,11},{9,10},{10,... | collective-permute-start | bytes 196616 | tf_op jit(solution)/shard_map/ppermute | solution.py:324
  71.0 0.0 collective-permute-done.7.low
  71.0 3.9 %collective-permute-done.8.high = bf16[256,128]{1,0:T(8,128)(2,1)S(1)} collective-permute-done((bf16[256,128]{1,0:T(8,128)(2,1)S(1)}, bf16[256,128]{1,0:T(8,128)(2,1)S(1)}, u32[]{:S(2)}, u32[]{:S(2)}) %collective-permute-start.8) | collective-permute-done | bytes 65568 | tf_op jit(solution)/shard_map/ppermute | solution.py:321
  75.0 0.1 collective-permute-start.11
  75.0 2.7 %collective-permute-start.13 = (bf16[2,256,128]{2,1,0:T(8,128)(2,1)S(1)}, bf16[2,256,128]{2,1,0:T(8,128)(2,1)S(1)}, u32[]{:S(2)}, u32[]{:S(2)}) collective-permute-start(bf16[2,256,128]{2,1,0:T(8,128)(2,1)S(1)} %pad_maximum_fusion._), channel_id=1, source_target_pairs={{0,3},{1,2},{2,1},{3,0},{4,7},{5,6},{6,5},{7,4},{8,11},{9,10},{10,... | collective-permute-start | bytes 393224 | tf_op jit(solution)/shard_map/ppermute | solution.py:324
  77.8 0.0 collective-permute-start.9
  77.8 5.9 %shard_map.202.blocks = bf16[65536,128]{1,0:T(8,128)(2,1)S(1)} custom-call(bf16[65536,128]{1,0:T(8,128)(2,1)} %bitcast.72, bf16[2,256,128]{2,1,0:T(8,128)(2,1)S(1)} %pad_maximum_fusion._), custom_call_target="tpu_custom_call" | custom-call | bytes 33554432 | tf_op jit(solution)/shard_map/pallas_call | solution.py:284
  83.7 0.0 collective-permute-done.12.own2
  83.8 0.0 collective-permute-done.14.own3
  83.8 0.0 collective-permute-done.13.near3
  83.8 12.3 %shard_map.203 = (f32[128,128]{1,0:T(8,128)}, f32[520,128]{1,0:T(8,128)S(1)}, f32[5,32]{1,0:T(8,128)S(1)}) custom-call(s32[1]{0:T(128)} %bitcast.me, s32[1]{0:T(128)} %bitcast.56.count, s32[512]{0:T(512)S(1)} %bitcast.70, s32[1,512]{1,0:T(1,128)S(1)} %get-tuple-element.50.tile, s32[1,512]{1,0:T(1,128)S(1)} %get-tuple-element.51.ray, ...), custom_call_target="tpu_custom_call" | custom-call | bytes 25165824 | tf_op jit(solution)/shard_map/pallas_call | solution.py:284
  96.1 0.7 shard_map.204
  96.8 0.1 broadcast_in_dim.11
  96.9 1.2 reshape.342
  98.1 9.4 %all-to-all-start = ((f32[128,1,288]{2,1,0:T(1,128)}), f32[128,1,288]{2,1,0:T(1,128)S(1)}, u32[]{:S(2)}, u32[]{:S(2)}) async-start(f32[128,1,288]{2,1,0:T(1,128)} %reshape.342), calls=%async_computation | async-start | bytes 393216 | tf_op jit(solution)/shard_map/all_to_all | solution.py:427
  107.5 3.3 %collective-permute-start.15 = (f32[520,128]{1,0:T(8,128)S(1)}, f32[520,128]{1,0:T(8,128)S(1)}, u32[]{:S(2)}, u32[]{:S(2)}) collective-permute-start(f32[520,128]{1,0:T(8,128)S(1)} %get-tuple-element.35.partial), channel_id=1, source_target_pairs={{0,4},{4,8},{8,12},{12,16},{16,20},{20,24},{24,28},{28,32},{32,36}... | collective-permute-start | bytes 798728 | tf_op jit(solution)/shard_map/ppermute | solution.py:321
  110.8 2.0 %collective-permute-start.16 = (f32[520,128]{1,0:T(8,128)S(1)}, f32[520,128]{1,0:T(8,128)S(1)}, u32[]{:S(2)}, u32[]{:S(2)}) collective-permute-start(f32[520,128]{1,0:T(8,128)S(1)} %get-tuple-element.35.partial), channel_id=1, source_target_pairs={{4,0},{8,4},{12,8},{16,12},{20,16},{24,20},{28,24},{32,28},{36,32}... | collective-permute-start | bytes 798728 | tf_op jit(solution)/shard_map/ppermute | solution.py:321
  112.8 1.0 all-to-all-done
  113.8 0.5 broadcast.207
  114.3 1.1 reduce.1
  115.5 0.2 reshape.343
  115.7 0.1 reduce_sum.9
  115.9 0.5 slice_bitcast_fusion.2
  116.4 0.6 slice_bitcast_fusion
  117.0 1.0 collective-permute-done.15.from_low
  117.9 6.6 %collective-permute-done.16.from_high = f32[520,128]{1,0:T(8,128)S(1)} collective-permute-done((f32[520,128]{1,0:T(8,128)S(1)}, f32[520,128]{1,0:T(8,128)S(1)}, u32[]{:S(2)}, u32[]{:S(2)}) %collective-permute-start.16) | collective-permute-done | bytes 266272 | tf_op jit(solution)/shard_map/ppermute | solution.py:321
  124.5 1.3 shard_map.205
  125.8 1.6 %collective-permute-start.17 = (f32[256,128]{1,0:T(8,128)S(1)}, f32[256,128]{1,0:T(8,128)S(1)}, u32[]{:S(2)}, u32[]{:S(2)}) collective-permute-start(f32[256,128]{1,0:T(8,128)S(1)} %get-tuple-element.40), channel_id=1, source_target_pairs={{0,1},{1,0},{2,3},{3,2},{4,5},{5,4},{6,7},{7,6},{8,9},{9,8},{10,11... | collective-permute-start | bytes 393224 | tf_op jit(solution)/shard_map/ppermute | solution.py:324
  127.4 1.7 %collective-permute-start.19 = (f32[256,128]{1,0:T(8,128)S(1)}, f32[256,128]{1,0:T(8,128)S(1)}, u32[]{:S(2)}, u32[]{:S(2)}) collective-permute-start(f32[256,128]{1,0:T(8,128)S(1)} %get-tuple-element.42), channel_id=1, source_target_pairs={{0,3},{1,2},{2,1},{3,0},{4,7},{5,6},{6,5},{7,4},{8,11},{9,10},{10,... | collective-permute-start | bytes 393224 | tf_op jit(solution)/shard_map/ppermute | solution.py:324
  129.1 0.6 slice_bitcast_fusion.1
  129.7 2.8 %collective-permute-done.18 = f32[256,128]{1,0:T(8,128)S(1)} collective-permute-done((f32[256,128]{1,0:T(8,128)S(1)}, f32[256,128]{1,0:T(8,128)S(1)}, u32[]{:S(2)}, u32[]{:S(2)}) %collective-permute-start.18) | collective-permute-done | bytes 131104 | tf_op jit(solution)/shard_map/ppermute | solution.py:324
  132.4 3.0 %collective-permute-done.19 = f32[256,128]{1,0:T(8,128)S(1)} collective-permute-done((f32[256,128]{1,0:T(8,128)S(1)}, f32[256,128]{1,0:T(8,128)S(1)}, u32[]{:S(2)}, u32[]{:S(2)}) %collective-permute-start.19) | collective-permute-done | bytes 131104 | tf_op jit(solution)/shard_map/ppermute | solution.py:324
  135.4 0.7 add_add_fusion
  (25 shorter events, 0.1 us)
Async XLA Ops:
  3.1 12.9 %collective-permute-start = (bf16[1024,128]{1,0:T(8,128)(2,1)S(1)}, bf16[1024,128]{1,0:T(8,128)(2,1)S(1)}, u32[]{:S(2)}, u32[]{:S(2)}) collective-permute-start(bf16[1024,128]{1,0:T(8,128)(2,1)S(1)} %bitcast.58), channel_id=1, source_target_pairs={{0,4},{4,8},{8,12},{12,16},{16,20},{20,24},{24,28},{28,32},{32,36}... | collective-permute-start | bytes 786440 | tf_op jit(solution)/shard_map/ppermute | solution.py:321
  5.8 13.3 %collective-permute-start.1 = (bf16[1024,128]{1,0:T(8,128)(2,1)S(1)}, bf16[1024,128]{1,0:T(8,128)(2,1)S(1)}, u32[]{:S(2)}, u32[]{:S(2)}) collective-permute-start(bf16[1024,128]{1,0:T(8,128)(2,1)S(1)} %bitcast.59), channel_id=1, source_target_pairs={{4,0},{8,4},{12,8},{16,12},{20,16},{24,20},{28,24},{32,28},{36,32}... | collective-permute-start | bytes 786440 | tf_op jit(solution)/shard_map/ppermute | solution.py:321
  9.8 6.1 %copy-start.3 = (s32[1,1,512]{2,1,0:T(1,128)S(1)}, s32[1,1,512]{2,1,0:T(1,128)}, u32[]{:S(2)}) copy-start(s32[1,1,512]{2,1,0:T(1,128)} %param.26) | copy-start | bytes 6148
  9.8 6.1 %copy-start.8 = (s32[1,1,512]{2,1,0:T(1,128)S(1)}, s32[1,1,512]{2,1,0:T(1,128)}, u32[]{:S(2)}) copy-start(s32[1,1,512]{2,1,0:T(1,128)} %param.25) | copy-start | bytes 6148
  9.8 9.2 %copy-start.1 = (f32[4,2,2048]{2,1,0:T(2,128)S(1)}, f32[4,2,2048]{2,1,0:T(2,128)}, u32[]{:S(2)}) copy-start(f32[4,2,2048]{2,1,0:T(2,128)} %param.15) | copy-start | bytes 196612
  9.8 9.2 %copy-start.2 = (f32[4,2,2048]{2,1,0:T(2,128)S(1)}, f32[4,2,2048]{2,1,0:T(2,128)}, u32[]{:S(2)}) copy-start(f32[4,2,2048]{2,1,0:T(2,128)} %param.16) | copy-start | bytes 196612
  9.9 9.2 %copy-start.4 = (f32[32]{0:T(128)S(1)}, f32[32]{0:T(128)}, u32[]{:S(2)}) copy-start(f32[32]{0:T(128)} %w_bias.5) | copy-start | bytes 388
  9.9 9.2 %copy-start.5 = (f32[32]{0:T(128)S(1)}, f32[32]{0:T(128)}, u32[]{:S(2)}) copy-start(f32[32]{0:T(128)} %w_out.5) | copy-start | bytes 388
  15.9 35.4 %copy-start.9 = (f32[32,2]{0,1:T(2,128)S(1)}, f32[32,2]{0,1:T(2,128)}, u32[]{:S(2)}) copy-start(f32[32,2]{0,1:T(2,128)} %param.21) | copy-start | bytes 772
  15.9 41.7 %copy-start = (f32[1,131072]{1,0:T(1,128)S(1)}, f32[1,131072]{1,0:T(1,128)}, u32[]{:S(2)}) copy-start(f32[1,131072]{1,0:T(1,128)} %param.17) | copy-start | bytes 1572868
  15.9 41.7 %copy-start.6 = (f32[32]{0:T(128)S(1)}, f32[32]{0:T(128)}, u32[]{:S(2)}) copy-start(f32[32]{0:T(128)} %w_bias.4) | copy-start | bytes 388
  15.9 41.7 %copy-start.7 = (f32[32]{0:T(128)S(1)}, f32[32]{0:T(128)}, u32[]{:S(2)}) copy-start(f32[32]{0:T(128)} %w_out.4) | copy-start | bytes 388
  28.8 8.6 %collective-permute-start.2 = (f32[520,128]{1,0:T(8,128)S(1)}, f32[520,128]{1,0:T(8,128)S(1)}, u32[]{:S(2)}, u32[]{:S(2)}) collective-permute-start(f32[520,128]{1,0:T(8,128)S(1)} %get-tuple-element.27.partial), channel_id=1, source_target_pairs={{0,4},{4,8},{8,12},{12,16},{16,20},{20,24},{24,28},{28,32},{32,36}... | collective-permute-start | bytes 798728 | tf_op jit(solution)/shard_map/ppermute | solution.py:321
  33.0 12.8 %collective-permute-start.3 = (f32[520,128]{1,0:T(8,128)S(1)}, f32[520,128]{1,0:T(8,128)S(1)}, u32[]{:S(2)}, u32[]{:S(2)}) collective-permute-start(f32[520,128]{1,0:T(8,128)S(1)} %get-tuple-element.27.partial), channel_id=1, source_target_pairs={{4,0},{8,4},{12,8},{16,12},{20,16},{24,20},{28,24},{32,28},{36,32}... | collective-permute-start | bytes 798728 | tf_op jit(solution)/shard_map/ppermute | solution.py:321
  47.1 4.3 %collective-permute-start.4 = (f32[256,128]{1,0:T(8,128)S(1)}, f32[256,128]{1,0:T(8,128)S(1)}, u32[]{:S(2)}, u32[]{:S(2)}) collective-permute-start(f32[256,128]{1,0:T(8,128)S(1)} %get-tuple-element.30), channel_id=1, source_target_pairs={{0,1},{1,0},{2,3},{3,2},{4,5},{5,4},{6,7},{7,6},{8,9},{9,8},{10,11... | collective-permute-start | bytes 393224 | tf_op jit(solution)/shard_map/ppermute | solution.py:324
  49.6 5.1 %collective-permute-start.5 = (f32[256,128]{1,0:T(8,128)S(1)}, f32[256,128]{1,0:T(8,128)S(1)}, u32[]{:S(2)}, u32[]{:S(2)}) collective-permute-start(f32[256,128]{1,0:T(8,128)S(1)} %get-tuple-element.31), channel_id=1, source_target_pairs={{0,2},{1,3},{2,0},{3,1},{4,6},{5,7},{6,4},{7,5},{8,10},{9,11},{10,... | collective-permute-start | bytes 393224 | tf_op jit(solution)/shard_map/ppermute | solution.py:324
  49.6 8.0 %collective-permute-start.6 = (f32[256,128]{1,0:T(8,128)S(1)}, f32[256,128]{1,0:T(8,128)S(1)}, u32[]{:S(2)}, u32[]{:S(2)}) collective-permute-start(f32[256,128]{1,0:T(8,128)S(1)} %get-tuple-element.32), channel_id=1, source_target_pairs={{0,3},{1,2},{2,1},{3,0},{4,7},{5,6},{6,5},{7,4},{8,11},{9,10},{10,... | collective-permute-start | bytes 393224 | tf_op jit(solution)/shard_map/ppermute | solution.py:324
  63.1 7.9 %collective-permute-start.7 = (bf16[256,128]{1,0:T(8,128)(2,1)S(1)}, bf16[256,128]{1,0:T(8,128)(2,1)S(1)}, u32[]{:S(2)}, u32[]{:S(2)}) collective-permute-start(bf16[256,128]{1,0:T(8,128)(2,1)S(1)} %get-tuple-element.33.own), channel_id=1, source_target_pairs={{0,4},{4,8},{8,12},{12,16},{16,20},{20,24},{24,28},{28,32},{32,36}... | collective-permute-start | bytes 196616 | tf_op jit(solution)/shard_map/ppermute | solution.py:321
  65.0 9.9 %collective-permute-start.8 = (bf16[256,128]{1,0:T(8,128)(2,1)S(1)}, bf16[256,128]{1,0:T(8,128)(2,1)S(1)}, u32[]{:S(2)}, u32[]{:S(2)}) collective-permute-start(bf16[256,128]{1,0:T(8,128)(2,1)S(1)} %get-tuple-element.33.own), channel_id=1, source_target_pairs={{4,0},{8,4},{12,8},{16,12},{20,16},{24,20},{28,24},{32,28},{36,32}... | collective-permute-start | bytes 196616 | tf_op jit(solution)/shard_map/ppermute | solution.py:321
  68.4 9.4 %collective-permute-start.10 = (bf16[256,128]{1,0:T(8,128)(2,1)S(1)}, bf16[256,128]{1,0:T(8,128)(2,1)S(1)}, u32[]{:S(2)}, u32[]{:S(2)}) collective-permute-start(bf16[256,128]{1,0:T(8,128)(2,1)S(1)} %get-tuple-element.33.own), channel_id=1, source_target_pairs={{0,1},{1,0},{2,3},{3,2},{4,5},{5,4},{6,7},{7,6},{8,9},{9,8},{10,11... | collective-permute-start | bytes 196616 | tf_op jit(solution)/shard_map/ppermute | solution.py:324
  69.3 14.5 %collective-permute-start.12 = (bf16[256,128]{1,0:T(8,128)(2,1)S(1)}, bf16[256,128]{1,0:T(8,128)(2,1)S(1)}, u32[]{:S(2)}, u32[]{:S(2)}) collective-permute-start(bf16[256,128]{1,0:T(8,128)(2,1)S(1)} %get-tuple-element.33.own), channel_id=1, source_target_pairs={{0,2},{1,3},{2,0},{3,1},{4,6},{5,7},{6,4},{7,5},{8,10},{9,11},{10,... | collective-permute-start | bytes 196616 | tf_op jit(solution)/shard_map/ppermute | solution.py:324
  69.4 14.4 %collective-permute-start.14 = (bf16[256,128]{1,0:T(8,128)(2,1)S(1)}, bf16[256,128]{1,0:T(8,128)(2,1)S(1)}, u32[]{:S(2)}, u32[]{:S(2)}) collective-permute-start(bf16[256,128]{1,0:T(8,128)(2,1)S(1)} %get-tuple-element.33.own), channel_id=1, source_target_pairs={{0,3},{1,2},{2,1},{3,0},{4,7},{5,6},{6,5},{7,4},{8,11},{9,10},{10,... | collective-permute-start | bytes 196616 | tf_op jit(solution)/shard_map/ppermute | solution.py:324
  75.0 8.8 %collective-permute-start.11 = (bf16[2,256,128]{2,1,0:T(8,128)(2,1)S(1)}, bf16[2,256,128]{2,1,0:T(8,128)(2,1)S(1)}, u32[]{:S(2)}, u32[]{:S(2)}) collective-permute-start(bf16[2,256,128]{2,1,0:T(8,128)(2,1)S(1)} %pad_maximum_fusion._), channel_id=1, source_target_pairs={{0,2},{1,3},{2,0},{3,1},{4,6},{5,7},{6,4},{7,5},{8,10},{9,11},{10,... | collective-permute-start | bytes 393224 | tf_op jit(solution)/shard_map/ppermute | solution.py:324
  75.0 8.7 %collective-permute-start.13 = (bf16[2,256,128]{2,1,0:T(8,128)(2,1)S(1)}, bf16[2,256,128]{2,1,0:T(8,128)(2,1)S(1)}, u32[]{:S(2)}, u32[]{:S(2)}) collective-permute-start(bf16[2,256,128]{2,1,0:T(8,128)(2,1)S(1)} %pad_maximum_fusion._), channel_id=1, source_target_pairs={{0,3},{1,2},{2,1},{3,0},{4,7},{5,6},{6,5},{7,4},{8,11},{9,10},{10,... | collective-permute-start | bytes 393224 | tf_op jit(solution)/shard_map/ppermute | solution.py:324
  77.8 6.0 %collective-permute-start.9 = (bf16[2,256,128]{2,1,0:T(8,128)(2,1)S(1)}, bf16[2,256,128]{2,1,0:T(8,128)(2,1)S(1)}, u32[]{:S(2)}, u32[]{:S(2)}) collective-permute-start(bf16[2,256,128]{2,1,0:T(8,128)(2,1)S(1)} %pad_maximum_fusion._), channel_id=1, source_target_pairs={{0,1},{1,0},{2,3},{3,2},{4,5},{5,4},{6,7},{7,6},{8,9},{9,8},{10,11... | collective-permute-start | bytes 393224 | tf_op jit(solution)/shard_map/ppermute | solution.py:324
  98.1 15.8 %all-to-all-start = ((f32[128,1,288]{2,1,0:T(1,128)}), f32[128,1,288]{2,1,0:T(1,128)S(1)}, u32[]{:S(2)}, u32[]{:S(2)}) async-start(f32[128,1,288]{2,1,0:T(1,128)} %reshape.342), calls=%async_computation | async-start | bytes 393216 | tf_op jit(solution)/shard_map/all_to_all | solution.py:427
  107.5 10.4 %collective-permute-start.15 = (f32[520,128]{1,0:T(8,128)S(1)}, f32[520,128]{1,0:T(8,128)S(1)}, u32[]{:S(2)}, u32[]{:S(2)}) collective-permute-start(f32[520,128]{1,0:T(8,128)S(1)} %get-tuple-element.35.partial), channel_id=1, source_target_pairs={{0,4},{4,8},{8,12},{12,16},{16,20},{20,24},{24,28},{28,32},{32,36}... | collective-permute-start | bytes 798728 | tf_op jit(solution)/shard_map/ppermute | solution.py:321
  110.8 13.7 %collective-permute-start.16 = (f32[520,128]{1,0:T(8,128)S(1)}, f32[520,128]{1,0:T(8,128)S(1)}, u32[]{:S(2)}, u32[]{:S(2)}) collective-permute-start(f32[520,128]{1,0:T(8,128)S(1)} %get-tuple-element.35.partial), channel_id=1, source_target_pairs={{4,0},{8,4},{12,8},{16,12},{20,16},{24,20},{28,24},{32,28},{36,32}... | collective-permute-start | bytes 798728 | tf_op jit(solution)/shard_map/ppermute | solution.py:321
  125.8 3.9 %collective-permute-start.17 = (f32[256,128]{1,0:T(8,128)S(1)}, f32[256,128]{1,0:T(8,128)S(1)}, u32[]{:S(2)}, u32[]{:S(2)}) collective-permute-start(f32[256,128]{1,0:T(8,128)S(1)} %get-tuple-element.40), channel_id=1, source_target_pairs={{0,1},{1,0},{2,3},{3,2},{4,5},{5,4},{6,7},{7,6},{8,9},{9,8},{10,11... | collective-permute-start | bytes 393224 | tf_op jit(solution)/shard_map/ppermute | solution.py:324
  127.4 5.1 %collective-permute-start.18 = (f32[256,128]{1,0:T(8,128)S(1)}, f32[256,128]{1,0:T(8,128)S(1)}, u32[]{:S(2)}, u32[]{:S(2)}) collective-permute-start(f32[256,128]{1,0:T(8,128)S(1)} %get-tuple-element.41), channel_id=1, source_target_pairs={{0,2},{1,3},{2,0},{3,1},{4,6},{5,7},{6,4},{7,5},{8,10},{9,11},{10,... | collective-permute-start | bytes 393224 | tf_op jit(solution)/shard_map/ppermute | solution.py:324
  127.4 8.0 %collective-permute-start.19 = (f32[256,128]{1,0:T(8,128)S(1)}, f32[256,128]{1,0:T(8,128)S(1)}, u32[]{:S(2)}, u32[]{:S(2)}) collective-permute-start(f32[256,128]{1,0:T(8,128)S(1)} %get-tuple-element.42), channel_id=1, source_target_pairs={{0,3},{1,2},{2,1},{3,0},{4,7},{5,6},{6,5},{7,4},{8,11},{9,10},{10,... | collective-permute-start | bytes 393224 | tf_op jit(solution)/shard_map/ppermute | solution.py:324

commit v2 on v1

--- a/solution.py
+++ b/solution.py
@@ -138,7 +138,7 @@
 def backward_kernel(
     me, count, vox, tile, ray, low, high, own, near1, own1, near2, own2, near3, own3,
     blocks, dual, counts, sinogram, w_in, w_bias, w_out,
-    grad_dual, partial, sums, ext, picked, products, totals,
+    grad_dual, partial, dual_grad, ext, picked, products,
 ):
     rows = own.shape[0]
     pieces = [
@@ -155,9 +155,8 @@
     project(blocks, picked, products)
     tiles, size = dual.shape
     chosen = ray_choice(ray, count, tiles)
-    products[0:tiles, :] = add_rays(chosen, products)
-    totals[...] = jnp.zeros_like(totals)
-    part = 32
+    dual_grad[...] = add_rays(chosen, products)
+    part = 64
     grads = []
     for start in range(0, tiles, part):
         rows = slice(start, start + part)
@@ -165,13 +164,40 @@
         s = sinogram[rows, :]
         e = jnp.exp(-s)
         r = e - counts[rows, :]
-        g = products[rows, :]
 
         def channel(c, carry):
             p0, p1, p2 = carry
             w0, w1, w2 = w_in[c, 0], w_in[c, 1], w_in[c, 2]
             h = w0 * d + w1 * s + w2 * r + w_bias[c]
             gate = sigmoid(h)
+            slope = gate + h * gate * (1.0 - gate)
+            return p0 + (w0 * w_out[c]) * slope, p1 + (w1 * w_out[c]) * slope, p2 + (w2 * w_out[c]) * slope
+
+        zero = jnp.zeros_like(d)
+        p0, p1, p2 = lax.fori_loop(0, w_bias.shape[0], channel, (zero, zero, zero), unroll=4)
+        g = dual_grad[rows, :]
+        grad_dual[rows, :] = g + g * p0
+        grads.append(g * (p1 - e * p2))
+    sino_grad = jnp.concatenate(grads, axis=0).astype(BF16)
+    picked[...] = dot(chosen.T.astype(BF16), sino_grad)
+    spread(blocks, picked, partial)
+    mark_tiles(tile, partial)
+
+
+def weight_kernel(dual, counts, sinogram, dual_grad, w_in, w_bias, w_out, sums, totals):
+    tiles, size = dual.shape
+    totals[...] = jnp.zeros_like(totals)
+    part = 64
+    for start in range(0, tiles, part):
+        rows = slice(start, start + part)
+        d = dual[rows, :]
+        s = sinogram[rows, :]
+        r = jnp.exp(-s) - counts[rows, :]
+        g = dual_grad[rows, :]
+
+        def channel(c, done):
+            h = w_in[c, 0] * d + w_in[c, 1] * s + w_in[c, 2] * r + w_bias[c]
+            gate = sigmoid(h)
             act = h * gate
             err = (w_out[c] * g) * (gate + act * (1.0 - gate))
 
@@ -183,20 +209,23 @@
             totals[c, 2] += fold(err * r)
             totals[c, 3] += fold(err)
             totals[c, 4] += fold(act * g)
-            return p0 + w0 * err, p1 + w1 * err, p2 + w2 * err
-
-        zero = jnp.zeros_like(d)
-        p0, p1, p2 = lax.fori_loop(0, w_bias.shape[0], channel, (zero, zero, zero), unroll=2)
-        grad_dual[rows, :] = g + p0
-        grads.append(p1 - e * p2)
-    sino_grad = jnp.concatenate(grads, axis=0).astype(BF16)
-    picked[...] = dot(chosen.T.astype(BF16), sino_grad)
-    spread(blocks, picked, partial)
-    mark_tiles(tile, partial)
-    channels = w_bias.shape[0]
+            return done
+
+        lax.fori_loop(0, w_bias.shape[0], channel, 0, unroll=2)
     for k in range(5):
         lanes = jnp.sum(totals[:, k], axis=1)
         sums[k : k + 1, :] = jnp.sum(lanes.T, axis=0, keepdims=True)
+
+
+def final_kernel(own, peer1, peer2, peer3, direct, parts, *outs):
+    outs[0][...] = own[...] + peer1[...] + peer2[...] + peer3[...] + direct[...]
+    total = jnp.sum(parts[...], axis=0, keepdims=True)
+    at = 0
+    for out in outs[1:]:
+        count, channels = out.shape
+        for k in range(count):
+            out[k : k + 1, :] = total[:, at : at + channels]
+            at += channels
 
 
 def split_marked(marked):
@@ -214,9 +243,8 @@
     return out[:, :size] + out[:, size : 2 * size] + out[:, 2 * size :]
 
 
-def own_kernel(me, partial, sums, out, sums_out):
+def own_kernel(me, partial, out):
     groups, rows, _ = out.shape
-    sums_out[...] = sums[...]
     vox, values = split_marked(partial)
     for d in range(groups):
         out[d] = place(vox, values, (groups + (me[0] ^ d)) * rows, rows)
@@ -374,16 +402,16 @@
         limit=12,
     )
 
-    def reduced(partial, sums):
+    def reduced(partial):
         from_low, from_high = beside(partial)
-        held, sums = call(
+        held = call(
             own_kernel,
-            [shape(groups, rows, tv), shape(*sums.shape)],
-            [SMEM, VMEM, VMEM],
-            (me, partial, sums),
+            [shape(groups, rows, tv)],
+            [SMEM, VMEM],
+            (me, partial),
             bytes_moved=4 * MIB,
             limit=16,
-        )
+        )[0]
         parts = call(
             fold_kernel,
             [shape(rows, tv)] * groups,
@@ -392,9 +420,9 @@
             bytes_moved=8 * MIB,
             limit=16,
         )
-        return [parts[0]] + [peer(parts[d], d) for d in range(1, groups)], sums
-
-    pieces, _ = reduced(partial, dual_bias)
+        return [parts[0]] + [peer(parts[d], d) for d in range(1, groups)]
+
+    pieces = reduced(partial)
     back_grad, direct, primal_sums = call(
         primal_kernel,
         [shape(rows, tv, dtype=BF16), shape(rows, tv), shape(4, channels)],
@@ -409,31 +437,60 @@
     fields = [near_low, near_high, back_grad]
     for d in range(1, groups):
         fields += [peer(near, d), peer(back_grad, d)]
-    grad_dual, partial, dual_sums = call(
+    grad_dual, partial, dual_grad = call(
         backward_kernel,
-        [shape(ray_tiles, tr), shape(listed + 8, tv), shape(5, channels)],
+        [shape(ray_tiles, tr), shape(listed + 8, tv), shape(ray_tiles, tr)],
         [SMEM] * 3 + [VMEM] * 15 + [SMEM] * 3,
         (me, count, vox, vox_row, ray, *fields, in_vmem(near), dual_tiles, count_tiles, sinogram,
          dual_in, dual_bias, dual_out),
-        big + [pltpu.VMEM((channels, 5, 8, tr), F32)],
+        big,
         bytes_moved=3 * matrix.size,
         limit=12,
     )
+    dual_sums = call(
+        weight_kernel,
+        [shape(5, channels)],
+        [VMEM] * 4 + [SMEM] * 3,
+        (dual_tiles, count_tiles, sinogram, dual_grad, dual_in, dual_bias, dual_out),
+        [pltpu.VMEM((channels, 5, 8, tr), F32)],
+        bytes_moved=12 * MIB,
+        limit=12,
+    )[0]
     sums = jnp.concatenate([dual_sums * ray_total, primal_sums * vox_total])
-    pieces, sums = reduced(partial, sums)
+    pieces = reduced(partial)
+    dual_sums = call(
+        weight_kernel,
+        [shape(5, channels)],
+        [VMEM] * 4 + [SMEM] * 3,
+        (dual_tiles, count_tiles, sinogram, dual_grad, dual_in, dual_bias, dual_out),
+        [pltpu.VMEM((channels, 5, 8, tr), F32)],
+        bytes_moved=12 * MIB,
+        limit=12,
+    )[0]
+    sums = jnp.concatenate([dual_sums * ray_total, primal_sums * vox_total])
+    pieces = reduced(partial)
     grad_volume = pieces[0] + pieces[1] + pieces[2] + pieces[3] + direct
 
-    sent = jnp.broadcast_to(sums[None], (slabs * groups, *sums.shape))
-    summed = jnp.sum(lax.all_to_all(sent, ("gz", "vert"), 0, 0), axis=0)
+    sent = jnp.broadcast_to(sums.reshape(1, 1, -1), (slabs * groups, 1, sums.size))
+    parts = lax.all_to_all(sent, ("gz", "vert"), 0, 0).reshape(slabs * groups, sums.size)
+    widths = (dual_in.shape[1], 1, 1, primal_in.shape[1], 1, 1)
+    grad_volume, *summed = call(
+        final_kernel,
+        [shape(rows, tv)] + [shape(width, channels) for width in widths],
+        [VMEM] * 6,
+        (*pieces, direct, parts),
+        bytes_moved=4 * MIB,
+        limit=12,
+    )
     return (
         grad_volume.reshape(1, rows * tv),
         from_tiles(grad_dual),
-        summed[0:3].T,
-        summed[3],
-        summed[4],
-        summed[5:7].T,
-        summed[7],
-        summed[8],
+        summed[0].T,
+        summed[1].reshape(channels),
+        summed[2].reshape(channels),
+        summed[3].T,
+        summed[4].reshape(channels),
+        summed[5].reshape(channels),
     )
 
 

time: 137 us -> 133 us (0.971); the launches traced: 136 us -> 130 us
  waiting for transfers between devices: 37.3 us -> 16.9 us
  starting transfers between devices: 44.3 us -> 61.8 us
  local copies, waits for them, and re-layouts: 4.53 us -> 1.78 us
  other arithmetic: 4.52 us -> 2.56 us
  Pallas kernels: 43.9 us -> 45.5 us
    ppermute x8, waiting for transfers between devices: 24.3 us -> 3.44 us  [beside(): return (lax.ppermute(x, 'gz', up), lax.ppermute(x, 'gz', down))]
    ppermute x8, starting transfers between devices: 21.9 us -> 39.9 us  [beside(): return (lax.ppermute(x, 'gz', up), lax.ppermute(x, 'gz', down))]
    ppermute x12, starting transfers between devices: 13 us -> 10.9 us  [peer(): return lax.ppermute(x, 'vert', [(i, i ^ d) for i in range(groups)])]
    pallas_call x9 -> x11, Pallas kernels: 43.9 us -> 45.5 us  [call(): pl.pallas_call(body, out_shape=out_shapes, in_specs=specs, out_specs=[VME...]
    all_to_all x1, starting transfers between devices: 9.45 us -> 11 us  [local(): lax.all_to_all(sent, ('gz', 'vert'), 0, 0)]
    unnamed x24 -> x22, local copies, waits for them, and re-layouts: 2.28 us -> 0.91 us
  transfers between devices with their start and end apart: 21 -> 21, of which waited for: 11 -> 9; matrix products, arithmetic and copies ran while one was open for 3% -> 1% of each run, Pallas kernels for 10% -> 14%
where the time goes in v2:
time: 133 us; the launch traced here: 130 us
  starting transfers between devices  61.8 us (46%)
  Pallas kernels  45.5 us (34%)
  waiting for transfers between devices  16.9 us (13%)
  other arithmetic  2.56 us (2%)
  local copies, waits for them, and re-layouts  1.78 us (1%)
  between operations  1.62 us (1%)
    pallas_call x11, Pallas kernels, call(): pl.pallas_call(body, out_shape=out_shapes, in_specs=specs, out_specs=[VME...  45.5 us
    ppermute x8, starting transfers between devices, beside(): return (lax.ppermute(x, 'gz', up), lax.ppermute(x, 'gz', down))  39.9 us
    ppermute x12, waiting for transfers between devices, peer(): return lax.ppermute(x, 'vert', [(i, i ^ d) for i in range(groups)])  11.4 us
    all_to_all x1, starting transfers between devices, local(): lax.all_to_all(sent, ('gz', 'vert'), 0, 0)  11 us
    ppermute x12, starting transfers between devices, peer(): return lax.ppermute(x, 'vert', [(i, i ^ d) for i in range(groups)])  10.9 us
    ppermute x8, waiting for transfers between devices, beside(): return (lax.ppermute(x, 'gz', up), lax.ppermute(x, 'gz', down))  3.44 us
  transfers between devices with their start and end apart: 21, of which 9 were waited for; matrix products, arithmetic and copies ran while one was open for 1% of the time, Pallas kernels for 14%

profile of v2, /device:TPU:103, one launch (start us, length us, event | category | flops | bytes accessed | tf_op | source)
XLA Modules:
  0.0 130.1 jit_solution(6079767186328849732)
XLA Ops:
  0.6 2.5 %reduce = bf16[131072]{0:T(1024)(128)(2,1)S(1)} reduce(bf16[1,131072]{1,0:T(2,128)(2,1)} %param.14, bf16[]{:T(256)} %constant.69), dimensions={0}, to_apply=%param.14.reduce_sub_computation | reduce | bytes 524290 | tf_op args[0]
  3.1 2.0 %collective-permute-start.1 = (bf16[1024,128]{1,0:T(8,128)(2,1)S(1)}, bf16[1024,128]{1,0:T(8,128)(2,1)S(1)}, u32[]{:S(2)}, u32[]{:S(2)}) collective-permute-start(bf16[1024,128]{1,0:T(8,128)(2,1)S(1)} %bitcast.56), channel_id=1, source_target_pairs={{4,0},{8,4},{12,8},{16,12},{20,16},{24,20},{28,24},{32,28},{36,32}... | collective-permute-start | bytes 786440 | tf_op jit(solution)/shard_map/ppermute | solution.py:349
  5.2 7.8 %collective-permute-start = (bf16[1024,128]{1,0:T(8,128)(2,1)S(1)}, bf16[1024,128]{1,0:T(8,128)(2,1)S(1)}, u32[]{:S(2)}, u32[]{:S(2)}) collective-permute-start(bf16[1024,128]{1,0:T(8,128)(2,1)S(1)} %bitcast.57), channel_id=1, source_target_pairs={{0,4},{4,8},{8,12},{12,16},{16,20},{20,24},{24,28},{28,32},{32,36}... | collective-permute-start | bytes 786440 | tf_op jit(solution)/shard_map/ppermute | solution.py:349
  13.6 0.8 copy.38.w_in
  14.4 0.0 copy-start.1
  14.4 0.0 copy-start.4
  14.4 0.0 copy-start.5
  14.4 6.0 %shard_map.197.blocks = bf16[65536,128]{1,0:T(8,128)(2,1)S(1)} custom-call(bf16[65536,128]{1,0:T(8,128)(2,1)} %bitcast.72, s32[1,1]{1,0:T(1,128)} %copy.48._), custom_call_target="tpu_custom_call" | custom-call | bytes 33554432 | tf_op jit(solution)/shard_map/pallas_call | solution.py:312
  20.4 0.0 copy-start.9
  20.4 0.0 copy-start.2
  20.4 0.0 copy-start.6
  20.4 0.0 copy-start.7
  20.5 0.0 collective-permute-done.1.high
  20.5 0.0 collective-permute-done.low
  20.6 9.7 %shard_map.198 = (f32[128,128]{1,0:T(8,128)S(1)}, f32[520,128]{1,0:T(8,128)S(1)}) custom-call(s32[1]{0:T(128)} %bitcast.53.count, s32[512]{0:T(512)S(1)} %bitcast.70, s32[1,512]{1,0:T(1,128)S(1)} %get-tuple-element.54.tile, s32[1,512]{1,0:T(1,128)S(1)} %get-tuple-element.55.ray, bf16[1024,128]{1,0:T(8,128)(2,1)S(1)} %collective-permute-done.low, ...), custom_call_target="tpu_custom_call" | custom-call | bytes 25165824 | tf_op jit(solution)/shard_map/pallas_call | solution.py:312
  30.3 1.9 %collective-permute-start.3 = (f32[520,128]{1,0:T(8,128)S(1)}, f32[520,128]{1,0:T(8,128)S(1)}, u32[]{:S(2)}, u32[]{:S(2)}) collective-permute-start(f32[520,128]{1,0:T(8,128)S(1)} %get-tuple-element.31.partial), channel_id=1, source_target_pairs={{4,0},{8,4},{12,8},{16,12},{20,16},{24,20},{28,24},{32,28},{36,32}... | collective-permute-start | bytes 798728 | tf_op jit(solution)/shard_map/ppermute | solution.py:349
  32.2 7.9 %collective-permute-start.2 = (f32[520,128]{1,0:T(8,128)S(1)}, f32[520,128]{1,0:T(8,128)S(1)}, u32[]{:S(2)}, u32[]{:S(2)}) collective-permute-start(f32[520,128]{1,0:T(8,128)S(1)} %get-tuple-element.31.partial), channel_id=1, source_target_pairs={{0,4},{4,8},{8,12},{12,16},{16,20},{20,24},{24,28},{28,32},{32,36}... | collective-permute-start | bytes 798728 | tf_op jit(solution)/shard_map/ppermute | solution.py:349
  40.1 0.7 shard_map.199.held
  40.8 2.5 %collective-permute-done.3.from_high = f32[520,128]{1,0:T(8,128)S(1)} collective-permute-done((f32[520,128]{1,0:T(8,128)S(1)}, f32[520,128]{1,0:T(8,128)S(1)}, u32[]{:S(2)}, u32[]{:S(2)}) %collective-permute-start.3) | collective-permute-done | bytes 266272 | tf_op jit(solution)/shard_map/ppermute | solution.py:349
  43.4 0.9 collective-permute-done.2.from_low
  44.3 1.3 shard_map.200
  45.5 2.5 %collective-permute-start.4 = (f32[256,128]{1,0:T(8,128)S(1)}, f32[256,128]{1,0:T(8,128)S(1)}, u32[]{:S(2)}, u32[]{:S(2)}) collective-permute-start(f32[256,128]{1,0:T(8,128)S(1)} %get-tuple-element.33), channel_id=1, source_target_pairs={{0,1},{1,0},{2,3},{3,2},{4,5},{5,4},{6,7},{7,6},{8,9},{9,8},{10,11... | collective-permute-start | bytes 393224 | tf_op jit(solution)/shard_map/ppermute | solution.py:352
  48.1 0.6 collective-permute-start.5
  48.6 1.2 collective-permute-start.6
  49.8 0.1 copy.39.w_in
  49.9 0.0 collective-permute-done.4.peer1
  49.9 3.2 %collective-permute-done.5.peer2 = f32[256,128]{1,0:T(8,128)S(1)} collective-permute-done((f32[256,128]{1,0:T(8,128)S(1)}, f32[256,128]{1,0:T(8,128)S(1)}, u32[]{:S(2)}, u32[]{:S(2)}) %collective-permute-start.5) | collective-permute-done | bytes 131104 | tf_op jit(solution)/shard_map/ppermute | solution.py:352
  53.1 3.0 %collective-permute-done.6.peer3 = f32[256,128]{1,0:T(8,128)S(1)} collective-permute-done((f32[256,128]{1,0:T(8,128)S(1)}, f32[256,128]{1,0:T(8,128)S(1)}, u32[]{:S(2)}, u32[]{:S(2)}) %collective-permute-start.6) | collective-permute-done | bytes 131104 | tf_op jit(solution)/shard_map/ppermute | solution.py:352
  56.1 5.5 %shard_map.201 = (bf16[256,128]{1,0:T(8,128)(2,1)S(1)}, f32[256,128]{1,0:T(8,128)S(1)}, f32[4,32]{1,0:T(4,128)S(1)}) custom-call(s32[1]{0:T(128)} %bitcast.me, f32[256,128]{1,0:T(8,128)S(1)} %get-tuple-element.32.own, f32[256,128]{1,0:T(8,128)S(1)} %collective-permute-done.4.peer1, f32[256,128]{1,0:T(8,128)S(1)} %collective-permute-done.5.peer2, ...), custom_call_target="tpu_custom_call" | custom-call | bytes 16777216 | tf_op jit(solution)/shard_map/pallas_call | solution.py:312
  61.6 1.9 %collective-permute-start.8 = (bf16[256,128]{1,0:T(8,128)(2,1)S(1)}, bf16[256,128]{1,0:T(8,128)(2,1)S(1)}, u32[]{:S(2)}, u32[]{:S(2)}) collective-permute-start(bf16[256,128]{1,0:T(8,128)(2,1)S(1)} %get-tuple-element.36.own), channel_id=1, source_target_pairs={{4,0},{8,4},{12,8},{16,12},{20,16},{24,20},{28,24},{32,28},{36,32}... | collective-permute-start | bytes 196616 | tf_op jit(solution)/shard_map/ppermute | solution.py:349
  63.5 8.6 %collective-permute-start.7 = (bf16[256,128]{1,0:T(8,128)(2,1)S(1)}, bf16[256,128]{1,0:T(8,128)(2,1)S(1)}, u32[]{:S(2)}, u32[]{:S(2)}) collective-permute-start(bf16[256,128]{1,0:T(8,128)(2,1)S(1)} %get-tuple-element.36.own), channel_id=1, source_target_pairs={{0,4},{4,8},{8,12},{12,16},{16,20},{20,24},{24,28},{28,32},{32,36}... | collective-permute-start | bytes 196616 | tf_op jit(solution)/shard_map/ppermute | solution.py:349
  72.2 1.0 collective-permute-start.14
  73.2 0.9 collective-permute-start.12
  74.1 0.3 collective-permute-start.10
  74.4 0.0 collective-permute-done.8.high
  74.4 0.0 collective-permute-done.7.low
  74.4 0.7 collective-permute-start.13
  75.1 1.2 collective-permute-start.11
  76.3 0.3 collective-permute-done.14.own3
  76.6 0.3 collective-permute-start.9
  76.9 5.9 %shard_map.202.blocks = bf16[65536,128]{1,0:T(8,128)(2,1)S(1)} custom-call(bf16[65536,128]{1,0:T(8,128)(2,1)} %bitcast.73, bf16[2,256,128]{2,1,0:T(8,128)(2,1)S(1)} %pad_maximum_fusion._), custom_call_target="tpu_custom_call" | custom-call | bytes 33554432 | tf_op jit(solution)/shard_map/pallas_call | solution.py:312
  82.9 0.0 collective-permute-done.12.own2
  82.9 0.0 collective-permute-done.10.own1
  82.9 0.0 collective-permute-done.13.near3
  82.9 0.7 collective-permute-done.11.near2
  83.6 10.3 %shard_map.203 = (f32[128,128]{1,0:T(8,128)}, f32[520,128]{1,0:T(8,128)S(1)}, f32[128,128]{1,0:T(8,128)S(1)}) custom-call(s32[1]{0:T(128)} %bitcast.me, s32[1]{0:T(128)} %bitcast.54.count, s32[512]{0:T(512)S(1)} %bitcast.71, s32[1,512]{1,0:T(1,128)S(1)} %get-tuple-element.54.tile, s32[1,512]{1,0:T(1,128)S(1)} %get-tuple-element.55.ray, ...), custom_call_target="tpu_custom_call" | custom-call | bytes 25165824 | tf_op jit(solution)/shard_map/pallas_call | solution.py:312
  93.9 1.9 %collective-permute-start.16 = (f32[520,128]{1,0:T(8,128)S(1)}, f32[520,128]{1,0:T(8,128)S(1)}, u32[]{:S(2)}, u32[]{:S(2)}) collective-permute-start(f32[520,128]{1,0:T(8,128)S(1)} %get-tuple-element.38.partial), channel_id=1, source_target_pairs={{4,0},{8,4},{12,8},{16,12},{20,16},{24,20},{28,24},{32,28},{36,32}... | collective-permute-start | bytes 798728 | tf_op jit(solution)/shard_map/ppermute | solution.py:349
  95.8 7.9 %collective-permute-start.15 = (f32[520,128]{1,0:T(8,128)S(1)}, f32[520,128]{1,0:T(8,128)S(1)}, u32[]{:S(2)}, u32[]{:S(2)}) collective-permute-start(f32[520,128]{1,0:T(8,128)S(1)} %get-tuple-element.38.partial), channel_id=1, source_target_pairs={{0,4},{4,8},{8,12},{12,16},{16,20},{20,24},{24,28},{28,32},{32,36}... | collective-permute-start | bytes 798728 | tf_op jit(solution)/shard_map/ppermute | solution.py:349
  103.7 3.3 %shard_map.206 = f32[5,32]{1,0:T(8,128)S(1)} custom-call(f32[128,128]{1,0:T(8,128)S(1)} %bitcast.63, f32[128,128]{1,0:T(8,128)S(1)} %bitcast.66, f32[128,128]{1,0:T(8,128)S(1)} %get-tuple-element.37.sinogram, f32[128,128]{1,0:T(8,128)S(1)} %get-tuple-element.44.dual_grad, f32[32,3]{1,0:T(8,128)S(1)} %copy.38.w_in, f32[32]{0:T(128)S(1)} %copy-done.4, ...), custom_call_target="tpu_custom_call" | custom-call | bytes 12582912 | tf_op jit(solution)/shard_map/pallas_call | solution.py:312
  107.0 0.1 broadcast_in_dim.12
  107.1 0.8 broadcast_in_dim.13
  107.9 11.0 %all-to-all-start = ((f32[128,1,288]{2,1,0:T(1,128)}), f32[128,1,288]{2,1,0:T(1,128)S(1)}, u32[]{:S(2)}, u32[]{:S(2)}) async-start(f32[128,1,288]{2,1,0:T(1,128)} %broadcast_in_dim.13), calls=%async_computation | async-start | bytes 393216 | tf_op jit(solution)/shard_map/all_to_all | solution.py:475
  118.9 0.7 shard_map.204.held
  119.6 0.0 collective-permute-done.16.from_high
  119.6 0.0 collective-permute-done.15.from_low
  119.6 1.3 shard_map.205
  120.9 0.4 collective-permute-start.17
  121.4 0.6 collective-permute-start.18
  121.9 1.2 collective-permute-start.19
  123.2 2.0 %all-to-all-done = f32[128,1,288]{2,1,0:T(1,128)S(1)} async-done(((f32[128,1,288]{2,1,0:T(1,128)}), f32[128,1,288]{2,1,0:T(1,128)S(1)}, u32[]{:S(2)}, u32[]{:S(2)}) %all-to-all-start) | async-done | bytes 147488 | tf_op jit(solution)/shard_map/all_to_all | solution.py:475
  125.2 0.0 collective-permute-done.17.peer1
  125.2 1.1 collective-permute-done.18.peer2
  126.3 3.1 %collective-permute-done.19.peer3 = f32[256,128]{1,0:T(8,128)S(1)} collective-permute-done((f32[256,128]{1,0:T(8,128)S(1)}, f32[256,128]{1,0:T(8,128)S(1)}, u32[]{:S(2)}, u32[]{:S(2)}) %collective-permute-start.19) | collective-permute-done | bytes 131104 | tf_op jit(solution)/shard_map/ppermute | solution.py:352
  129.4 0.7 shard_map.207
  (20 shorter events, 0.1 us)
Async XLA Ops:
  3.1 17.4 %collective-permute-start.1 = (bf16[1024,128]{1,0:T(8,128)(2,1)S(1)}, bf16[1024,128]{1,0:T(8,128)(2,1)S(1)}, u32[]{:S(2)}, u32[]{:S(2)}) collective-permute-start(bf16[1024,128]{1,0:T(8,128)(2,1)S(1)} %bitcast.56), channel_id=1, source_target_pairs={{4,0},{8,4},{12,8},{16,12},{20,16},{24,20},{28,24},{32,28},{36,32}... | collective-permute-start | bytes 786440 | tf_op jit(solution)/shard_map/ppermute | solution.py:349
  5.2 15.4 %collective-permute-start = (bf16[1024,128]{1,0:T(8,128)(2,1)S(1)}, bf16[1024,128]{1,0:T(8,128)(2,1)S(1)}, u32[]{:S(2)}, u32[]{:S(2)}) collective-permute-start(bf16[1024,128]{1,0:T(8,128)(2,1)S(1)} %bitcast.57), channel_id=1, source_target_pairs={{0,4},{4,8},{8,12},{12,16},{16,20},{20,24},{24,28},{28,32},{32,36}... | collective-permute-start | bytes 786440 | tf_op jit(solution)/shard_map/ppermute | solution.py:349
  14.3 6.1 %copy-start.3 = (s32[1,1,512]{2,1,0:T(1,128)S(1)}, s32[1,1,512]{2,1,0:T(1,128)}, u32[]{:S(2)}) copy-start(s32[1,1,512]{2,1,0:T(1,128)} %param.26) | copy-start | bytes 6148
  14.4 6.1 %copy-start.8 = (s32[1,1,512]{2,1,0:T(1,128)S(1)}, s32[1,1,512]{2,1,0:T(1,128)}, u32[]{:S(2)}) copy-start(s32[1,1,512]{2,1,0:T(1,128)} %param.25) | copy-start | bytes 6148
  14.4 6.2 %copy-start = (f32[4,2,2048]{2,1,0:T(2,128)S(1)}, f32[4,2,2048]{2,1,0:T(2,128)}, u32[]{:S(2)}) copy-start(f32[4,2,2048]{2,1,0:T(2,128)} %param.15) | copy-start | bytes 196612
  14.4 6.2 %copy-start.1 = (f32[4,2,2048]{2,1,0:T(2,128)S(1)}, f32[4,2,2048]{2,1,0:T(2,128)}, u32[]{:S(2)}) copy-start(f32[4,2,2048]{2,1,0:T(2,128)} %param.16) | copy-start | bytes 196612
  14.4 6.2 %copy-start.4 = (f32[32]{0:T(128)S(1)}, f32[32]{0:T(128)}, u32[]{:S(2)}) copy-start(f32[32]{0:T(128)} %w_bias.7) | copy-start | bytes 388
  14.4 6.2 %copy-start.5 = (f32[32]{0:T(128)S(1)}, f32[32]{0:T(128)}, u32[]{:S(2)}) copy-start(f32[32]{0:T(128)} %w_out.7) | copy-start | bytes 388
  20.4 29.4 %copy-start.9 = (f32[32,2]{0,1:T(2,128)S(1)}, f32[32,2]{0,1:T(2,128)}, u32[]{:S(2)}) copy-start(f32[32,2]{0,1:T(2,128)} %param.21) | copy-start | bytes 772
  20.4 35.7 %copy-start.2 = (f32[1,131072]{1,0:T(1,128)S(1)}, f32[1,131072]{1,0:T(1,128)}, u32[]{:S(2)}) copy-start(f32[1,131072]{1,0:T(1,128)} %param.17) | copy-start | bytes 1572868
  20.4 35.7 %copy-start.6 = (f32[32]{0:T(128)S(1)}, f32[32]{0:T(128)}, u32[]{:S(2)}) copy-start(f32[32]{0:T(128)} %w_bias.5) | copy-start | bytes 388
  20.4 35.7 %copy-start.7 = (f32[32]{0:T(128)S(1)}, f32[32]{0:T(128)}, u32[]{:S(2)}) copy-start(f32[32]{0:T(128)} %w_out.5) | copy-start | bytes 388
  30.3 13.1 %collective-permute-start.3 = (f32[520,128]{1,0:T(8,128)S(1)}, f32[520,128]{1,0:T(8,128)S(1)}, u32[]{:S(2)}, u32[]{:S(2)}) collective-permute-start(f32[520,128]{1,0:T(8,128)S(1)} %get-tuple-element.31.partial), channel_id=1, source_target_pairs={{4,0},{8,4},{12,8},{16,12},{20,16},{24,20},{28,24},{32,28},{36,32}... | collective-permute-start | bytes 798728 | tf_op jit(solution)/shard_map/ppermute | solution.py:349
  32.2 12.0 %collective-permute-start.2 = (f32[520,128]{1,0:T(8,128)S(1)}, f32[520,128]{1,0:T(8,128)S(1)}, u32[]{:S(2)}, u32[]{:S(2)}) collective-permute-start(f32[520,128]{1,0:T(8,128)S(1)} %get-tuple-element.31.partial), channel_id=1, source_target_pairs={{0,4},{4,8},{8,12},{12,16},{16,20},{20,24},{24,28},{28,32},{32,36}... | collective-permute-start | bytes 798728 | tf_op jit(solution)/shard_map/ppermute | solution.py:349
  45.5 4.3 %collective-permute-start.4 = (f32[256,128]{1,0:T(8,128)S(1)}, f32[256,128]{1,0:T(8,128)S(1)}, u32[]{:S(2)}, u32[]{:S(2)}) collective-permute-start(f32[256,128]{1,0:T(8,128)S(1)} %get-tuple-element.33), channel_id=1, source_target_pairs={{0,1},{1,0},{2,3},{3,2},{4,5},{5,4},{6,7},{7,6},{8,9},{9,8},{10,11... | collective-permute-start | bytes 393224 | tf_op jit(solution)/shard_map/ppermute | solution.py:352
  48.1 5.1 %collective-permute-start.5 = (f32[256,128]{1,0:T(8,128)S(1)}, f32[256,128]{1,0:T(8,128)S(1)}, u32[]{:S(2)}, u32[]{:S(2)}) collective-permute-start(f32[256,128]{1,0:T(8,128)S(1)} %get-tuple-element.34), channel_id=1, source_target_pairs={{0,2},{1,3},{2,0},{3,1},{4,6},{5,7},{6,4},{7,5},{8,10},{9,11},{10,... | collective-permute-start | bytes 393224 | tf_op jit(solution)/shard_map/ppermute | solution.py:352
  48.6 7.5 %collective-permute-start.6 = (f32[256,128]{1,0:T(8,128)S(1)}, f32[256,128]{1,0:T(8,128)S(1)}, u32[]{:S(2)}, u32[]{:S(2)}) collective-permute-start(f32[256,128]{1,0:T(8,128)S(1)} %get-tuple-element.35), channel_id=1, source_target_pairs={{0,3},{1,2},{2,1},{3,0},{4,7},{5,6},{6,5},{7,4},{8,11},{9,10},{10,... | collective-permute-start | bytes 393224 | tf_op jit(solution)/shard_map/ppermute | solution.py:352
  61.6 12.8 %collective-permute-start.8 = (bf16[256,128]{1,0:T(8,128)(2,1)S(1)}, bf16[256,128]{1,0:T(8,128)(2,1)S(1)}, u32[]{:S(2)}, u32[]{:S(2)}) collective-permute-start(bf16[256,128]{1,0:T(8,128)(2,1)S(1)} %get-tuple-element.36.own), channel_id=1, source_target_pairs={{4,0},{8,4},{12,8},{16,12},{20,16},{24,20},{28,24},{32,28},{36,32}... | collective-permute-start | bytes 196616 | tf_op jit(solution)/shard_map/ppermute | solution.py:349
  63.5 10.9 %collective-permute-start.7 = (bf16[256,128]{1,0:T(8,128)(2,1)S(1)}, bf16[256,128]{1,0:T(8,128)(2,1)S(1)}, u32[]{:S(2)}, u32[]{:S(2)}) collective-permute-start(bf16[256,128]{1,0:T(8,128)(2,1)S(1)} %get-tuple-element.36.own), channel_id=1, source_target_pairs={{0,4},{4,8},{8,12},{12,16},{16,20},{20,24},{24,28},{28,32},{32,36}... | collective-permute-start | bytes 196616 | tf_op jit(solution)/shard_map/ppermute | solution.py:349
  72.2 4.5 %collective-permute-start.14 = (bf16[256,128]{1,0:T(8,128)(2,1)S(1)}, bf16[256,128]{1,0:T(8,128)(2,1)S(1)}, u32[]{:S(2)}, u32[]{:S(2)}) collective-permute-start(bf16[256,128]{1,0:T(8,128)(2,1)S(1)} %get-tuple-element.36.own), channel_id=1, source_target_pairs={{0,3},{1,2},{2,1},{3,0},{4,7},{5,6},{6,5},{7,4},{8,11},{9,10},{10,... | collective-permute-start | bytes 196616 | tf_op jit(solution)/shard_map/ppermute | solution.py:352
  73.2 9.7 %collective-permute-start.12 = (bf16[256,128]{1,0:T(8,128)(2,1)S(1)}, bf16[256,128]{1,0:T(8,128)(2,1)S(1)}, u32[]{:S(2)}, u32[]{:S(2)}) collective-permute-start(bf16[256,128]{1,0:T(8,128)(2,1)S(1)} %get-tuple-element.36.own), channel_id=1, source_target_pairs={{0,2},{1,3},{2,0},{3,1},{4,6},{5,7},{6,4},{7,5},{8,10},{9,11},{10,... | collective-permute-start | bytes 196616 | tf_op jit(solution)/shard_map/ppermute | solution.py:352
  74.1 8.8 %collective-permute-start.10 = (bf16[256,128]{1,0:T(8,128)(2,1)S(1)}, bf16[256,128]{1,0:T(8,128)(2,1)S(1)}, u32[]{:S(2)}, u32[]{:S(2)}) collective-permute-start(bf16[256,128]{1,0:T(8,128)(2,1)S(1)} %get-tuple-element.36.own), channel_id=1, source_target_pairs={{0,1},{1,0},{2,3},{3,2},{4,5},{5,4},{6,7},{7,6},{8,9},{9,8},{10,11... | collective-permute-start | bytes 196616 | tf_op jit(solution)/shard_map/ppermute | solution.py:352
  74.4 8.5 %collective-permute-start.13 = (bf16[2,256,128]{2,1,0:T(8,128)(2,1)S(1)}, bf16[2,256,128]{2,1,0:T(8,128)(2,1)S(1)}, u32[]{:S(2)}, u32[]{:S(2)}) collective-permute-start(bf16[2,256,128]{2,1,0:T(8,128)(2,1)S(1)} %pad_maximum_fusion._), channel_id=1, source_target_pairs={{0,3},{1,2},{2,1},{3,0},{4,7},{5,6},{6,5},{7,4},{8,11},{9,10},{10,... | collective-permute-start | bytes 393224 | tf_op jit(solution)/shard_map/ppermute | solution.py:352
  75.1 8.4 %collective-permute-start.11 = (bf16[2,256,128]{2,1,0:T(8,128)(2,1)S(1)}, bf16[2,256,128]{2,1,0:T(8,128)(2,1)S(1)}, u32[]{:S(2)}, u32[]{:S(2)}) collective-permute-start(bf16[2,256,128]{2,1,0:T(8,128)(2,1)S(1)} %pad_maximum_fusion._), channel_id=1, source_target_pairs={{0,2},{1,3},{2,0},{3,1},{4,6},{5,7},{6,4},{7,5},{8,10},{9,11},{10,... | collective-permute-start | bytes 393224 | tf_op jit(solution)/shard_map/ppermute | solution.py:352
  76.6 6.9 %collective-permute-start.9 = (bf16[2,256,128]{2,1,0:T(8,128)(2,1)S(1)}, bf16[2,256,128]{2,1,0:T(8,128)(2,1)S(1)}, u32[]{:S(2)}, u32[]{:S(2)}) collective-permute-start(bf16[2,256,128]{2,1,0:T(8,128)(2,1)S(1)} %pad_maximum_fusion._), channel_id=1, source_target_pairs={{0,1},{1,0},{2,3},{3,2},{4,5},{5,4},{6,7},{7,6},{8,9},{9,8},{10,11... | collective-permute-start | bytes 393224 | tf_op jit(solution)/shard_map/ppermute | solution.py:352
  93.9 25.7 %collective-permute-start.16 = (f32[520,128]{1,0:T(8,128)S(1)}, f32[520,128]{1,0:T(8,128)S(1)}, u32[]{:S(2)}, u32[]{:S(2)}) collective-permute-start(f32[520,128]{1,0:T(8,128)S(1)} %get-tuple-element.38.partial), channel_id=1, source_target_pairs={{4,0},{8,4},{12,8},{16,12},{20,16},{24,20},{28,24},{32,28},{36,32}... | collective-permute-start | bytes 798728 | tf_op jit(solution)/shard_map/ppermute | solution.py:349
  95.8 23.8 %collective-permute-start.15 = (f32[520,128]{1,0:T(8,128)S(1)}, f32[520,128]{1,0:T(8,128)S(1)}, u32[]{:S(2)}, u32[]{:S(2)}) collective-permute-start(f32[520,128]{1,0:T(8,128)S(1)} %get-tuple-element.38.partial), channel_id=1, source_target_pairs={{0,4},{4,8},{8,12},{12,16},{16,20},{20,24},{24,28},{28,32},{32,36}... | collective-permute-start | bytes 798728 | tf_op jit(solution)/shard_map/ppermute | solution.py:349
  107.9 17.3 %all-to-all-start = ((f32[128,1,288]{2,1,0:T(1,128)}), f32[128,1,288]{2,1,0:T(1,128)S(1)}, u32[]{:S(2)}, u32[]{:S(2)}) async-start(f32[128,1,288]{2,1,0:T(1,128)} %broadcast_in_dim.13), calls=%async_computation | async-start | bytes 393216 | tf_op jit(solution)/shard_map/all_to_all | solution.py:475
  120.9 4.3 %collective-permute-start.17 = (f32[256,128]{1,0:T(8,128)S(1)}, f32[256,128]{1,0:T(8,128)S(1)}, u32[]{:S(2)}, u32[]{:S(2)}) collective-permute-start(f32[256,128]{1,0:T(8,128)S(1)} %get-tuple-element.40), channel_id=1, source_target_pairs={{0,1},{1,0},{2,3},{3,2},{4,5},{5,4},{6,7},{7,6},{8,9},{9,8},{10,11... | collective-permute-start | bytes 393224 | tf_op jit(solution)/shard_map/ppermute | solution.py:352
  121.4 4.9 %collective-permute-start.18 = (f32[256,128]{1,0:T(8,128)S(1)}, f32[256,128]{1,0:T(8,128)S(1)}, u32[]{:S(2)}, u32[]{:S(2)}) collective-permute-start(f32[256,128]{1,0:T(8,128)S(1)} %get-tuple-element.41), channel_id=1, source_target_pairs={{0,2},{1,3},{2,0},{3,1},{4,6},{5,7},{6,4},{7,5},{8,10},{9,11},{10,... | collective-permute-start | bytes 393224 | tf_op jit(solution)/shard_map/ppermute | solution.py:352
  121.9 7.5 %collective-permute-start.19 = (f32[256,128]{1,0:T(8,128)S(1)}, f32[256,128]{1,0:T(8,128)S(1)}, u32[]{:S(2)}, u32[]{:S(2)}) collective-permute-start(f32[256,128]{1,0:T(8,128)S(1)} %get-tuple-element.42), channel_id=1, source_target_pairs={{0,3},{1,2},{2,1},{3,0},{4,7},{5,6},{6,5},{7,4},{8,11},{9,10},{10,... | collective-permute-start | bytes 393224 | tf_op jit(solution)/shard_map/ppermute | solution.py:352

commit v3 on v2

--- a/solution.py
+++ b/solution.py
@@ -33,14 +33,18 @@
     return jnp.dot(a, b, preferred_element_type=F32)
 
 
-def hold_kernel(blocks, _, held, sems):
+def start_copies(blocks, held, sems):
     per = held.shape[0] // CHUNKS
     copies = []
     for i in range(CHUNKS):
         rows = pl.ds(i * per, per)
         copies.append(pltpu.make_async_copy(blocks.at[rows, :], held.at[rows, :], sems.at[i]))
         copies[i].start()
-    for copy in copies:
+    return copies
+
+
+def hold_kernel(blocks, _, held, sems):
+    for copy in start_copies(blocks, held, sems):
         copy.wait()
 
 
@@ -54,10 +58,13 @@
     lax.fori_loop(0, picked.shape[0] // 16, body, 0)
 
 
-def project(held, picked, products):
+def project(held, picked, products, copies=()):
     count, size = picked.shape
     row = lax.broadcasted_iota(jnp.int32, (GROUP, size), 0)
-    for g in range(count // GROUP):
+    groups = count // GROUP
+    for g in range(groups):
+        if copies and g % (groups // CHUNKS) == 0:
+            copies[g // (groups // CHUNKS)].wait()
         x = picked[g * GROUP : (g + 1) * GROUP, :].astype(BF16)
         full = lax.dot_general(
             x,
@@ -138,8 +145,9 @@
 def backward_kernel(
     me, count, vox, tile, ray, low, high, own, near1, own1, near2, own2, near3, own3,
     blocks, dual, counts, sinogram, w_in, w_bias, w_out,
-    grad_dual, partial, dual_grad, ext, picked, products,
+    grad_dual, partial, dual_grad, ext, picked, products, held, sems,
 ):
+    copies = start_copies(blocks, held, sems)
     rows = own.shape[0]
     pieces = [
         (low, own, high),
@@ -152,7 +160,7 @@
             at = pl.multiple_of((i * len(pieces) + (me[0] ^ d)) * rows, rows)
             ext[pl.ds(at, rows), :] = field[...].astype(F32)
     gather_tiles(vox, ext, picked)
-    project(blocks, picked, products)
+    project(held, picked, products, copies)
     tiles, size = dual.shape
     chosen = ray_choice(ray, count, tiles)
     dual_grad[...] = add_rays(chosen, products)
@@ -180,7 +188,7 @@
         grads.append(g * (p1 - e * p2))
     sino_grad = jnp.concatenate(grads, axis=0).astype(BF16)
     picked[...] = dot(chosen.T.astype(BF16), sino_grad)
-    spread(blocks, picked, partial)
+    spread(held, picked, partial)
     mark_tiles(tile, partial)
 
 
@@ -281,20 +289,20 @@
 
         def channel(c, carry):
             p0, p1 = carry
-            w0, w1 = w_in[c, 0], w_in[c, 1]
-            h = w0 * v + w1 * b + w_bias[c]
-            gate = sigmoid(h)
-            act = h * gate
-            err = (w_out[c] * t) * (gate + act * (1.0 - gate))
+            w0, w1, wo = w_in[c, 0], w_in[c, 1], 0.5 * w_out[c]
+            half = (0.5 * w0) * v + ((0.5 * w1) * b + 0.5 * w_bias[c])
+            more = jnp.tanh(half) + 1.0
+            act = half * more
+            err = t * (more * ((half - act) + (half + 1.0)))
 
             def fold(x):
                 return jnp.sum(x.reshape(part // 8, 8, size), axis=0)
 
-            totals[c, 0] += fold(err * v)
-            totals[c, 1] += fold(err * b)
-            totals[c, 2] += fold(err)
+            totals[c, 0] += wo * fold(err * v)
+            totals[c, 1] += wo * fold(err * b)
+            totals[c, 2] += wo * fold(err)
             totals[c, 3] += fold(act * t)
-            return p0 + w0 * err, p1 + w1 * err
+            return p0 + (w0 * wo) * err, p1 + (w1 * wo) * err
 
         zero = jnp.zeros_like(t)
         p0, p1 = lax.fori_loop(0, w_bias.shape[0], channel, (zero, zero), unroll=2)
@@ -361,12 +369,14 @@
 
     matrix = blocks.reshape(listed * tr, tv)
 
+    in_hbm = pltpu.with_memory_space_constraint(matrix, pltpu.HBM)
+
     def in_vmem(after):
         held = call(
             hold_kernel,
             [pltpu.VMEM(matrix.shape, BF16)],
             [HBM, HBM],
-            (pltpu.with_memory_space_constraint(matrix, pltpu.HBM), after),
+            (in_hbm, after),
             [pltpu.SemaphoreType.DMA((CHUNKS,))],
             bytes_moved=4 * matrix.size,
             limit=12,
@@ -440,12 +450,12 @@
     grad_dual, partial, dual_grad = call(
         backward_kernel,
         [shape(ray_tiles, tr), shape(listed + 8, tv), shape(ray_tiles, tr)],
-        [SMEM] * 3 + [VMEM] * 15 + [SMEM] * 3,
-        (me, count, vox, vox_row, ray, *fields, in_vmem(near), dual_tiles, count_tiles, sinogram,
+        [SMEM] * 3 + [VMEM] * 11 + [HBM] + [VMEM] * 3 + [SMEM] * 3,
+        (me, count, vox, vox_row, ray, *fields, in_hbm, dual_tiles, count_tiles, sinogram,
          dual_in, dual_bias, dual_out),
-        big,
+        big + [pltpu.VMEM(matrix.shape, BF16), pltpu.SemaphoreType.DMA((CHUNKS,))],
         bytes_moved=3 * matrix.size,
-        limit=12,
+        limit=28,
     )
     dual_sums = call(
         weight_kernel,

time: 133 us -> 129 us (0.970)
  waiting for transfers between devices: 16.9 us -> 34.8 us
  starting transfers between devices: 61.8 us -> 44.1 us
  Pallas kernels: 45.5 us -> 41.8 us
    ppermute x8, starting transfers between devices: 39.9 us -> 21.9 us  [beside(): return (lax.ppermute(x, 'gz', up), lax.ppermute(x, 'gz', down))]
    ppermute x8, waiting for transfers between devices: 3.44 us -> 17.1 us  [beside(): return (lax.ppermute(x, 'gz', up), lax.ppermute(x, 'gz', down))]
    ppermute x12, waiting for transfers between devices: 11.4 us -> 15.7 us  [peer(): return lax.ppermute(x, 'vert', [(i, i ^ d) for i in range(groups)])]
    pallas_call x11 -> x10, Pallas kernels: 45.5 us -> 41.8 us  [call(): pl.pallas_call(body, out_shape=out_shapes, in_specs=specs, out_specs=[VME...]
  transfers between devices with their start and end apart: 21 -> 21, of which waited for: 9 -> 11; matrix products, arithmetic and copies ran while one was open for 1% -> 1% of each run, Pallas kernels for 14% -> 9%
where the time goes in v3:
time: 129 us; the launch traced here: 127 us
  starting transfers between devices  44.1 us (34%)
  Pallas kernels  41.8 us (32%)
  waiting for transfers between devices  34.8 us (27%)
  other arithmetic  2.56 us (2%)
  local copies, waits for them, and re-layouts  1.78 us (1%)
  between operations  1.59 us (1%)
    pallas_call x10, Pallas kernels, call(): pl.pallas_call(body, out_shape=out_shapes, in_specs=specs, out_specs=[VME...  41.8 us
    ppermute x8, starting transfers between devices, beside(): return (lax.ppermute(x, 'gz', up), lax.ppermute(x, 'gz', down))  21.9 us
    ppermute x8, waiting for transfers between devices, beside(): return (lax.ppermute(x, 'gz', up), lax.ppermute(x, 'gz', down))  17.1 us
    ppermute x12, waiting for transfers between devices, peer(): return lax.ppermute(x, 'vert', [(i, i ^ d) for i in range(groups)])  15.7 us
    ppermute x12, starting transfers between devices, peer(): return lax.ppermute(x, 'vert', [(i, i ^ d) for i in range(groups)])  11.9 us
    all_to_all x1, starting transfers between devices, local(): lax.all_to_all(sent, ('gz', 'vert'), 0, 0)  10.3 us
  transfers between devices with their start and end apart: 21, of which 11 were waited for; matrix products, arithmetic and copies ran while one was open for 1% of the time, Pallas kernels for 9%

profile of v3, /device:TPU:103, one launch (start us, length us, event | category | flops | bytes accessed | tf_op | source)
XLA Modules:
  0.0 126.7 jit_solution(9263864266910326745)
XLA Ops:
  0.6 2.5 %reduce = bf16[131072]{0:T(1024)(128)(2,1)S(1)} reduce(bf16[1,131072]{1,0:T(2,128)(2,1)} %param.14, bf16[]{:T(256)} %constant.69), dimensions={0}, to_apply=%param.14.reduce_sub_computation | reduce | bytes 524290 | tf_op args[0]
  3.1 2.7 %collective-permute-start = (bf16[1024,128]{1,0:T(8,128)(2,1)S(1)}, bf16[1024,128]{1,0:T(8,128)(2,1)S(1)}, u32[]{:S(2)}, u32[]{:S(2)}) collective-permute-start(bf16[1024,128]{1,0:T(8,128)(2,1)S(1)} %bitcast.56), channel_id=1, source_target_pairs={{0,4},{4,8},{8,12},{12,16},{16,20},{20,24},{24,28},{28,32},{32,36}... | collective-permute-start | bytes 786440 | tf_op jit(solution)/shard_map/ppermute | solution.py:357
  5.8 2.6 %collective-permute-start.1 = (bf16[1024,128]{1,0:T(8,128)(2,1)S(1)}, bf16[1024,128]{1,0:T(8,128)(2,1)S(1)}, u32[]{:S(2)}, u32[]{:S(2)}) collective-permute-start(bf16[1024,128]{1,0:T(8,128)(2,1)S(1)} %bitcast.57), channel_id=1, source_target_pairs={{4,0},{8,4},{12,8},{16,12},{20,16},{24,20},{28,24},{32,28},{36,32}... | collective-permute-start | bytes 786440 | tf_op jit(solution)/shard_map/ppermute | solution.py:357
  9.1 0.8 copy.38.w_in
  9.8 0.0 copy-start.1
  9.9 0.0 copy-start.4
  9.9 0.0 copy-start.5
  9.9 6.0 %shard_map.197.blocks = bf16[65536,128]{1,0:T(8,128)(2,1)S(1)} custom-call(bf16[65536,128]{1,0:T(8,128)(2,1)} %bitcast.72, s32[1,1]{1,0:T(1,128)} %copy.48._), custom_call_target="tpu_custom_call" | custom-call | bytes 33554432 | tf_op jit(solution)/shard_map/pallas_call | solution.py:320
  15.9 0.0 copy-start.9
  15.9 0.0 copy-start.2
  15.9 0.0 copy-start.6
  15.9 0.0 copy-start.7
  16.0 0.0 collective-permute-done.low
  16.0 3.1 %collective-permute-done.1.high = bf16[1024,128]{1,0:T(8,128)(2,1)S(1)} collective-permute-done((bf16[1024,128]{1,0:T(8,128)(2,1)S(1)}, bf16[1024,128]{1,0:T(8,128)(2,1)S(1)}, u32[]{:S(2)}, u32[]{:S(2)}) %collective-permute-start.1) | collective-permute-done | bytes 262176 | tf_op jit(solution)/shard_map/ppermute | solution.py:357
  19.1 9.7 %shard_map.198 = (f32[128,128]{1,0:T(8,128)S(1)}, f32[520,128]{1,0:T(8,128)S(1)}) custom-call(s32[1]{0:T(128)} %bitcast.53.count, s32[512]{0:T(512)S(1)} %bitcast.70, s32[1,512]{1,0:T(1,128)S(1)} %get-tuple-element.54.tile, s32[1,512]{1,0:T(1,128)S(1)} %get-tuple-element.55.ray, bf16[1024,128]{1,0:T(8,128)(2,1)S(1)} %collective-permute-done.low, ...), custom_call_target="tpu_custom_call" | custom-call | bytes 25165824 | tf_op jit(solution)/shard_map/pallas_call | solution.py:320
  28.8 4.2 %collective-permute-start.2 = (f32[520,128]{1,0:T(8,128)S(1)}, f32[520,128]{1,0:T(8,128)S(1)}, u32[]{:S(2)}, u32[]{:S(2)}) collective-permute-start(f32[520,128]{1,0:T(8,128)S(1)} %get-tuple-element.31.partial), channel_id=1, source_target_pairs={{0,4},{4,8},{8,12},{12,16},{16,20},{20,24},{24,28},{28,32},{32,36}... | collective-permute-start | bytes 798728 | tf_op jit(solution)/shard_map/ppermute | solution.py:357
  33.0 1.9 %collective-permute-start.3 = (f32[520,128]{1,0:T(8,128)S(1)}, f32[520,128]{1,0:T(8,128)S(1)}, u32[]{:S(2)}, u32[]{:S(2)}) collective-permute-start(f32[520,128]{1,0:T(8,128)S(1)} %get-tuple-element.31.partial), channel_id=1, source_target_pairs={{4,0},{8,4},{12,8},{16,12},{20,16},{24,20},{28,24},{32,28},{36,32}... | collective-permute-start | bytes 798728 | tf_op jit(solution)/shard_map/ppermute | solution.py:357
  34.9 0.7 shard_map.199.held
  35.6 1.8 %collective-permute-done.2.from_low = f32[520,128]{1,0:T(8,128)S(1)} collective-permute-done((f32[520,128]{1,0:T(8,128)S(1)}, f32[520,128]{1,0:T(8,128)S(1)}, u32[]{:S(2)}, u32[]{:S(2)}) %collective-permute-start.2) | collective-permute-done | bytes 266272 | tf_op jit(solution)/shard_map/ppermute | solution.py:357
  37.4 8.3 %collective-permute-done.3.from_high = f32[520,128]{1,0:T(8,128)S(1)} collective-permute-done((f32[520,128]{1,0:T(8,128)S(1)}, f32[520,128]{1,0:T(8,128)S(1)}, u32[]{:S(2)}, u32[]{:S(2)}) %collective-permute-start.3) | collective-permute-done | bytes 266272 | tf_op jit(solution)/shard_map/ppermute | solution.py:357
  45.8 1.3 %shard_map.200 = (f32[256,128]{1,0:T(8,128)S(1)}, f32[256,128]{1,0:T(8,128)S(1)}, f32[256,128]{1,0:T(8,128)S(1)}, f32[256,128]{1,0:T(8,128)S(1)}) custom-call(s32[1]{0:T(128)} %bitcast.me, f32[4,256,128]{2,1,0:T(8,128)S(1)} %shard_map.199.held, f32[520,128]{1,0:T(8,128)S(1)} %collective-permute-done.2.from_low, f32[520,128]{1,0:T(8,128)S(1)} %collective-permute-done.3.from_high), custom_call_target="tpu_custom_call" | custom-call | bytes 8388608 | tf_op jit(solution)/shard_map/pallas_call | solution.py:320
  47.1 2.5 %collective-permute-start.4 = (f32[256,128]{1,0:T(8,128)S(1)}, f32[256,128]{1,0:T(8,128)S(1)}, u32[]{:S(2)}, u32[]{:S(2)}) collective-permute-start(f32[256,128]{1,0:T(8,128)S(1)} %get-tuple-element.33), channel_id=1, source_target_pairs={{0,1},{1,0},{2,3},{3,2},{4,5},{5,4},{6,7},{7,6},{8,9},{9,8},{10,11... | collective-permute-start | bytes 393224 | tf_op jit(solution)/shard_map/ppermute | solution.py:360
  49.6 0.0 collective-permute-start.5
  49.6 1.7 %collective-permute-start.6 = (f32[256,128]{1,0:T(8,128)S(1)}, f32[256,128]{1,0:T(8,128)S(1)}, u32[]{:S(2)}, u32[]{:S(2)}) collective-permute-start(f32[256,128]{1,0:T(8,128)S(1)} %get-tuple-element.35), channel_id=1, source_target_pairs={{0,3},{1,2},{2,1},{3,0},{4,7},{5,6},{6,5},{7,4},{8,11},{9,10},{10,... | collective-permute-start | bytes 393224 | tf_op jit(solution)/shard_map/ppermute | solution.py:360
  51.3 0.1 copy.39.w_in
  51.4 0.0 collective-permute-done.4.peer1
  51.4 3.2 %collective-permute-done.5.peer2 = f32[256,128]{1,0:T(8,128)S(1)} collective-permute-done((f32[256,128]{1,0:T(8,128)S(1)}, f32[256,128]{1,0:T(8,128)S(1)}, u32[]{:S(2)}, u32[]{:S(2)}) %collective-permute-start.5) | collective-permute-done | bytes 131104 | tf_op jit(solution)/shard_map/ppermute | solution.py:360
  54.6 3.0 %collective-permute-done.6.peer3 = f32[256,128]{1,0:T(8,128)S(1)} collective-permute-done((f32[256,128]{1,0:T(8,128)S(1)}, f32[256,128]{1,0:T(8,128)S(1)}, u32[]{:S(2)}, u32[]{:S(2)}) %collective-permute-start.6) | collective-permute-done | bytes 131104 | tf_op jit(solution)/shard_map/ppermute | solution.py:360
  57.6 5.3 %shard_map.201 = (bf16[256,128]{1,0:T(8,128)(2,1)S(1)}, f32[256,128]{1,0:T(8,128)S(1)}, f32[4,32]{1,0:T(4,128)S(1)}) custom-call(s32[1]{0:T(128)} %bitcast.me, f32[256,128]{1,0:T(8,128)S(1)} %get-tuple-element.32.own, f32[256,128]{1,0:T(8,128)S(1)} %collective-permute-done.4.peer1, f32[256,128]{1,0:T(8,128)S(1)} %collective-permute-done.5.peer2, ...), custom_call_target="tpu_custom_call" | custom-call | bytes 16777216 | tf_op jit(solution)/shard_map/pallas_call | solution.py:320
  62.9 1.9 %collective-permute-start.7 = (bf16[256,128]{1,0:T(8,128)(2,1)S(1)}, bf16[256,128]{1,0:T(8,128)(2,1)S(1)}, u32[]{:S(2)}, u32[]{:S(2)}) collective-permute-start(bf16[256,128]{1,0:T(8,128)(2,1)S(1)} %get-tuple-element.36.own), channel_id=1, source_target_pairs={{0,4},{4,8},{8,12},{12,16},{16,20},{20,24},{24,28},{28,32},{32,36}... | collective-permute-start | bytes 196616 | tf_op jit(solution)/shard_map/ppermute | solution.py:357
  64.8 3.4 %collective-permute-start.8 = (bf16[256,128]{1,0:T(8,128)(2,1)S(1)}, bf16[256,128]{1,0:T(8,128)(2,1)S(1)}, u32[]{:S(2)}, u32[]{:S(2)}) collective-permute-start(bf16[256,128]{1,0:T(8,128)(2,1)S(1)} %get-tuple-element.36.own), channel_id=1, source_target_pairs={{4,0},{8,4},{12,8},{16,12},{20,16},{24,20},{28,24},{32,28},{36,32}... | collective-permute-start | bytes 196616 | tf_op jit(solution)/shard_map/ppermute | solution.py:357
  68.2 0.9 collective-permute-start.10
  69.0 0.1 collective-permute-start.12
  69.2 1.6 %collective-permute-start.14 = (bf16[256,128]{1,0:T(8,128)(2,1)S(1)}, bf16[256,128]{1,0:T(8,128)(2,1)S(1)}, u32[]{:S(2)}, u32[]{:S(2)}) collective-permute-start(bf16[256,128]{1,0:T(8,128)(2,1)S(1)} %get-tuple-element.36.own), channel_id=1, source_target_pairs={{0,3},{1,2},{2,1},{3,0},{4,7},{5,6},{6,5},{7,4},{8,11},{9,10},{10,... | collective-permute-start | bytes 196616 | tf_op jit(solution)/shard_map/ppermute | solution.py:360
  70.8 0.0 collective-permute-done.7.low
  70.8 3.9 %collective-permute-done.8.high = bf16[256,128]{1,0:T(8,128)(2,1)S(1)} collective-permute-done((bf16[256,128]{1,0:T(8,128)(2,1)S(1)}, bf16[256,128]{1,0:T(8,128)(2,1)S(1)}, u32[]{:S(2)}, u32[]{:S(2)}) %collective-permute-start.8) | collective-permute-done | bytes 65568 | tf_op jit(solution)/shard_map/ppermute | solution.py:357
  74.7 0.1 collective-permute-start.11
  74.8 2.7 %collective-permute-start.13 = (bf16[2,256,128]{2,1,0:T(8,128)(2,1)S(1)}, bf16[2,256,128]{2,1,0:T(8,128)(2,1)S(1)}, u32[]{:S(2)}, u32[]{:S(2)}) collective-permute-start(bf16[2,256,128]{2,1,0:T(8,128)(2,1)S(1)} %pad_maximum_fusion), channel_id=1, source_target_pairs={{0,3},{1,2},{2,1},{3,0},{4,7},{5,6},{6,5},{7,4},{8,11},{9,10},{10,... | collective-permute-start | bytes 393224 | tf_op jit(solution)/shard_map/ppermute | solution.py:360
  77.6 0.0 collective-permute-done.10.own1
  77.6 0.0 collective-permute-start.9
  77.6 0.0 collective-permute-done.12.own2
  77.6 0.0 collective-permute-done.14.own3
  77.6 1.0 collective-permute-done.11.near2
  78.6 4.2 %collective-permute-done.13.near3 = bf16[2,256,128]{2,1,0:T(8,128)(2,1)S(1)} collective-permute-done((bf16[2,256,128]{2,1,0:T(8,128)(2,1)S(1)}, bf16[2,256,128]{2,1,0:T(8,128)(2,1)S(1)}, u32[]{:S(2)}, u32[]{:S(2)}) %collective-permute-start.13) | collective-permute-done | bytes 131104 | tf_op jit(solution)/shard_map/ppermute | solution.py:360
  82.9 0.0 collective-permute-done.9.near1
  82.9 12.8 %shard_map.202 = (f32[128,128]{1,0:T(8,128)}, f32[520,128]{1,0:T(8,128)S(1)}, f32[128,128]{1,0:T(8,128)S(1)}) custom-call(s32[1]{0:T(128)} %bitcast.me, s32[1]{0:T(128)} %bitcast.54.count, s32[512]{0:T(512)S(1)} %bitcast.71, s32[1,512]{1,0:T(1,128)S(1)} %get-tuple-element.54.tile, s32[1,512]{1,0:T(1,128)S(1)} %get-tuple-element.55.ray, ...), custom_call_target="tpu_custom_call" | custom-call | bytes 25165824 | tf_op jit(solution)/shard_map/pallas_call | solution.py:320
  95.7 3.2 %collective-permute-start.15 = (f32[520,128]{1,0:T(8,128)S(1)}, f32[520,128]{1,0:T(8,128)S(1)}, u32[]{:S(2)}, u32[]{:S(2)}) collective-permute-start(f32[520,128]{1,0:T(8,128)S(1)} %get-tuple-element.38.partial), channel_id=1, source_target_pairs={{0,4},{4,8},{8,12},{12,16},{16,20},{20,24},{24,28},{28,32},{32,36}... | collective-permute-start | bytes 798728 | tf_op jit(solution)/shard_map/ppermute | solution.py:357
  98.9 2.0 %collective-permute-start.16 = (f32[520,128]{1,0:T(8,128)S(1)}, f32[520,128]{1,0:T(8,128)S(1)}, u32[]{:S(2)}, u32[]{:S(2)}) collective-permute-start(f32[520,128]{1,0:T(8,128)S(1)} %get-tuple-element.38.partial), channel_id=1, source_target_pairs={{4,0},{8,4},{12,8},{16,12},{20,16},{24,20},{28,24},{32,28},{36,32}... | collective-permute-start | bytes 798728 | tf_op jit(solution)/shard_map/ppermute | solution.py:357
  101.0 3.3 %shard_map.205 = f32[5,32]{1,0:T(8,128)S(1)} custom-call(f32[128,128]{1,0:T(8,128)S(1)} %bitcast.63, f32[128,128]{1,0:T(8,128)S(1)} %bitcast.66, f32[128,128]{1,0:T(8,128)S(1)} %get-tuple-element.37.sinogram, f32[128,128]{1,0:T(8,128)S(1)} %get-tuple-element.44.dual_grad, f32[32,3]{1,0:T(8,128)S(1)} %copy.38.w_in, f32[32]{0:T(128)S(1)} %copy-done.4, ...), custom_call_target="tpu_custom_call" | custom-call | bytes 12582912 | tf_op jit(solution)/shard_map/pallas_call | solution.py:320
  104.3 0.1 broadcast_in_dim.12
  104.4 0.8 broadcast_in_dim.13
  105.2 10.3 %all-to-all-start = ((f32[128,1,288]{2,1,0:T(1,128)}), f32[128,1,288]{2,1,0:T(1,128)S(1)}, u32[]{:S(2)}, u32[]{:S(2)}) async-start(f32[128,1,288]{2,1,0:T(1,128)} %broadcast_in_dim.13), calls=%async_computation | async-start | bytes 393216 | tf_op jit(solution)/shard_map/all_to_all | solution.py:485
  115.5 0.7 shard_map.203.held
  116.2 0.0 collective-permute-done.15.from_low
  116.3 0.0 collective-permute-done.16.from_high
  116.3 1.3 %shard_map.204 = (f32[256,128]{1,0:T(8,128)S(1)}, f32[256,128]{1,0:T(8,128)S(1)}, f32[256,128]{1,0:T(8,128)S(1)}, f32[256,128]{1,0:T(8,128)S(1)}) custom-call(s32[1]{0:T(128)} %bitcast.me, f32[4,256,128]{2,1,0:T(8,128)S(1)} %shard_map.203.held, f32[520,128]{1,0:T(8,128)S(1)} %collective-permute-done.15.from_low, f32[520,128]{1,0:T(8,128)S(1)} %collective-permute-done.16.from_high), custom_call_target="tpu_custom_call" | custom-call | bytes 8388608 | tf_op jit(solution)/shard_map/pallas_call | solution.py:320
  117.6 0.4 collective-permute-start.17
  118.0 0.6 collective-permute-start.18
  118.6 1.2 collective-permute-start.19
  119.8 2.0 %all-to-all-done = f32[128,1,288]{2,1,0:T(1,128)S(1)} async-done(((f32[128,1,288]{2,1,0:T(1,128)}), f32[128,1,288]{2,1,0:T(1,128)S(1)}, u32[]{:S(2)}, u32[]{:S(2)}) %all-to-all-start) | async-done | bytes 147488 | tf_op jit(solution)/shard_map/all_to_all | solution.py:485
  121.8 0.0 collective-permute-done.17.peer1
  121.9 1.1 collective-permute-done.18.peer2
  122.9 3.1 %collective-permute-done.19.peer3 = f32[256,128]{1,0:T(8,128)S(1)} collective-permute-done((f32[256,128]{1,0:T(8,128)S(1)}, f32[256,128]{1,0:T(8,128)S(1)}, u32[]{:S(2)}, u32[]{:S(2)}) %collective-permute-start.19) | collective-permute-done | bytes 131104 | tf_op jit(solution)/shard_map/ppermute | solution.py:360
  126.0 0.7 shard_map.206
  (19 shorter events, 0.1 us)
Async XLA Ops:
  3.1 12.9 %collective-permute-start = (bf16[1024,128]{1,0:T(8,128)(2,1)S(1)}, bf16[1024,128]{1,0:T(8,128)(2,1)S(1)}, u32[]{:S(2)}, u32[]{:S(2)}) collective-permute-start(bf16[1024,128]{1,0:T(8,128)(2,1)S(1)} %bitcast.56), channel_id=1, source_target_pairs={{0,4},{4,8},{8,12},{12,16},{16,20},{20,24},{24,28},{28,32},{32,36}... | collective-permute-start | bytes 786440 | tf_op jit(solution)/shard_map/ppermute | solution.py:357
  5.8 13.3 %collective-permute-start.1 = (bf16[1024,128]{1,0:T(8,128)(2,1)S(1)}, bf16[1024,128]{1,0:T(8,128)(2,1)S(1)}, u32[]{:S(2)}, u32[]{:S(2)}) collective-permute-start(bf16[1024,128]{1,0:T(8,128)(2,1)S(1)} %bitcast.57), channel_id=1, source_target_pairs={{4,0},{8,4},{12,8},{16,12},{20,16},{24,20},{28,24},{32,28},{36,32}... | collective-permute-start | bytes 786440 | tf_op jit(solution)/shard_map/ppermute | solution.py:357
  9.8 6.1 %copy-start.3 = (s32[1,1,512]{2,1,0:T(1,128)S(1)}, s32[1,1,512]{2,1,0:T(1,128)}, u32[]{:S(2)}) copy-start(s32[1,1,512]{2,1,0:T(1,128)} %param.26) | copy-start | bytes 6148
  9.8 6.1 %copy-start.8 = (s32[1,1,512]{2,1,0:T(1,128)S(1)}, s32[1,1,512]{2,1,0:T(1,128)}, u32[]{:S(2)}) copy-start(s32[1,1,512]{2,1,0:T(1,128)} %param.25) | copy-start | bytes 6148
  9.8 9.2 %copy-start = (f32[4,2,2048]{2,1,0:T(2,128)S(1)}, f32[4,2,2048]{2,1,0:T(2,128)}, u32[]{:S(2)}) copy-start(f32[4,2,2048]{2,1,0:T(2,128)} %param.15) | copy-start | bytes 196612
  9.8 9.2 %copy-start.1 = (f32[4,2,2048]{2,1,0:T(2,128)S(1)}, f32[4,2,2048]{2,1,0:T(2,128)}, u32[]{:S(2)}) copy-start(f32[4,2,2048]{2,1,0:T(2,128)} %param.16) | copy-start | bytes 196612
  9.9 9.2 %copy-start.4 = (f32[32]{0:T(128)S(1)}, f32[32]{0:T(128)}, u32[]{:S(2)}) copy-start(f32[32]{0:T(128)} %w_bias.7) | copy-start | bytes 388
  9.9 9.2 %copy-start.5 = (f32[32]{0:T(128)S(1)}, f32[32]{0:T(128)}, u32[]{:S(2)}) copy-start(f32[32]{0:T(128)} %w_out.7) | copy-start | bytes 388
  15.9 35.4 %copy-start.9 = (f32[32,2]{0,1:T(2,128)S(1)}, f32[32,2]{0,1:T(2,128)}, u32[]{:S(2)}) copy-start(f32[32,2]{0,1:T(2,128)} %param.21) | copy-start | bytes 772
  15.9 41.7 %copy-start.2 = (f32[1,131072]{1,0:T(1,128)S(1)}, f32[1,131072]{1,0:T(1,128)}, u32[]{:S(2)}) copy-start(f32[1,131072]{1,0:T(1,128)} %param.17) | copy-start | bytes 1572868
  15.9 41.7 %copy-start.6 = (f32[32]{0:T(128)S(1)}, f32[32]{0:T(128)}, u32[]{:S(2)}) copy-start(f32[32]{0:T(128)} %w_bias.5) | copy-start | bytes 388
  15.9 41.7 %copy-start.7 = (f32[32]{0:T(128)S(1)}, f32[32]{0:T(128)}, u32[]{:S(2)}) copy-start(f32[32]{0:T(128)} %w_out.5) | copy-start | bytes 388
  28.8 8.6 %collective-permute-start.2 = (f32[520,128]{1,0:T(8,128)S(1)}, f32[520,128]{1,0:T(8,128)S(1)}, u32[]{:S(2)}, u32[]{:S(2)}) collective-permute-start(f32[520,128]{1,0:T(8,128)S(1)} %get-tuple-element.31.partial), channel_id=1, source_target_pairs={{0,4},{4,8},{8,12},{12,16},{16,20},{20,24},{24,28},{28,32},{32,36}... | collective-permute-start | bytes 798728 | tf_op jit(solution)/shard_map/ppermute | solution.py:357
  33.0 12.8 %collective-permute-start.3 = (f32[520,128]{1,0:T(8,128)S(1)}, f32[520,128]{1,0:T(8,128)S(1)}, u32[]{:S(2)}, u32[]{:S(2)}) collective-permute-start(f32[520,128]{1,0:T(8,128)S(1)} %get-tuple-element.31.partial), channel_id=1, source_target_pairs={{4,0},{8,4},{12,8},{16,12},{20,16},{24,20},{28,24},{32,28},{36,32}... | collective-permute-start | bytes 798728 | tf_op jit(solution)/shard_map/ppermute | solution.py:357
  47.1 4.3 %collective-permute-start.4 = (f32[256,128]{1,0:T(8,128)S(1)}, f32[256,128]{1,0:T(8,128)S(1)}, u32[]{:S(2)}, u32[]{:S(2)}) collective-permute-start(f32[256,128]{1,0:T(8,128)S(1)} %get-tuple-element.33), channel_id=1, source_target_pairs={{0,1},{1,0},{2,3},{3,2},{4,5},{5,4},{6,7},{7,6},{8,9},{9,8},{10,11... | collective-permute-start | bytes 393224 | tf_op jit(solution)/shard_map/ppermute | solution.py:360
  49.6 5.1 %collective-permute-start.5 = (f32[256,128]{1,0:T(8,128)S(1)}, f32[256,128]{1,0:T(8,128)S(1)}, u32[]{:S(2)}, u32[]{:S(2)}) collective-permute-start(f32[256,128]{1,0:T(8,128)S(1)} %get-tuple-element.34), channel_id=1, source_target_pairs={{0,2},{1,3},{2,0},{3,1},{4,6},{5,7},{6,4},{7,5},{8,10},{9,11},{10,... | collective-permute-start | bytes 393224 | tf_op jit(solution)/shard_map/ppermute | solution.py:360
  49.6 8.0 %collective-permute-start.6 = (f32[256,128]{1,0:T(8,128)S(1)}, f32[256,128]{1,0:T(8,128)S(1)}, u32[]{:S(2)}, u32[]{:S(2)}) collective-permute-start(f32[256,128]{1,0:T(8,128)S(1)} %get-tuple-element.35), channel_id=1, source_target_pairs={{0,3},{1,2},{2,1},{3,0},{4,7},{5,6},{6,5},{7,4},{8,11},{9,10},{10,... | collective-permute-start | bytes 393224 | tf_op jit(solution)/shard_map/ppermute | solution.py:360
  62.9 7.9 %collective-permute-start.7 = (bf16[256,128]{1,0:T(8,128)(2,1)S(1)}, bf16[256,128]{1,0:T(8,128)(2,1)S(1)}, u32[]{:S(2)}, u32[]{:S(2)}) collective-permute-start(bf16[256,128]{1,0:T(8,128)(2,1)S(1)} %get-tuple-element.36.own), channel_id=1, source_target_pairs={{0,4},{4,8},{8,12},{12,16},{16,20},{20,24},{24,28},{28,32},{32,36}... | collective-permute-start | bytes 196616 | tf_op jit(solution)/shard_map/ppermute | solution.py:357
  64.8 9.9 %collective-permute-start.8 = (bf16[256,128]{1,0:T(8,128)(2,1)S(1)}, bf16[256,128]{1,0:T(8,128)(2,1)S(1)}, u32[]{:S(2)}, u32[]{:S(2)}) collective-permute-start(bf16[256,128]{1,0:T(8,128)(2,1)S(1)} %get-tuple-element.36.own), channel_id=1, source_target_pairs={{4,0},{8,4},{12,8},{16,12},{20,16},{24,20},{28,24},{32,28},{36,32}... | collective-permute-start | bytes 196616 | tf_op jit(solution)/shard_map/ppermute | solution.py:357
  68.2 9.4 %collective-permute-start.10 = (bf16[256,128]{1,0:T(8,128)(2,1)S(1)}, bf16[256,128]{1,0:T(8,128)(2,1)S(1)}, u32[]{:S(2)}, u32[]{:S(2)}) collective-permute-start(bf16[256,128]{1,0:T(8,128)(2,1)S(1)} %get-tuple-element.36.own), channel_id=1, source_target_pairs={{0,1},{1,0},{2,3},{3,2},{4,5},{5,4},{6,7},{7,6},{8,9},{9,8},{10,11... | collective-permute-start | bytes 196616 | tf_op jit(solution)/shard_map/ppermute | solution.py:360
  69.0 8.5 %collective-permute-start.12 = (bf16[256,128]{1,0:T(8,128)(2,1)S(1)}, bf16[256,128]{1,0:T(8,128)(2,1)S(1)}, u32[]{:S(2)}, u32[]{:S(2)}) collective-permute-start(bf16[256,128]{1,0:T(8,128)(2,1)S(1)} %get-tuple-element.36.own), channel_id=1, source_target_pairs={{0,2},{1,3},{2,0},{3,1},{4,6},{5,7},{6,4},{7,5},{8,10},{9,11},{10,... | collective-permute-start | bytes 196616 | tf_op jit(solution)/shard_map/ppermute | solution.py:360
  69.2 8.4 %collective-permute-start.14 = (bf16[256,128]{1,0:T(8,128)(2,1)S(1)}, bf16[256,128]{1,0:T(8,128)(2,1)S(1)}, u32[]{:S(2)}, u32[]{:S(2)}) collective-permute-start(bf16[256,128]{1,0:T(8,128)(2,1)S(1)} %get-tuple-element.36.own), channel_id=1, source_target_pairs={{0,3},{1,2},{2,1},{3,0},{4,7},{5,6},{6,5},{7,4},{8,11},{9,10},{10,... | collective-permute-start | bytes 196616 | tf_op jit(solution)/shard_map/ppermute | solution.py:360
  74.7 3.9 %collective-permute-start.11 = (bf16[2,256,128]{2,1,0:T(8,128)(2,1)S(1)}, bf16[2,256,128]{2,1,0:T(8,128)(2,1)S(1)}, u32[]{:S(2)}, u32[]{:S(2)}) collective-permute-start(bf16[2,256,128]{2,1,0:T(8,128)(2,1)S(1)} %pad_maximum_fusion), channel_id=1, source_target_pairs={{0,2},{1,3},{2,0},{3,1},{4,6},{5,7},{6,4},{7,5},{8,10},{9,11},{10,... | collective-permute-start | bytes 393224 | tf_op jit(solution)/shard_map/ppermute | solution.py:360
  74.8 8.0 %collective-permute-start.13 = (bf16[2,256,128]{2,1,0:T(8,128)(2,1)S(1)}, bf16[2,256,128]{2,1,0:T(8,128)(2,1)S(1)}, u32[]{:S(2)}, u32[]{:S(2)}) collective-permute-start(bf16[2,256,128]{2,1,0:T(8,128)(2,1)S(1)} %pad_maximum_fusion), channel_id=1, source_target_pairs={{0,3},{1,2},{2,1},{3,0},{4,7},{5,6},{6,5},{7,4},{8,11},{9,10},{10,... | collective-permute-start | bytes 393224 | tf_op jit(solution)/shard_map/ppermute | solution.py:360
  77.6 5.3 %collective-permute-start.9 = (bf16[2,256,128]{2,1,0:T(8,128)(2,1)S(1)}, bf16[2,256,128]{2,1,0:T(8,128)(2,1)S(1)}, u32[]{:S(2)}, u32[]{:S(2)}) collective-permute-start(bf16[2,256,128]{2,1,0:T(8,128)(2,1)S(1)} %pad_maximum_fusion), channel_id=1, source_target_pairs={{0,1},{1,0},{2,3},{3,2},{4,5},{5,4},{6,7},{7,6},{8,9},{9,8},{10,11... | collective-permute-start | bytes 393224 | tf_op jit(solution)/shard_map/ppermute | solution.py:360
  95.7 20.5 %collective-permute-start.15 = (f32[520,128]{1,0:T(8,128)S(1)}, f32[520,128]{1,0:T(8,128)S(1)}, u32[]{:S(2)}, u32[]{:S(2)}) collective-permute-start(f32[520,128]{1,0:T(8,128)S(1)} %get-tuple-element.38.partial), channel_id=1, source_target_pairs={{0,4},{4,8},{8,12},{12,16},{16,20},{20,24},{24,28},{28,32},{32,36}... | collective-permute-start | bytes 798728 | tf_op jit(solution)/shard_map/ppermute | solution.py:357
  98.9 17.3 %collective-permute-start.16 = (f32[520,128]{1,0:T(8,128)S(1)}, f32[520,128]{1,0:T(8,128)S(1)}, u32[]{:S(2)}, u32[]{:S(2)}) collective-permute-start(f32[520,128]{1,0:T(8,128)S(1)} %get-tuple-element.38.partial), channel_id=1, source_target_pairs={{4,0},{8,4},{12,8},{16,12},{20,16},{24,20},{28,24},{32,28},{36,32}... | collective-permute-start | bytes 798728 | tf_op jit(solution)/shard_map/ppermute | solution.py:357
  105.2 16.6 %all-to-all-start = ((f32[128,1,288]{2,1,0:T(1,128)}), f32[128,1,288]{2,1,0:T(1,128)S(1)}, u32[]{:S(2)}, u32[]{:S(2)}) async-start(f32[128,1,288]{2,1,0:T(1,128)} %broadcast_in_dim.13), calls=%async_computation | async-start | bytes 393216 | tf_op jit(solution)/shard_map/all_to_all | solution.py:485
  117.6 4.3 %collective-permute-start.17 = (f32[256,128]{1,0:T(8,128)S(1)}, f32[256,128]{1,0:T(8,128)S(1)}, u32[]{:S(2)}, u32[]{:S(2)}) collective-permute-start(f32[256,128]{1,0:T(8,128)S(1)} %get-tuple-element.40), channel_id=1, source_target_pairs={{0,1},{1,0},{2,3},{3,2},{4,5},{5,4},{6,7},{7,6},{8,9},{9,8},{10,11... | collective-permute-start | bytes 393224 | tf_op jit(solution)/shard_map/ppermute | solution.py:360
  118.0 4.9 %collective-permute-start.18 = (f32[256,128]{1,0:T(8,128)S(1)}, f32[256,128]{1,0:T(8,128)S(1)}, u32[]{:S(2)}, u32[]{:S(2)}) collective-permute-start(f32[256,128]{1,0:T(8,128)S(1)} %get-tuple-element.41), channel_id=1, source_target_pairs={{0,2},{1,3},{2,0},{3,1},{4,6},{5,7},{6,4},{7,5},{8,10},{9,11},{10,... | collective-permute-start | bytes 393224 | tf_op jit(solution)/shard_map/ppermute | solution.py:360
  118.6 7.5 %collective-permute-start.19 = (f32[256,128]{1,0:T(8,128)S(1)}, f32[256,128]{1,0:T(8,128)S(1)}, u32[]{:S(2)}, u32[]{:S(2)}) collective-permute-start(f32[256,128]{1,0:T(8,128)S(1)} %get-tuple-element.42), channel_id=1, source_target_pairs={{0,3},{1,2},{2,1},{3,0},{4,7},{5,6},{6,5},{7,4},{8,11},{9,10},{10,... | collective-permute-start | bytes 393224 | tf_op jit(solution)/shard_map/ppermute | solution.py:360

commit v4 on v3

--- a/solution.py
+++ b/solution.py
@@ -204,22 +204,24 @@
         g = dual_grad[rows, :]
 
         def channel(c, done):
-            h = w_in[c, 0] * d + w_in[c, 1] * s + w_in[c, 2] * r + w_bias[c]
-            gate = sigmoid(h)
-            act = h * gate
-            err = (w_out[c] * g) * (gate + act * (1.0 - gate))
+            half = (0.5 * w_in[c, 0]) * d + (0.5 * w_in[c, 1]) * s
+            half = half + ((0.5 * w_in[c, 2]) * r + 0.5 * w_bias[c])
+            more = jnp.tanh(half) + 1.0
+            act = half * more
+            wo = 0.5 * w_out[c]
+            err = g * (more * ((half - act) + (half + 1.0)))
 
             def fold(x):
                 return jnp.sum(x.reshape(part // 8, 8, size), axis=0)
 
-            totals[c, 0] += fold(err * d)
-            totals[c, 1] += fold(err * s)
-            totals[c, 2] += fold(err * r)
-            totals[c, 3] += fold(err)
+            totals[c, 0] += wo * fold(err * d)
+            totals[c, 1] += wo * fold(err * s)
+            totals[c, 2] += wo * fold(err * r)
+            totals[c, 3] += wo * fold(err)
             totals[c, 4] += fold(act * g)
             return done
 
-        lax.fori_loop(0, w_bias.shape[0], channel, 0, unroll=2)
+        lax.fori_loop(0, w_bias.shape[0], channel, 0, unroll=4)
     for k in range(5):
         lanes = jnp.sum(totals[:, k], axis=1)
         sums[k : k + 1, :] = jnp.sum(lanes.T, axis=0, keepdims=True)

time: 129 us -> 129 us (level)
  no operation moved by 1% of the time
where the time goes in v4:
time: 129 us; the launch traced here: 126 us
  starting transfers between devices  44.1 us (34%)
  Pallas kernels  41.6 us (32%)
  waiting for transfers between devices  34.8 us (27%)
  other arithmetic  2.56 us (2%)
  local copies, waits for them, and re-layouts  1.78 us (1%)
  between operations  1.59 us (1%)
    pallas_call x10, Pallas kernels, call(): pl.pallas_call(body, out_shape=out_shapes, in_specs=specs, out_specs=[VME...  41.6 us
    ppermute x8, starting transfers between devices, beside(): return (lax.ppermute(x, 'gz', up), lax.ppermute(x, 'gz', down))  21.9 us
    ppermute x8, waiting for transfers between devices, beside(): return (lax.ppermute(x, 'gz', up), lax.ppermute(x, 'gz', down))  17.1 us
    ppermute x12, waiting for transfers between devices, peer(): return lax.ppermute(x, 'vert', [(i, i ^ d) for i in range(groups)])  15.7 us
    ppermute x12, starting transfers between devices, peer(): return lax.ppermute(x, 'vert', [(i, i ^ d) for i in range(groups)])  11.9 us
    all_to_all x1, starting transfers between devices, local(): lax.all_to_all(sent, ('gz', 'vert'), 0, 0)  10.3 us
  transfers between devices with their start and end apart: 21, of which 11 were waited for; matrix products, arithmetic and copies ran while one was open for 1% of the time, Pallas kernels for 9%

profile of v4, /device:TPU:103, one launch (start us, length us, event | category | flops | bytes accessed | tf_op | source)
XLA Modules:
  0.0 126.4 jit_solution(13689621541840591186)
XLA Ops:
  0.6 2.5 %reduce = bf16[131072]{0:T(1024)(128)(2,1)S(1)} reduce(bf16[1,131072]{1,0:T(2,128)(2,1)} %param.14, bf16[]{:T(256)} %constant.69), dimensions={0}, to_apply=%param.14.reduce_sub_computation | reduce | bytes 524290 | tf_op args[0]
  3.1 2.7 %collective-permute-start = (bf16[1024,128]{1,0:T(8,128)(2,1)S(1)}, bf16[1024,128]{1,0:T(8,128)(2,1)S(1)}, u32[]{:S(2)}, u32[]{:S(2)}) collective-permute-start(bf16[1024,128]{1,0:T(8,128)(2,1)S(1)} %bitcast.56), channel_id=1, source_target_pairs={{0,4},{4,8},{8,12},{12,16},{16,20},{20,24},{24,28},{28,32},{32,36}... | collective-permute-start | bytes 786440 | tf_op jit(solution)/shard_map/ppermute | solution.py:359
  5.8 2.6 %collective-permute-start.1 = (bf16[1024,128]{1,0:T(8,128)(2,1)S(1)}, bf16[1024,128]{1,0:T(8,128)(2,1)S(1)}, u32[]{:S(2)}, u32[]{:S(2)}) collective-permute-start(bf16[1024,128]{1,0:T(8,128)(2,1)S(1)} %bitcast.57), channel_id=1, source_target_pairs={{4,0},{8,4},{12,8},{16,12},{20,16},{24,20},{28,24},{32,28},{36,32}... | collective-permute-start | bytes 786440 | tf_op jit(solution)/shard_map/ppermute | solution.py:359
  9.1 0.8 copy.38.w_in
  9.8 0.0 copy-start.1
  9.9 0.0 copy-start.4
  9.9 0.0 copy-start.5
  9.9 6.0 %shard_map.197.blocks = bf16[65536,128]{1,0:T(8,128)(2,1)S(1)} custom-call(bf16[65536,128]{1,0:T(8,128)(2,1)} %bitcast.72, s32[1,1]{1,0:T(1,128)} %copy.48._), custom_call_target="tpu_custom_call" | custom-call | bytes 33554432 | tf_op jit(solution)/shard_map/pallas_call | solution.py:322
  15.9 0.0 copy-start.9
  15.9 0.0 copy-start.2
  15.9 0.0 copy-start.6
  15.9 0.0 copy-start.7
  16.0 0.0 collective-permute-done.low
  16.0 3.1 %collective-permute-done.1.high = bf16[1024,128]{1,0:T(8,128)(2,1)S(1)} collective-permute-done((bf16[1024,128]{1,0:T(8,128)(2,1)S(1)}, bf16[1024,128]{1,0:T(8,128)(2,1)S(1)}, u32[]{:S(2)}, u32[]{:S(2)}) %collective-permute-start.1) | collective-permute-done | bytes 262176 | tf_op jit(solution)/shard_map/ppermute | solution.py:359
  19.1 9.7 %shard_map.198 = (f32[128,128]{1,0:T(8,128)S(1)}, f32[520,128]{1,0:T(8,128)S(1)}) custom-call(s32[1]{0:T(128)} %bitcast.53.count, s32[512]{0:T(512)S(1)} %bitcast.70, s32[1,512]{1,0:T(1,128)S(1)} %get-tuple-element.54.tile, s32[1,512]{1,0:T(1,128)S(1)} %get-tuple-element.55.ray, bf16[1024,128]{1,0:T(8,128)(2,1)S(1)} %collective-permute-done.low, ...), custom_call_target="tpu_custom_call" | custom-call | bytes 25165824 | tf_op jit(solution)/shard_map/pallas_call | solution.py:322
  28.8 4.2 %collective-permute-start.2 = (f32[520,128]{1,0:T(8,128)S(1)}, f32[520,128]{1,0:T(8,128)S(1)}, u32[]{:S(2)}, u32[]{:S(2)}) collective-permute-start(f32[520,128]{1,0:T(8,128)S(1)} %get-tuple-element.31.partial), channel_id=1, source_target_pairs={{0,4},{4,8},{8,12},{12,16},{16,20},{20,24},{24,28},{28,32},{32,36}... | collective-permute-start | bytes 798728 | tf_op jit(solution)/shard_map/ppermute | solution.py:359
  33.0 1.9 %collective-permute-start.3 = (f32[520,128]{1,0:T(8,128)S(1)}, f32[520,128]{1,0:T(8,128)S(1)}, u32[]{:S(2)}, u32[]{:S(2)}) collective-permute-start(f32[520,128]{1,0:T(8,128)S(1)} %get-tuple-element.31.partial), channel_id=1, source_target_pairs={{4,0},{8,4},{12,8},{16,12},{20,16},{24,20},{28,24},{32,28},{36,32}... | collective-permute-start | bytes 798728 | tf_op jit(solution)/shard_map/ppermute | solution.py:359
  34.9 0.7 shard_map.199.held
  35.6 1.8 %collective-permute-done.2.from_low = f32[520,128]{1,0:T(8,128)S(1)} collective-permute-done((f32[520,128]{1,0:T(8,128)S(1)}, f32[520,128]{1,0:T(8,128)S(1)}, u32[]{:S(2)}, u32[]{:S(2)}) %collective-permute-start.2) | collective-permute-done | bytes 266272 | tf_op jit(solution)/shard_map/ppermute | solution.py:359
  37.4 8.3 %collective-permute-done.3.from_high = f32[520,128]{1,0:T(8,128)S(1)} collective-permute-done((f32[520,128]{1,0:T(8,128)S(1)}, f32[520,128]{1,0:T(8,128)S(1)}, u32[]{:S(2)}, u32[]{:S(2)}) %collective-permute-start.3) | collective-permute-done | bytes 266272 | tf_op jit(solution)/shard_map/ppermute | solution.py:359
  45.8 1.3 %shard_map.200 = (f32[256,128]{1,0:T(8,128)S(1)}, f32[256,128]{1,0:T(8,128)S(1)}, f32[256,128]{1,0:T(8,128)S(1)}, f32[256,128]{1,0:T(8,128)S(1)}) custom-call(s32[1]{0:T(128)} %bitcast.me, f32[4,256,128]{2,1,0:T(8,128)S(1)} %shard_map.199.held, f32[520,128]{1,0:T(8,128)S(1)} %collective-permute-done.2.from_low, f32[520,128]{1,0:T(8,128)S(1)} %collective-permute-done.3.from_high), custom_call_target="tpu_custom_call" | custom-call | bytes 8388608 | tf_op jit(solution)/shard_map/pallas_call | solution.py:322
  47.1 2.5 %collective-permute-start.4 = (f32[256,128]{1,0:T(8,128)S(1)}, f32[256,128]{1,0:T(8,128)S(1)}, u32[]{:S(2)}, u32[]{:S(2)}) collective-permute-start(f32[256,128]{1,0:T(8,128)S(1)} %get-tuple-element.33), channel_id=1, source_target_pairs={{0,1},{1,0},{2,3},{3,2},{4,5},{5,4},{6,7},{7,6},{8,9},{9,8},{10,11... | collective-permute-start | bytes 393224 | tf_op jit(solution)/shard_map/ppermute | solution.py:362
  49.6 0.0 collective-permute-start.5
  49.6 1.7 %collective-permute-start.6 = (f32[256,128]{1,0:T(8,128)S(1)}, f32[256,128]{1,0:T(8,128)S(1)}, u32[]{:S(2)}, u32[]{:S(2)}) collective-permute-start(f32[256,128]{1,0:T(8,128)S(1)} %get-tuple-element.35), channel_id=1, source_target_pairs={{0,3},{1,2},{2,1},{3,0},{4,7},{5,6},{6,5},{7,4},{8,11},{9,10},{10,... | collective-permute-start | bytes 393224 | tf_op jit(solution)/shard_map/ppermute | solution.py:362
  51.3 0.1 copy.39.w_in
  51.4 0.0 collective-permute-done.4.peer1
  51.4 3.2 %collective-permute-done.5.peer2 = f32[256,128]{1,0:T(8,128)S(1)} collective-permute-done((f32[256,128]{1,0:T(8,128)S(1)}, f32[256,128]{1,0:T(8,128)S(1)}, u32[]{:S(2)}, u32[]{:S(2)}) %collective-permute-start.5) | collective-permute-done | bytes 131104 | tf_op jit(solution)/shard_map/ppermute | solution.py:362
  54.6 3.0 %collective-permute-done.6.peer3 = f32[256,128]{1,0:T(8,128)S(1)} collective-permute-done((f32[256,128]{1,0:T(8,128)S(1)}, f32[256,128]{1,0:T(8,128)S(1)}, u32[]{:S(2)}, u32[]{:S(2)}) %collective-permute-start.6) | collective-permute-done | bytes 131104 | tf_op jit(solution)/shard_map/ppermute | solution.py:362
  57.6 5.3 %shard_map.201 = (bf16[256,128]{1,0:T(8,128)(2,1)S(1)}, f32[256,128]{1,0:T(8,128)S(1)}, f32[4,32]{1,0:T(4,128)S(1)}) custom-call(s32[1]{0:T(128)} %bitcast.me, f32[256,128]{1,0:T(8,128)S(1)} %get-tuple-element.32.own, f32[256,128]{1,0:T(8,128)S(1)} %collective-permute-done.4.peer1, f32[256,128]{1,0:T(8,128)S(1)} %collective-permute-done.5.peer2, ...), custom_call_target="tpu_custom_call" | custom-call | bytes 16777216 | tf_op jit(solution)/shard_map/pallas_call | solution.py:322
  62.9 1.9 %collective-permute-start.7 = (bf16[256,128]{1,0:T(8,128)(2,1)S(1)}, bf16[256,128]{1,0:T(8,128)(2,1)S(1)}, u32[]{:S(2)}, u32[]{:S(2)}) collective-permute-start(bf16[256,128]{1,0:T(8,128)(2,1)S(1)} %get-tuple-element.36.own), channel_id=1, source_target_pairs={{0,4},{4,8},{8,12},{12,16},{16,20},{20,24},{24,28},{28,32},{32,36}... | collective-permute-start | bytes 196616 | tf_op jit(solution)/shard_map/ppermute | solution.py:359
  64.8 3.4 %collective-permute-start.8 = (bf16[256,128]{1,0:T(8,128)(2,1)S(1)}, bf16[256,128]{1,0:T(8,128)(2,1)S(1)}, u32[]{:S(2)}, u32[]{:S(2)}) collective-permute-start(bf16[256,128]{1,0:T(8,128)(2,1)S(1)} %get-tuple-element.36.own), channel_id=1, source_target_pairs={{4,0},{8,4},{12,8},{16,12},{20,16},{24,20},{28,24},{32,28},{36,32}... | collective-permute-start | bytes 196616 | tf_op jit(solution)/shard_map/ppermute | solution.py:359
  68.2 0.9 collective-permute-start.10
  69.1 0.1 collective-permute-start.12
  69.2 1.6 %collective-permute-start.14 = (bf16[256,128]{1,0:T(8,128)(2,1)S(1)}, bf16[256,128]{1,0:T(8,128)(2,1)S(1)}, u32[]{:S(2)}, u32[]{:S(2)}) collective-permute-start(bf16[256,128]{1,0:T(8,128)(2,1)S(1)} %get-tuple-element.36.own), channel_id=1, source_target_pairs={{0,3},{1,2},{2,1},{3,0},{4,7},{5,6},{6,5},{7,4},{8,11},{9,10},{10,... | collective-permute-start | bytes 196616 | tf_op jit(solution)/shard_map/ppermute | solution.py:362
  70.8 0.0 collective-permute-done.7.low
  70.8 3.9 %collective-permute-done.8.high = bf16[256,128]{1,0:T(8,128)(2,1)S(1)} collective-permute-done((bf16[256,128]{1,0:T(8,128)(2,1)S(1)}, bf16[256,128]{1,0:T(8,128)(2,1)S(1)}, u32[]{:S(2)}, u32[]{:S(2)}) %collective-permute-start.8) | collective-permute-done | bytes 65568 | tf_op jit(solution)/shard_map/ppermute | solution.py:359
  74.7 0.1 collective-permute-start.11
  74.8 2.7 %collective-permute-start.13 = (bf16[2,256,128]{2,1,0:T(8,128)(2,1)S(1)}, bf16[2,256,128]{2,1,0:T(8,128)(2,1)S(1)}, u32[]{:S(2)}, u32[]{:S(2)}) collective-permute-start(bf16[2,256,128]{2,1,0:T(8,128)(2,1)S(1)} %pad_maximum_fusion), channel_id=1, source_target_pairs={{0,3},{1,2},{2,1},{3,0},{4,7},{5,6},{6,5},{7,4},{8,11},{9,10},{10,... | collective-permute-start | bytes 393224 | tf_op jit(solution)/shard_map/ppermute | solution.py:362
  77.6 0.0 collective-permute-done.10.own1
  77.6 0.0 collective-permute-start.9
  77.6 0.0 collective-permute-done.12.own2
  77.6 0.0 collective-permute-done.14.own3
  77.6 1.0 collective-permute-done.11.near2
  78.6 4.2 %collective-permute-done.13.near3 = bf16[2,256,128]{2,1,0:T(8,128)(2,1)S(1)} collective-permute-done((bf16[2,256,128]{2,1,0:T(8,128)(2,1)S(1)}, bf16[2,256,128]{2,1,0:T(8,128)(2,1)S(1)}, u32[]{:S(2)}, u32[]{:S(2)}) %collective-permute-start.13) | collective-permute-done | bytes 131104 | tf_op jit(solution)/shard_map/ppermute | solution.py:362
  82.9 0.0 collective-permute-done.9.near1
  82.9 12.8 %shard_map.202 = (f32[128,128]{1,0:T(8,128)}, f32[520,128]{1,0:T(8,128)S(1)}, f32[128,128]{1,0:T(8,128)S(1)}) custom-call(s32[1]{0:T(128)} %bitcast.me, s32[1]{0:T(128)} %bitcast.54.count, s32[512]{0:T(512)S(1)} %bitcast.71, s32[1,512]{1,0:T(1,128)S(1)} %get-tuple-element.54.tile, s32[1,512]{1,0:T(1,128)S(1)} %get-tuple-element.55.ray, ...), custom_call_target="tpu_custom_call" | custom-call | bytes 25165824 | tf_op jit(solution)/shard_map/pallas_call | solution.py:322
  95.7 3.2 %collective-permute-start.15 = (f32[520,128]{1,0:T(8,128)S(1)}, f32[520,128]{1,0:T(8,128)S(1)}, u32[]{:S(2)}, u32[]{:S(2)}) collective-permute-start(f32[520,128]{1,0:T(8,128)S(1)} %get-tuple-element.38.partial), channel_id=1, source_target_pairs={{0,4},{4,8},{8,12},{12,16},{16,20},{20,24},{24,28},{28,32},{32,36}... | collective-permute-start | bytes 798728 | tf_op jit(solution)/shard_map/ppermute | solution.py:359
  99.0 2.0 %collective-permute-start.16 = (f32[520,128]{1,0:T(8,128)S(1)}, f32[520,128]{1,0:T(8,128)S(1)}, u32[]{:S(2)}, u32[]{:S(2)}) collective-permute-start(f32[520,128]{1,0:T(8,128)S(1)} %get-tuple-element.38.partial), channel_id=1, source_target_pairs={{4,0},{8,4},{12,8},{16,12},{20,16},{24,20},{28,24},{32,28},{36,32}... | collective-permute-start | bytes 798728 | tf_op jit(solution)/shard_map/ppermute | solution.py:359
  101.0 3.0 %shard_map.205 = f32[5,32]{1,0:T(8,128)S(1)} custom-call(f32[128,128]{1,0:T(8,128)S(1)} %bitcast.63, f32[128,128]{1,0:T(8,128)S(1)} %bitcast.66, f32[128,128]{1,0:T(8,128)S(1)} %get-tuple-element.37.sinogram, f32[128,128]{1,0:T(8,128)S(1)} %get-tuple-element.44.dual_grad, f32[32,3]{1,0:T(8,128)S(1)} %copy.38.w_in, f32[32]{0:T(128)S(1)} %copy-done.4, ...), custom_call_target="tpu_custom_call" | custom-call | bytes 12582912 | tf_op jit(solution)/shard_map/pallas_call | solution.py:322
  104.0 0.1 broadcast_in_dim.12
  104.1 0.8 broadcast_in_dim.13
  104.9 10.3 %all-to-all-start = ((f32[128,1,288]{2,1,0:T(1,128)}), f32[128,1,288]{2,1,0:T(1,128)S(1)}, u32[]{:S(2)}, u32[]{:S(2)}) async-start(f32[128,1,288]{2,1,0:T(1,128)} %broadcast_in_dim.13), calls=%async_computation | async-start | bytes 393216 | tf_op jit(solution)/shard_map/all_to_all | solution.py:487
  115.2 0.7 shard_map.203.held
  116.0 0.0 collective-permute-done.15.from_low
  116.0 0.0 collective-permute-done.16.from_high
  116.0 1.3 %shard_map.204 = (f32[256,128]{1,0:T(8,128)S(1)}, f32[256,128]{1,0:T(8,128)S(1)}, f32[256,128]{1,0:T(8,128)S(1)}, f32[256,128]{1,0:T(8,128)S(1)}) custom-call(s32[1]{0:T(128)} %bitcast.me, f32[4,256,128]{2,1,0:T(8,128)S(1)} %shard_map.203.held, f32[520,128]{1,0:T(8,128)S(1)} %collective-permute-done.15.from_low, f32[520,128]{1,0:T(8,128)S(1)} %collective-permute-done.16.from_high), custom_call_target="tpu_custom_call" | custom-call | bytes 8388608 | tf_op jit(solution)/shard_map/pallas_call | solution.py:322
  117.3 0.4 collective-permute-start.17
  117.7 0.6 collective-permute-start.18
  118.3 1.2 collective-permute-start.19
  119.5 2.0 %all-to-all-done = f32[128,1,288]{2,1,0:T(1,128)S(1)} async-done(((f32[128,1,288]{2,1,0:T(1,128)}), f32[128,1,288]{2,1,0:T(1,128)S(1)}, u32[]{:S(2)}, u32[]{:S(2)}) %all-to-all-start) | async-done | bytes 147488 | tf_op jit(solution)/shard_map/all_to_all | solution.py:487
  121.5 0.0 collective-permute-done.17.peer1
  121.6 1.1 collective-permute-done.18.peer2
  122.6 3.1 %collective-permute-done.19.peer3 = f32[256,128]{1,0:T(8,128)S(1)} collective-permute-done((f32[256,128]{1,0:T(8,128)S(1)}, f32[256,128]{1,0:T(8,128)S(1)}, u32[]{:S(2)}, u32[]{:S(2)}) %collective-permute-start.19) | collective-permute-done | bytes 131104 | tf_op jit(solution)/shard_map/ppermute | solution.py:362
  125.7 0.7 shard_map.206
  (19 shorter events, 0.1 us)
Async XLA Ops:
  3.1 12.9 %collective-permute-start = (bf16[1024,128]{1,0:T(8,128)(2,1)S(1)}, bf16[1024,128]{1,0:T(8,128)(2,1)S(1)}, u32[]{:S(2)}, u32[]{:S(2)}) collective-permute-start(bf16[1024,128]{1,0:T(8,128)(2,1)S(1)} %bitcast.56), channel_id=1, source_target_pairs={{0,4},{4,8},{8,12},{12,16},{16,20},{20,24},{24,28},{28,32},{32,36}... | collective-permute-start | bytes 786440 | tf_op jit(solution)/shard_map/ppermute | solution.py:359
  5.8 13.3 %collective-permute-start.1 = (bf16[1024,128]{1,0:T(8,128)(2,1)S(1)}, bf16[1024,128]{1,0:T(8,128)(2,1)S(1)}, u32[]{:S(2)}, u32[]{:S(2)}) collective-permute-start(bf16[1024,128]{1,0:T(8,128)(2,1)S(1)} %bitcast.57), channel_id=1, source_target_pairs={{4,0},{8,4},{12,8},{16,12},{20,16},{24,20},{28,24},{32,28},{36,32}... | collective-permute-start | bytes 786440 | tf_op jit(solution)/shard_map/ppermute | solution.py:359
  9.8 6.1 %copy-start.3 = (s32[1,1,512]{2,1,0:T(1,128)S(1)}, s32[1,1,512]{2,1,0:T(1,128)}, u32[]{:S(2)}) copy-start(s32[1,1,512]{2,1,0:T(1,128)} %param.26) | copy-start | bytes 6148
  9.8 6.1 %copy-start.8 = (s32[1,1,512]{2,1,0:T(1,128)S(1)}, s32[1,1,512]{2,1,0:T(1,128)}, u32[]{:S(2)}) copy-start(s32[1,1,512]{2,1,0:T(1,128)} %param.25) | copy-start | bytes 6148
  9.8 9.2 %copy-start = (f32[4,2,2048]{2,1,0:T(2,128)S(1)}, f32[4,2,2048]{2,1,0:T(2,128)}, u32[]{:S(2)}) copy-start(f32[4,2,2048]{2,1,0:T(2,128)} %param.15) | copy-start | bytes 196612
  9.8 9.2 %copy-start.1 = (f32[4,2,2048]{2,1,0:T(2,128)S(1)}, f32[4,2,2048]{2,1,0:T(2,128)}, u32[]{:S(2)}) copy-start(f32[4,2,2048]{2,1,0:T(2,128)} %param.16) | copy-start | bytes 196612
  9.9 9.2 %copy-start.4 = (f32[32]{0:T(128)S(1)}, f32[32]{0:T(128)}, u32[]{:S(2)}) copy-start(f32[32]{0:T(128)} %w_bias.7) | copy-start | bytes 388
  9.9 9.2 %copy-start.5 = (f32[32]{0:T(128)S(1)}, f32[32]{0:T(128)}, u32[]{:S(2)}) copy-start(f32[32]{0:T(128)} %w_out.7) | copy-start | bytes 388
  15.9 35.4 %copy-start.9 = (f32[32,2]{0,1:T(2,128)S(1)}, f32[32,2]{0,1:T(2,128)}, u32[]{:S(2)}) copy-start(f32[32,2]{0,1:T(2,128)} %param.21) | copy-start | bytes 772
  15.9 41.7 %copy-start.2 = (f32[1,131072]{1,0:T(1,128)S(1)}, f32[1,131072]{1,0:T(1,128)}, u32[]{:S(2)}) copy-start(f32[1,131072]{1,0:T(1,128)} %param.17) | copy-start | bytes 1572868
  15.9 41.7 %copy-start.6 = (f32[32]{0:T(128)S(1)}, f32[32]{0:T(128)}, u32[]{:S(2)}) copy-start(f32[32]{0:T(128)} %w_bias.5) | copy-start | bytes 388
  15.9 41.7 %copy-start.7 = (f32[32]{0:T(128)S(1)}, f32[32]{0:T(128)}, u32[]{:S(2)}) copy-start(f32[32]{0:T(128)} %w_out.5) | copy-start | bytes 388
  28.8 8.6 %collective-permute-start.2 = (f32[520,128]{1,0:T(8,128)S(1)}, f32[520,128]{1,0:T(8,128)S(1)}, u32[]{:S(2)}, u32[]{:S(2)}) collective-permute-start(f32[520,128]{1,0:T(8,128)S(1)} %get-tuple-element.31.partial), channel_id=1, source_target_pairs={{0,4},{4,8},{8,12},{12,16},{16,20},{20,24},{24,28},{28,32},{32,36}... | collective-permute-start | bytes 798728 | tf_op jit(solution)/shard_map/ppermute | solution.py:359
  33.0 12.8 %collective-permute-start.3 = (f32[520,128]{1,0:T(8,128)S(1)}, f32[520,128]{1,0:T(8,128)S(1)}, u32[]{:S(2)}, u32[]{:S(2)}) collective-permute-start(f32[520,128]{1,0:T(8,128)S(1)} %get-tuple-element.31.partial), channel_id=1, source_target_pairs={{4,0},{8,4},{12,8},{16,12},{20,16},{24,20},{28,24},{32,28},{36,32}... | collective-permute-start | bytes 798728 | tf_op jit(solution)/shard_map/ppermute | solution.py:359
  47.1 4.3 %collective-permute-start.4 = (f32[256,128]{1,0:T(8,128)S(1)}, f32[256,128]{1,0:T(8,128)S(1)}, u32[]{:S(2)}, u32[]{:S(2)}) collective-permute-start(f32[256,128]{1,0:T(8,128)S(1)} %get-tuple-element.33), channel_id=1, source_target_pairs={{0,1},{1,0},{2,3},{3,2},{4,5},{5,4},{6,7},{7,6},{8,9},{9,8},{10,11... | collective-permute-start | bytes 393224 | tf_op jit(solution)/shard_map/ppermute | solution.py:362
  49.6 5.1 %collective-permute-start.5 = (f32[256,128]{1,0:T(8,128)S(1)}, f32[256,128]{1,0:T(8,128)S(1)}, u32[]{:S(2)}, u32[]{:S(2)}) collective-permute-start(f32[256,128]{1,0:T(8,128)S(1)} %get-tuple-element.34), channel_id=1, source_target_pairs={{0,2},{1,3},{2,0},{3,1},{4,6},{5,7},{6,4},{7,5},{8,10},{9,11},{10,... | collective-permute-start | bytes 393224 | tf_op jit(solution)/shard_map/ppermute | solution.py:362
  49.6 8.0 %collective-permute-start.6 = (f32[256,128]{1,0:T(8,128)S(1)}, f32[256,128]{1,0:T(8,128)S(1)}, u32[]{:S(2)}, u32[]{:S(2)}) collective-permute-start(f32[256,128]{1,0:T(8,128)S(1)} %get-tuple-element.35), channel_id=1, source_target_pairs={{0,3},{1,2},{2,1},{3,0},{4,7},{5,6},{6,5},{7,4},{8,11},{9,10},{10,... | collective-permute-start | bytes 393224 | tf_op jit(solution)/shard_map/ppermute | solution.py:362
  62.9 7.9 %collective-permute-start.7 = (bf16[256,128]{1,0:T(8,128)(2,1)S(1)}, bf16[256,128]{1,0:T(8,128)(2,1)S(1)}, u32[]{:S(2)}, u32[]{:S(2)}) collective-permute-start(bf16[256,128]{1,0:T(8,128)(2,1)S(1)} %get-tuple-element.36.own), channel_id=1, source_target_pairs={{0,4},{4,8},{8,12},{12,16},{16,20},{20,24},{24,28},{28,32},{32,36}... | collective-permute-start | bytes 196616 | tf_op jit(solution)/shard_map/ppermute | solution.py:359
  64.8 9.9 %collective-permute-start.8 = (bf16[256,128]{1,0:T(8,128)(2,1)S(1)}, bf16[256,128]{1,0:T(8,128)(2,1)S(1)}, u32[]{:S(2)}, u32[]{:S(2)}) collective-permute-start(bf16[256,128]{1,0:T(8,128)(2,1)S(1)} %get-tuple-element.36.own), channel_id=1, source_target_pairs={{4,0},{8,4},{12,8},{16,12},{20,16},{24,20},{28,24},{32,28},{36,32}... | collective-permute-start | bytes 196616 | tf_op jit(solution)/shard_map/ppermute | solution.py:359
  68.2 9.4 %collective-permute-start.10 = (bf16[256,128]{1,0:T(8,128)(2,1)S(1)}, bf16[256,128]{1,0:T(8,128)(2,1)S(1)}, u32[]{:S(2)}, u32[]{:S(2)}) collective-permute-start(bf16[256,128]{1,0:T(8,128)(2,1)S(1)} %get-tuple-element.36.own), channel_id=1, source_target_pairs={{0,1},{1,0},{2,3},{3,2},{4,5},{5,4},{6,7},{7,6},{8,9},{9,8},{10,11... | collective-permute-start | bytes 196616 | tf_op jit(solution)/shard_map/ppermute | solution.py:362
  69.1 8.5 %collective-permute-start.12 = (bf16[256,128]{1,0:T(8,128)(2,1)S(1)}, bf16[256,128]{1,0:T(8,128)(2,1)S(1)}, u32[]{:S(2)}, u32[]{:S(2)}) collective-permute-start(bf16[256,128]{1,0:T(8,128)(2,1)S(1)} %get-tuple-element.36.own), channel_id=1, source_target_pairs={{0,2},{1,3},{2,0},{3,1},{4,6},{5,7},{6,4},{7,5},{8,10},{9,11},{10,... | collective-permute-start | bytes 196616 | tf_op jit(solution)/shard_map/ppermute | solution.py:362
  69.2 8.4 %collective-permute-start.14 = (bf16[256,128]{1,0:T(8,128)(2,1)S(1)}, bf16[256,128]{1,0:T(8,128)(2,1)S(1)}, u32[]{:S(2)}, u32[]{:S(2)}) collective-permute-start(bf16[256,128]{1,0:T(8,128)(2,1)S(1)} %get-tuple-element.36.own), channel_id=1, source_target_pairs={{0,3},{1,2},{2,1},{3,0},{4,7},{5,6},{6,5},{7,4},{8,11},{9,10},{10,... | collective-permute-start | bytes 196616 | tf_op jit(solution)/shard_map/ppermute | solution.py:362
  74.7 3.9 %collective-permute-start.11 = (bf16[2,256,128]{2,1,0:T(8,128)(2,1)S(1)}, bf16[2,256,128]{2,1,0:T(8,128)(2,1)S(1)}, u32[]{:S(2)}, u32[]{:S(2)}) collective-permute-start(bf16[2,256,128]{2,1,0:T(8,128)(2,1)S(1)} %pad_maximum_fusion), channel_id=1, source_target_pairs={{0,2},{1,3},{2,0},{3,1},{4,6},{5,7},{6,4},{7,5},{8,10},{9,11},{10,... | collective-permute-start | bytes 393224 | tf_op jit(solution)/shard_map/ppermute | solution.py:362
  74.8 8.0 %collective-permute-start.13 = (bf16[2,256,128]{2,1,0:T(8,128)(2,1)S(1)}, bf16[2,256,128]{2,1,0:T(8,128)(2,1)S(1)}, u32[]{:S(2)}, u32[]{:S(2)}) collective-permute-start(bf16[2,256,128]{2,1,0:T(8,128)(2,1)S(1)} %pad_maximum_fusion), channel_id=1, source_target_pairs={{0,3},{1,2},{2,1},{3,0},{4,7},{5,6},{6,5},{7,4},{8,11},{9,10},{10,... | collective-permute-start | bytes 393224 | tf_op jit(solution)/shard_map/ppermute | solution.py:362
  77.6 5.3 %collective-permute-start.9 = (bf16[2,256,128]{2,1,0:T(8,128)(2,1)S(1)}, bf16[2,256,128]{2,1,0:T(8,128)(2,1)S(1)}, u32[]{:S(2)}, u32[]{:S(2)}) collective-permute-start(bf16[2,256,128]{2,1,0:T(8,128)(2,1)S(1)} %pad_maximum_fusion), channel_id=1, source_target_pairs={{0,1},{1,0},{2,3},{3,2},{4,5},{5,4},{6,7},{7,6},{8,9},{9,8},{10,11... | collective-permute-start | bytes 393224 | tf_op jit(solution)/shard_map/ppermute | solution.py:362
  95.7 20.3 %collective-permute-start.15 = (f32[520,128]{1,0:T(8,128)S(1)}, f32[520,128]{1,0:T(8,128)S(1)}, u32[]{:S(2)}, u32[]{:S(2)}) collective-permute-start(f32[520,128]{1,0:T(8,128)S(1)} %get-tuple-element.38.partial), channel_id=1, source_target_pairs={{0,4},{4,8},{8,12},{12,16},{16,20},{20,24},{24,28},{28,32},{32,36}... | collective-permute-start | bytes 798728 | tf_op jit(solution)/shard_map/ppermute | solution.py:359
  99.0 17.0 %collective-permute-start.16 = (f32[520,128]{1,0:T(8,128)S(1)}, f32[520,128]{1,0:T(8,128)S(1)}, u32[]{:S(2)}, u32[]{:S(2)}) collective-permute-start(f32[520,128]{1,0:T(8,128)S(1)} %get-tuple-element.38.partial), channel_id=1, source_target_pairs={{4,0},{8,4},{12,8},{16,12},{20,16},{24,20},{28,24},{32,28},{36,32}... | collective-permute-start | bytes 798728 | tf_op jit(solution)/shard_map/ppermute | solution.py:359
  104.9 16.6 %all-to-all-start = ((f32[128,1,288]{2,1,0:T(1,128)}), f32[128,1,288]{2,1,0:T(1,128)S(1)}, u32[]{:S(2)}, u32[]{:S(2)}) async-start(f32[128,1,288]{2,1,0:T(1,128)} %broadcast_in_dim.13), calls=%async_computation | async-start | bytes 393216 | tf_op jit(solution)/shard_map/all_to_all | solution.py:487
  117.3 4.3 %collective-permute-start.17 = (f32[256,128]{1,0:T(8,128)S(1)}, f32[256,128]{1,0:T(8,128)S(1)}, u32[]{:S(2)}, u32[]{:S(2)}) collective-permute-start(f32[256,128]{1,0:T(8,128)S(1)} %get-tuple-element.40), channel_id=1, source_target_pairs={{0,1},{1,0},{2,3},{3,2},{4,5},{5,4},{6,7},{7,6},{8,9},{9,8},{10,11... | collective-permute-start | bytes 393224 | tf_op jit(solution)/shard_map/ppermute | solution.py:362
  117.7 4.9 %collective-permute-start.18 = (f32[256,128]{1,0:T(8,128)S(1)}, f32[256,128]{1,0:T(8,128)S(1)}, u32[]{:S(2)}, u32[]{:S(2)}) collective-permute-start(f32[256,128]{1,0:T(8,128)S(1)} %get-tuple-element.41), channel_id=1, source_target_pairs={{0,2},{1,3},{2,0},{3,1},{4,6},{5,7},{6,4},{7,5},{8,10},{9,11},{10,... | collective-permute-start | bytes 393224 | tf_op jit(solution)/shard_map/ppermute | solution.py:362
  118.3 7.5 %collective-permute-start.19 = (f32[256,128]{1,0:T(8,128)S(1)}, f32[256,128]{1,0:T(8,128)S(1)}, u32[]{:S(2)}, u32[]{:S(2)}) collective-permute-start(f32[256,128]{1,0:T(8,128)S(1)} %get-tuple-element.42), channel_id=1, source_target_pairs={{0,3},{1,2},{2,1},{3,0},{4,7},{5,6},{6,5},{7,4},{8,11},{9,10},{10,... | collective-permute-start | bytes 393224 | tf_op jit(solution)/shard_map/ppermute | solution.py:362
